TPU v7x, 256 devices: a whole 4x4x8 slice. The times are simulated.
256 devices in a mesh: slide: 8 (over x_lo, y), tile: 32 (over x_hi, z, core).
Axes of the slice: x: 4 (x_hi: 2, x_lo: 2; x = x_hi * 2 + x_lo), y: 4, z: 8, core: 2. Of those that a mesh axis runs over, the one named last changes fastest.
Arguments:
- tiles: bfloat16 [8, 1024, 64, 1024], P('slide', 'tile'), may hold values from -18 to 18
- counts: int32 [8, 32], P('slide', 'tile'), may hold values from 1 to 32, 512 in all within a row
- slide_ids: int32 [8, 1024], P('slide', 'tile'), may hold values from 0 to 3, as said below
- pooled_cot: bfloat16 [32, 1024], P('slide', 'tile'), may hold values from -6 to 6
- w_up: bfloat16 [1024, 256], replicated, may hold values from -0.1875 to 0.1875
- w_down: bfloat16 [256, 1024], replicated, may hold values from -0.375 to 0.375
- gain_up: float32 [256], replicated, may hold values from 0.25 to 1.75
- gain_down: float32 [1024], replicated, may hold values from 0.25 to 1.75
- attn_v: bfloat16 [1024, 256], replicated, may hold values from -0.375 to 0.375
- attn_u: bfloat16 [1024, 256], replicated, may hold values from -0.375 to 0.375
- attn_w: float32 [256], replicated, may hold values from -0.75 to 0.75
Outputs:
- pooled: float32 [32, 1024], P('slide')
- grad_w_up: float32 [1024, 256], replicated
- grad_w_down: float32 [256, 1024], replicated
- grad_gain_up: float32 [256], replicated
- grad_gain_down: float32 [1024], replicated
- grad_attn_v: float32 [1024, 256], replicated
- grad_attn_u: float32 [1024, 256], replicated
- grad_attn_w: float32 [256], replicated
Inputs may be any that keep to these rules, and one draw needn't show every extreme that they name: In every band the counts sum to exactly 512, and some device of each band holds exactly 32. `slide_ids`: every slide of a band is named by local slot 0 of some device of that band.
All inputs are finite; a program needn't handle non-finite values.
Results may differ from a plain program's by a relative error of at most 0.0046.
The roundings to bfloat16 on the way count: a program that leaves them out, or rounds other values in their place, can miss the bound.
Values may be sent and summed in bfloat16 or wider, within the bound.
No kernel may reach another device: no remote copies, remote signals or barrier semaphores. Data moves between devices by JAX's collectives and lax.ppermute only.
A program may use at most 64 MiB of HBM per device.

v0:
```python
import jax
import jax.numpy as jnp
from jax import lax
from jax.sharding import PartitionSpec as P

OWN = 16


HIGHEST = lax.Precision.HIGHEST


def forward(tile_rows, w_up, w_down, gain_up, gain_down, attn_v, attn_u, attn_w, positions):
    up_proj = jnp.dot(tile_rows, w_up, preferred_element_type=jnp.float32)
    scaled_up = up_proj * gain_up
    hidden = jax.nn.relu(scaled_up).astype(jnp.bfloat16)
    down_proj = jnp.dot(hidden, w_down, preferred_element_type=jnp.float32)
    residual_sum = tile_rows.astype(jnp.float32) + down_proj * gain_down
    width = residual_sum.shape[-1]
    features = jnp.mean(jax.nn.relu(residual_sum).reshape(-1, positions, width), axis=1)
    features_b = features.astype(jnp.bfloat16)
    tanh_gate = jnp.tanh(jnp.dot(features_b, attn_v, preferred_element_type=jnp.float32))
    sigm_gate = jax.nn.sigmoid(jnp.dot(features_b, attn_u, preferred_element_type=jnp.float32))
    score = jnp.sum(tanh_gate * sigm_gate * attn_w, axis=-1)
    weight = jax.nn.sigmoid(score)
    return (
        up_proj,
        scaled_up,
        hidden,
        down_proj,
        residual_sum,
        features,
        features_b,
        tanh_gate,
        sigm_gate,
        weight,
    )


def backward(
    tile_rows,
    saved_state,
    member,
    pooled,
    denominator,
    cot_full,
    w_up,
    w_down,
    gain_up,
    gain_down,
    attn_v,
    attn_u,
    attn_w,
    positions,
):
    (
        up_proj,
        scaled_up,
        hidden,
        down_proj,
        residual_sum,
        features,
        features_b,
        tanh_gate,
        sigm_gate,
        weight,
    ) = saved_state
    cot_tile = jnp.dot(member, cot_full, precision=HIGHEST)
    pooled_tile = jnp.dot(member, pooled, precision=HIGHEST)
    den_sum = jnp.sum(member * denominator[None, :], axis=1)
    den_tile = jnp.where(jnp.sum(member, axis=1) > 0.5, den_sum, 1.0)
    weight_share = weight / den_tile
    dfeatures = weight_share[:, None] * cot_tile
    dweight = jnp.sum(cot_tile * (features - pooled_tile), axis=1) / den_tile
    dscore = dweight * weight * (1.0 - weight)
    grad_attn_w = jnp.sum(dscore[:, None] * tanh_gate * sigm_gate, axis=0)
    grad_tanh = dscore[:, None] * attn_w * sigm_gate * (1.0 - tanh_gate * tanh_gate)
    grad_sigm = dscore[:, None] * attn_w * tanh_gate * sigm_gate * (1.0 - sigm_gate)
    features_f = features_b.astype(jnp.float32)
    grad_attn_v = jnp.dot(features_f.T, grad_tanh, precision=HIGHEST)
    grad_attn_u = jnp.dot(features_f.T, grad_sigm, precision=HIGHEST)
    dfeatures = dfeatures + jnp.dot(grad_tanh, attn_v.astype(jnp.float32).T, precision=HIGHEST)
    dfeatures = dfeatures + jnp.dot(grad_sigm, attn_u.astype(jnp.float32).T, precision=HIGHEST)
    tile_total = dfeatures.shape[0]
    width = dfeatures.shape[1]
    active = residual_sum.reshape(tile_total, positions, width) > 0
    dresidual = jnp.where(active, (dfeatures / positions)[:, None, :], 0.0).reshape(-1, width)
    grad_gain_down = jnp.sum(dresidual * down_proj, axis=0)
    dback = (dresidual * gain_down).astype(jnp.bfloat16)
    grad_w_down = jnp.dot(hidden.T, dback, preferred_element_type=jnp.float32)
    dhidden = jnp.dot(dback, w_down.T, preferred_element_type=jnp.float32)
    dscaled = jnp.where(scaled_up > 0, dhidden, 0.0)
    grad_gain_up = jnp.sum(dscaled * up_proj, axis=0)
    dup = (dscaled * gain_up).astype(jnp.bfloat16)
    grad_w_up = jnp.dot(tile_rows.T, dup, preferred_element_type=jnp.float32)
    return (
        grad_w_up,
        grad_w_down,
        grad_gain_up,
        grad_gain_down,
        grad_attn_v,
        grad_attn_u,
        grad_attn_w,
    )


def per_device(
    tiles, counts, slide_ids, pooled_cot, w_up, w_down, gain_up, gain_down, attn_v, attn_u, attn_w
):
    slot_total = tiles.shape[1]
    positions = tiles.shape[2]
    feat_width = tiles.shape[3]
    local_tiles = tiles[0]
    slide_list = slide_ids[0]
    slide_total = pooled_cot.shape[0]
    slide_range = jnp.arange(slide_total, dtype=jnp.int32)
    weights_all = (w_up, w_down, gain_up, gain_down, attn_v, attn_u, attn_w)
    tile_axis = lax.axis_size("tile")
    my_index = lax.axis_index("tile")
    every_count, every_list = (
        lax.all_gather(counts.reshape(1), "tile", axis=0, tiled=True),
        lax.all_gather(slide_list, "tile", axis=0, tiled=True),
    )
    every_list = every_list.reshape(tile_axis, slot_total)
    offsets = jnp.cumsum(every_count) - every_count
    peer_ids = jnp.arange(tile_axis, dtype=jnp.int32)
    own_offset = jnp.sum(jnp.where(peer_ids == my_index, offsets, 0))
    pair_depth = -(-slot_total // tile_axis)
    rounds = jnp.arange(pair_depth, dtype=jnp.int32)
    send_slot = (peer_ids[:, None] - own_offset) % tile_axis + rounds[None, :] * tile_axis
    outgoing = local_tiles[jnp.minimum(send_slot, slot_total - 1)]
    incoming = lax.all_to_all(outgoing, "tile", split_axis=0, concat_axis=0, tiled=True)
    came_slot = (my_index - offsets[:, None]) % tile_axis + rounds[None, :] * tile_axis
    live_slots = came_slot < every_count[:, None]
    target = (offsets[:, None] + came_slot) // tile_axis
    own_range = jnp.arange(OWN, dtype=jnp.int32)
    pick_table = (target.reshape(-1)[None, :] == own_range[:, None]) & live_slots.reshape(-1)[
        None, :
    ]
    flat_rows = incoming.reshape(tile_axis * pair_depth, positions * feat_width)
    picked = jnp.dot(
        pick_table.astype(jnp.bfloat16), flat_rows, preferred_element_type=jnp.float32
    ).astype(jnp.bfloat16)
    came_slide = jnp.take_along_axis(every_list, jnp.minimum(came_slot, slot_total - 1), axis=1)
    slide_of = jnp.sum(jnp.where(pick_table, came_slide.reshape(-1)[None, :], 0), axis=1)
    tile_rows = picked.reshape(-1, feat_width)
    member = (slide_of[:, None] == slide_range[None, :]).astype(jnp.float32)
    saved_state = forward(tile_rows, *weights_all, positions)
    features = saved_state[5]
    weight = saved_state[9]
    numerator = jnp.dot(member.T, weight[:, None] * features, precision=HIGHEST)
    denominator = jnp.sum(member * weight[:, None], axis=0)
    numerator, denominator = lax.psum((numerator, denominator), "tile")
    pooled = numerator / denominator[:, None]
    cot_full = lax.all_gather(pooled_cot, "tile", axis=1, tiled=True).astype(jnp.float32)
    gradients = backward(
        tile_rows, saved_state, member, pooled, denominator, cot_full, *weights_all, positions
    )
    gradients = lax.psum(
        (
            gradients[0],
            gradients[1],
            gradients[2],
            gradients[3],
            gradients[4],
            gradients[5],
            gradients[6],
        ),
        ("slide", "tile"),
    )
    return (pooled,) + tuple(gradients)


def solution(mesh):
    return jax.shard_map(
        per_device,
        mesh=mesh,
        in_specs=(
            P("slide", "tile", None, None),
            P("slide", "tile"),
            P("slide", "tile"),
            P("slide", "tile"),
            P(),
            P(),
            P(),
            P(),
            P(),
            P(),
            P(),
        ),
        out_specs=(P("slide", None), P(), P(), P(), P(), P(), P(), P()),
        check_vma=False,
    )
```

profile of v0, /device:TPU:1, one launch (start us, length us, event | category | flops | bytes accessed | tf_op | source)
XLA Modules:
  0.0 604.6 jit_solution(680273303178870075)
XLA Ops:
  7.9 1.3 dynamic-slice
  10.5 0.8 bitcast_dynamic-update-slice_fusion
  11.3 18.7 %all-reduce.2 = (s32[32]{0:T(128)S(1)}, s32[1024]{0:T(1024)S(1)}) all-reduce(s32[32]{0:T(128)S(1)} %bitcast_dynamic-update-slice_fusion.1, s32[1024]{0:T(1024)S(1)} %bitcast_dynamic-update-slice_fusion), channel_id=2, replica_groups=mesh['slide'=8,'tile'=32] {'tile'}, use_global_device_ids=true, to_apply=%add | all-reduce | flops 1056 | bytes 8448 | tf_op jit(solution)/shard_map/all_gather | solution.py:120
  32.4 5.0 gather_fusion
  37.4 8.5 %all-to-all-start = ((bf16[32,1,64,1024]{3,2,1,0:T(8,128)(2,1)}), bf16[32,1,64,1024]{3,2,1,0:T(8,128)(2,1)}, u32[]{:S(2)}, u32[]{:S(2)}) async-start(bf16[32,1,64,1024]{3,2,1,0:T(8,128)(2,1)} %bitcast.55), calls=%async_computation | async-start | bytes 8388608 | tf_op jit(solution)/shard_map/all_to_all | solution.py:131
  46.0 126.7 %all-gather.2 = bf16[32,32,4]{1,2,0:T(4,128)(2,1)S(1)} all-gather(bf16[1,32,4]{1,2,0:T(4,128)(2,1)S(1)} %bitcast.59), channel_id=1, replica_groups=mesh['slide'=8,'tile'=32] {'tile'}, dimensions={0}, use_global_device_ids=true | all-gather | bytes 8448 | tf_op jit(solution)/shard_map/all_gather | solution.py:154
  173.1 4.5 copy.26
  177.6 2.0 convolution_convert_fusion
  179.7 2.2 reshape.226
  182.7 2.9 bitcast_reduce_fusion
  186.5 123.2 %all-reduce.5 = (f32[4,1024]{1,0:T(4,128)S(1)}, f32[4]{0:T(128)S(1)}) all-reduce(f32[4,1024]{1,0:T(4,128)S(1)} %fusion.16, f32[4]{0:T(128)S(1)} %select_reduce_fusion.2), channel_id=1, replica_groups=mesh['slide'=8,'tile'=32] {'tile'}, use_global_device_ids=true, to_apply=%region_5.6 | all-reduce | flops 4100 | bytes 32800 | tf_op jit(solution)/shard_map/psum | solution.py:152
  310.8 1.6 fusion.7
  312.3 3.5 fusion.3
  315.8 1.7 fusion.14
  317.6 0.8 multiply_reduce_fusion
  318.3 1.6 fusion.41
  319.9 1.6 fusion.38
  321.5 1.7 fusion.12
  323.4 80.0 %all-reduce.3 = (f32[256]{0:T(256)}, f32[1024]{0:T(1024)}, f32[256]{0:T(256)}) all-reduce(f32[256]{0:T(256)S(1)} %get-tuple-element.36, f32[1024]{0:T(1024)S(1)} %get-tuple-element.25, f32[256]{0:T(256)S(1)} %multiply_reduce_fusion.1), channel_id=1, replica_groups=mesh['slide'=8,'tile'=32] {'slide','tile'}, use_global_device_ids=true, to_apply=%region_14.15 | all-reduce | flops 1536 | bytes 12288 | tf_op jit(solution)/shard_map/psum | solution.py:158
  403.4 187.7 %all-reduce.8.cloned.1.call-done = (f32[1024,256]{1,0:T(8,128)}, f32[256,1024]{1,0:T(8,128)}, f32[1024,256]{1,0:T(8,128)}, f32[1024,256]{1,0:T(8,128)}) async-done(((f32[1024,256]{1,0:T(8,128)}, f32[256,1024]{1,0:T(8,128)}, f32[1024,256]{1,0:T(8,128)}, f32[1024,256]{1,0:T(8,128)}), (f32[1024,256]{1,0:T(8,128)}, f32[256,1024]{1,0:T(8,128)}, f32[1024,256]{1,0:T(8,128)}, ...) | async-done | bytes 4194320 | tf_op jit(solution)/shard_map/psum | solution.py:158
  591.1 2.4 copy.34
  593.5 2.3 copy.35
  595.8 1.0 copy.36
  596.8 1.0 copy.37
  (62 shorter events, 6.3 us)
Async XLA Ops:
  7.2 175.5 %copy-start = (bf16[256,1024]{1,0:T(8,128)(2,1)S(1)}, bf16[256,1024]{1,0:T(8,128)(2,1)}, u32[]{:S(2)}) copy-start(bf16[256,1024]{1,0:T(8,128)(2,1)} %param.16) | copy-start | bytes 1572868
  37.4 8.6 %copy-start.11 = (bf16[4,32]{1,0:T(4,128)(2,1)S(1)}, bf16[4,32]{1,0:T(4,128)(2,1)}, u32[]{:S(2)}) copy-start(bf16[4,32]{1,0:T(4,128)(2,1)} %param.14) | copy-start | bytes 772
  37.4 135.7 %all-to-all-start = ((bf16[32,1,64,1024]{3,2,1,0:T(8,128)(2,1)}), bf16[32,1,64,1024]{3,2,1,0:T(8,128)(2,1)}, u32[]{:S(2)}, u32[]{:S(2)}) async-start(bf16[32,1,64,1024]{3,2,1,0:T(8,128)(2,1)} %bitcast.55), calls=%async_computation | async-start | bytes 8388608 | tf_op jit(solution)/shard_map/all_to_all | solution.py:131
  45.9 545.2 %all-reduce.8.cloned.1.call-start = ((), (), s32[]{:S(2)}) async-start(), calls=%async_computation.1 | async-start | bytes 8388608 | tf_op jit(solution)/shard_map/psum | solution.py:158
  177.6 4.3 copy-start.12
  179.7 3.0 copy-start.9
  179.7 3.0 copy-start.10
  182.7 3.2 copy-start.1
  182.7 3.0 copy-start.4
  182.7 3.2 copy-start.3
  182.7 3.2 copy-start.8
  309.9 6.0 copy-start.7
  312.3 3.5 copy-start.2
  591.1 4.7 copy-start.6
  591.1 5.7 copy-start.5
Sparse Core Ops, SparseCore 0:
  323.4 267.6 all-reduce.7
where the time goes:
time: 606 us; the launch traced here: 605 us
  blocking collectives  349 us (58%)
  waiting for transfers between devices  188 us (31%)
  local copies, waits for them, and re-layouts  22.2 us (4%)
  matrix products  16.4 us (3%)
  between operations  15.7 us (3%)
  starting transfers between devices  8.55 us (1%)
    psum x1, waiting for transfers between devices, per_device(): lax.psum((gradients[0], gradients[1], gradients[2], gradients[3], gradien...  188 us
    all_gather x1, blocking collectives, per_device(): lax.all_gather(pooled_cot, 'tile', axis=1, tiled=True).astype(jnp.float32)  127 us
    psum x1, blocking collectives, per_device(): numerator, denominator = lax.psum((numerator, denominator), 'tile')  123 us
    psum x1, blocking collectives, per_device(): lax.psum((gradients[0], gradients[1], gradients[2], gradients[3], gradien...  80 us
    all_gather x1, blocking collectives, per_device(): lax.all_gather(counts.reshape(1), 'tile', axis=0, tiled=True)  18.7 us
    unnamed x39, local copies, waits for them, and re-layouts  14.2 us
  transfers between devices with their start and end apart: 2, of which 1 were waited for; matrix products, arithmetic and copies ran while one was open for 0% of the time, Pallas kernels for 0%

commit v1 on v0

v1 whole, which is shorter than its diff:
```python
import jax
import jax.numpy as jnp
from jax import lax
from jax.experimental import pallas as pl
from jax.experimental.pallas import tpu as pltpu
from jax.sharding import Mesh
from jax.sharding import PartitionSpec as P

F32 = jnp.float32
BF16 = jnp.bfloat16

FINE = ("x_lo", "y", "x_hi", "z", "core")
SLIDE = ("x_lo", "y")
TILE = ("x_hi", "z", "core")
PEERS = ("x_hi", "z")
PLANE = ("x_lo", "y", "x_hi")
N_PEERS = 16
N_PLANE = 16
N_Z = 8

SLOTS = 32
POS = 64
FEAT = 1024
BOT = 256
ATT = 256
LANE = 128
STEPS = 4
GROUP = SLOTS // STEPS
PIECE = 32
HALF = 16
BLOCKS = FEAT // LANE
MAIN = PIECE * BLOCKS
TALL = MAIN + HALF
ROWS = GROUP * POS

VMEM_LIMIT = 48 * 1024 * 1024


def params():
    return pltpu.CompilerParams(vmem_limit_bytes=VMEM_LIMIT)


def nn(a, b):
    return jnp.dot(a, b, preferred_element_type=F32)


def nt(a, b):
    return lax.dot_general(a, b, (((1,), (1,)), ((), ())), preferred_element_type=F32)


def tn(a, b):
    return lax.dot_general(a, b, (((0,), (0,)), ((), ())), preferred_element_type=F32)


def sigmoid(v):
    return 1.0 / (1.0 + jnp.exp(-v))


def column(row):
    n = row.shape[1]
    i = lax.broadcasted_iota(jnp.int32, (n, n), 0)
    j = lax.broadcasted_iota(jnp.int32, (n, n), 1)
    return jnp.sum(jnp.where(i == j, jnp.broadcast_to(row, (n, n)), 0), axis=1, keepdims=True)


def members(ids_ref, count):
    ids = column(ids_ref[...])
    slot = lax.broadcasted_iota(jnp.int32, (SLOTS, 1), 0)
    live = slot < count
    return [jnp.logical_and(live, ids == c) for c in range(4)], live


def split3(v):
    hi = v.astype(BF16)
    rest = v - hi.astype(F32)
    mid = rest.astype(BF16)
    low = (rest - mid.astype(F32)).astype(BF16)
    return [hi, mid, low]


def forward_kernel(
    count_ref, x_ref, ids_ref, cot_ref, wu_ref, wd_ref, gu_ref, gd_ref, av_ref, au_ref, aw_ref,
    mask_ref, hid_ref, up_ref, feat_ref, act_ref, tanh_ref, sigm_ref, weight_ref, pack_ref,
):
    step = pl.program_id(0)
    x = x_ref[...]
    up = nn(x, wu_ref[...])
    up_ref[...] = up
    hidden = jnp.maximum(up * gu_ref[...], 0.0).astype(BF16)
    hid_ref[...] = hidden
    down = nn(hidden, wd_ref[...])
    res = x.astype(F32) + down * gd_ref[...]
    positive = res > 0
    mask_ref[...] = jnp.where(positive, 1.0, 0.0).astype(BF16)
    feats = jnp.sum(jnp.maximum(res, 0.0).reshape(GROUP, POS, FEAT), axis=1) * (1.0 / POS)
    acts = jnp.sum(jnp.where(positive, down, 0.0).reshape(GROUP, POS, FEAT), axis=1)
    at = pl.ds(pl.multiple_of(step * GROUP, GROUP), GROUP)
    feat_ref[at, :] = feats
    act_ref[at, :] = acts

    @pl.when(step == STEPS - 1)
    def _():
        feat = feat_ref[...]
        feat_b = feat.astype(BF16)
        tanh = jnp.tanh(nn(feat_b, av_ref[...]))
        sigm = sigmoid(nn(feat_b, au_ref[...]))
        tanh_ref[...] = tanh
        sigm_ref[...] = sigm
        weight = sigmoid(jnp.sum(tanh * sigm * aw_ref[...], axis=1, keepdims=True))
        weight_ref[...] = jnp.broadcast_to(weight, (SLOTS, LANE))
        member, _ = members(ids_ref, count_ref[0, 0])
        for c in range(4):
            share = jnp.where(member[c], weight, 0.0)
            num = jnp.sum(share * feat, axis=0, keepdims=True)
            den = jnp.sum(share, axis=0, keepdims=True)
            for r in range(8):
                pack_ref[8 * c + r : 8 * c + r + 1, :] = num[:, LANE * r : LANE * (r + 1)]
            pack_ref[36 + c : 37 + c, :] = jnp.broadcast_to(den, (1, LANE))
        quarter = lax.rem(lax.axis_index("z"), 2) * 2 + lax.axis_index("core")
        lane = lax.broadcasted_iota(jnp.int32, (4, LANE), 1)
        mine = jnp.logical_and(lane >= quarter * 32, lane < quarter * 32 + 32)
        cot = cot_ref[...].astype(F32)
        cot = jnp.concatenate([cot, cot, cot, cot], axis=1)
        pack_ref[32:36, :] = jnp.where(mine, cot, 0.0)


def pair_kernel(mine_ref, other_ref, out_ref):
    half = lax.axis_index("core") * 16
    at = pl.ds(pl.multiple_of(half, 16), 16)
    top = mine_ref[at, :] + other_ref[at, :]
    tail = mine_ref[32:40, :] + other_ref[32:40, :]
    for p in range(N_PEERS):
        out_ref[p, 0:16, :] = top
        out_ref[p, 16:24, :] = tail


def middle_kernel(
    count_ref, ids_ref, got_ref, other_ref, feat_ref, act_ref, tanh_ref, sigm_ref, weight_ref,
    av_ref, au_ref, aw_ref, gd_ref,
    back_ref, pooled_ref, small_ref, keep_ref, send_ref,
):
    core = lax.axis_index("core")
    total = got_ref[0]
    total_o = other_ref[0, 0:16, :]
    for p in range(1, N_PEERS):
        total = total + got_ref[p]
        total_o = total_o + other_ref[p, 0:16, :]
    low = jnp.where(core == 0, total[0:16], total_o)
    high = jnp.where(core == 0, total_o, total[0:16])
    cot = jnp.concatenate(
        [got_ref[2 * b, 16:20, :] + got_ref[2 * b + 1, 16:20, :] for b in range(8)], axis=1
    )
    member, live = members(ids_ref, count_ref[0, 0])
    cot_tile = jnp.zeros((SLOTS, FEAT), F32)
    pooled_tile = jnp.zeros((SLOTS, FEAT), F32)
    den_tile = jnp.where(live, 0.0, 1.0)
    for c in range(4):
        part = (low, high)[c // 2]
        base = 8 * (c % 2)
        num = jnp.concatenate([part[base + r : base + r + 1, :] for r in range(8)], axis=1)
        den = total[20 + c : 21 + c, 0:1]
        pooled = num / den
        pooled_ref[c : c + 1, :] = pooled
        cot_tile = jnp.where(member[c], cot[c : c + 1, :], cot_tile)
        pooled_tile = jnp.where(member[c], pooled, pooled_tile)
        den_tile = jnp.where(member[c], den, den_tile)
    feat = feat_ref[...]
    tanh = tanh_ref[...]
    sigm = sigm_ref[...]
    weight = weight_ref[:, 0:1]
    aw = aw_ref[...]
    dweight = jnp.sum(cot_tile * (feat - pooled_tile), axis=1, keepdims=True) / den_tile
    dscore = dweight * weight * (1.0 - weight)
    grad_aw = jnp.sum(dscore * tanh * sigm, axis=0, keepdims=True)
    grad_t = dscore * aw * sigm * (1.0 - tanh * tanh)
    grad_s = dscore * aw * tanh * sigm * (1.0 - sigm)
    parts_t = jnp.concatenate(split3(grad_t), axis=0)
    parts_s = jnp.concatenate(split3(grad_s), axis=0)
    feat_b = feat.astype(BF16)
    feat_3 = jnp.concatenate([feat_b, feat_b, feat_b], axis=0)
    grad_v = tn(parts_t, feat_3)
    grad_u = tn(parts_s, feat_3)

    @pl.when(core == 0)
    def _():
        keep_ref[...] = grad_v
        send_ref[...] = grad_u.astype(BF16)

    @pl.when(core != 0)
    def _():
        keep_ref[...] = grad_u
        send_ref[...] = grad_v.astype(BF16)

    from_t = nt(parts_t, av_ref[...])
    from_s = nt(parts_s, au_ref[...])
    dfeat = (weight / den_tile) * cot_tile
    dfeat = dfeat + (from_t[0:32] + from_t[32:64] + from_t[64:96])
    dfeat = dfeat + (from_s[0:32] + from_s[32:64] + from_s[64:96])
    dfeat = dfeat * (1.0 / POS)
    back_ref[...] = (dfeat * gd_ref[...]).astype(BF16).astype(F32)
    grad_gd = jnp.sum(dfeat * act_ref[...], axis=0, keepdims=True)
    for r in range(8):
        small_ref[r : r + 1, :] = grad_gd[:, LANE * r : LANE * (r + 1)]
    for r in range(2):
        small_ref[8 + r : 9 + r, :] = grad_aw[:, LANE * r : LANE * (r + 1)]
    small_ref[10:16, :] = jnp.zeros((6, LANE), F32)


def backward_kernel(
    x_ref, mask_ref, hid_ref, up_ref, back_ref, small_ref, wd_ref, gu_ref,
    keep_ref, send_ref, extra_ref, down_acc, up_acc, gain_acc,
):
    step = pl.program_id(0)

    @pl.when(step == 0)
    def _():
        down_acc[...] = jnp.zeros_like(down_acc)
        up_acc[...] = jnp.zeros_like(up_acc)
        gain_acc[...] = jnp.zeros_like(gain_acc)

    rows = back_ref[pl.ds(pl.multiple_of(step * GROUP, GROUP), GROUP), :].astype(BF16)
    dback = jnp.concatenate(
        [
            mask_ref[POS * k : POS * (k + 1), :] * jnp.broadcast_to(rows[k : k + 1, :], (POS, FEAT))
            for k in range(GROUP)
        ],
        axis=0,
    )
    down_acc[...] += tn(hid_ref[...], dback)
    dhid = nt(dback, wd_ref[...])
    up = up_ref[...]
    gu = gu_ref[...]
    dscaled = jnp.where(up * gu > 0, dhid, 0.0)
    gain_acc[...] += jnp.sum((dscaled * up).reshape(ROWS // 8, 8, BOT), axis=0)
    dup = (dscaled * gu).astype(BF16)
    up_acc[...] += tn(dup, x_ref[...])

    @pl.when(step == STEPS - 1)
    def _():
        core = lax.axis_index("core")
        gain = jnp.sum(gain_acc[...], axis=0, keepdims=True)
        small = jnp.concatenate(
            [
                small_ref[0:10, :],
                gain[:, 0:LANE],
                gain[:, LANE : 2 * LANE],
                jnp.zeros((HALF - 12, LANE), F32),
            ],
            axis=0,
        )
        down = down_acc[...]
        up_grad = up_acc[...]
        send_ref[BOT : BOT + HALF, :] = jnp.zeros((HALF, FEAT), BF16)

        @pl.when(core == 0)
        def _():
            keep_ref[...] = down
            extra_ref[...] = small
            send_ref[0:BOT, :] = up_grad.astype(BF16)

        @pl.when(core != 0)
        def _():
            keep_ref[...] = up_grad
            extra_ref[...] = jnp.zeros((HALF, LANE), F32)
            send_ref[0:BOT, :] = down.astype(BF16)
            send_ref[BOT : BOT + HALF, 0:LANE] = small.astype(BF16)


def paired_kernel(keep_a_ref, got_a_ref, keep_b_ref, got_b_ref, extra_ref, out_ref):
    for p in range(N_PLANE):
        at = slice(HALF * p, HALF * (p + 1))
        for j in range(BLOCKS):
            lanes = slice(LANE * j, LANE * (j + 1))
            sum_a = keep_a_ref[at, lanes] + got_a_ref[at, lanes].astype(F32)
            sum_b = keep_b_ref[at, lanes] + got_b_ref[at, lanes].astype(F32)
            out_ref[p, PIECE * j : PIECE * j + HALF, :] = sum_a.astype(BF16)
            out_ref[p, PIECE * j + HALF : PIECE * (j + 1), :] = sum_b.astype(BF16)
        if p == 0:
            small = extra_ref[...] + got_b_ref[BOT : BOT + HALF, 0:LANE].astype(F32)
            out_ref[p, MAIN:TALL, :] = small.astype(BF16)
        else:
            out_ref[p, MAIN:TALL, :] = jnp.zeros((HALF, LANE), BF16)


def plane_sum_kernel(got_ref, out_ref):
    total = got_ref[0].astype(F32)
    for p in range(1, N_PLANE):
        total = total + got_ref[p].astype(F32)
    for j in range(N_Z):
        out_ref[j, 0:PIECE, :] = total[PIECE * j : PIECE * (j + 1)]
        out_ref[j, PIECE:, :] = total[MAIN:TALL]


def z_sum_kernel(got_ref, out_ref, small_ref):
    total = got_ref[0]
    for p in range(1, N_Z):
        total = total + got_ref[p]
    main = total[0:PIECE].astype(BF16)
    for j in range(N_Z):
        out_ref[j] = main
    small_ref[...] = total[PIECE:].astype(BF16)


def join_kernel(got_ref, small_ref, out_ref):
    for p in range(N_PLANE):
        for j in range(N_Z):
            out_ref[p, PIECE * j : PIECE * (j + 1), :] = got_ref[j]
        out_ref[p, MAIN:TALL, :] = small_ref[...]


def unpack_kernel(
    mine_ref, other_ref, sm_ref, so_ref,
    up_ref, down_ref, v_ref, u_ref, gup_ref, gdown_ref, aw_ref,
):
    first = lax.axis_index("core") == 0
    for j in range(2):
        attn = slice(PIECE * j, PIECE * j + HALF)
        enc = slice(PIECE * j + HALF, PIECE * (j + 1))
        lanes = slice(LANE * j, LANE * (j + 1))
        am = mine_ref[:, attn, :].astype(F32).reshape(ATT, LANE)
        ao = other_ref[:, attn, :].astype(F32).reshape(ATT, LANE)
        bm = mine_ref[:, enc, :].astype(F32).reshape(BOT, LANE)
        bo = other_ref[:, enc, :].astype(F32).reshape(BOT, LANE)
        v_ref[lanes, :] = jnp.where(first, am, ao).T
        u_ref[lanes, :] = jnp.where(first, ao, am).T
        down_ref[:, lanes] = jnp.where(first, bm, bo)
        up_ref[lanes, :] = jnp.where(first, bo, bm).T
    small = jnp.where(first, sm_ref[0].astype(F32), so_ref[0].astype(F32))
    for r in range(8):
        gdown_ref[:, LANE * r : LANE * (r + 1)] = small[r : r + 1, :]
    for r in range(2):
        aw_ref[:, LANE * r : LANE * (r + 1)] = small[8 + r : 9 + r, :]
        gup_ref[:, LANE * r : LANE * (r + 1)] = small[10 + r : 11 + r, :]


def whole_spec(shape):
    return pl.BlockSpec(shape, lambda *_: (0,) * len(shape))


def call(body, outs, *args, name):
    return pl.pallas_call(
        body,
        out_shape=[jax.ShapeDtypeStruct(s, d) for s, d in outs],
        compiler_params=params(),
        name=name,
    )(*args)


def swap(v):
    return lax.ppermute(v, "core", [(0, 1), (1, 0)])


def in_hbm(*arrays):
    return [pltpu.with_memory_space_constraint(v, pltpu.HBM) for v in arrays]


def reduce_all(keep_a, got_a, keep_b, got_b, extra):
    pieces = (N_PLANE, TALL, LANE)
    (paired,) = call(
        paired_kernel, [(pieces, BF16)], keep_a, got_a, keep_b, got_b, extra, name="paired"
    )
    got = lax.all_to_all(paired, PLANE, 0, 0, tiled=True)
    (parts,) = call(
        plane_sum_kernel, [((N_Z, PIECE + HALF, LANE), F32)], got, name="plane_sum"
    )
    got = lax.all_to_all(parts, "z", 0, 0, tiled=True)
    main, small = call(
        z_sum_kernel,
        [((N_Z, PIECE, LANE), BF16), ((HALF, LANE), BF16)],
        got,
        name="z_sum",
    )
    got = lax.all_to_all(main, "z", 0, 0, tiled=True)
    (whole,) = call(join_kernel, [(pieces, BF16)], got, small, name="join")
    return lax.all_to_all(whole, PLANE, 0, 0, tiled=True)


def per_device(
    tiles, counts, slide_ids, pooled_cot, w_up, w_down, gain_up, gain_down, attn_v, attn_u, attn_w
):
    rows = tiles.reshape(SLOTS * POS, FEAT)
    gu = gain_up.reshape(1, BOT)
    gd = gain_down.reshape(1, FEAT)
    aw = attn_w.reshape(1, ATT)
    smem = pl.BlockSpec(memory_space=pltpu.SMEM)
    mask, hid, up, feat, act, tanh, sigm, weight, pack = pl.pallas_call(
        forward_kernel,
        grid=(STEPS,),
        in_specs=[
            smem,
            pl.BlockSpec((ROWS, FEAT), lambda i: (i, 0)),
            whole_spec((1, SLOTS)),
            whole_spec((4, 32)),
            whole_spec((FEAT, BOT)),
            whole_spec((BOT, FEAT)),
            whole_spec((1, BOT)),
            whole_spec((1, FEAT)),
            whole_spec((FEAT, ATT)),
            whole_spec((FEAT, ATT)),
            whole_spec((1, ATT)),
        ],
        out_specs=[
            pl.BlockSpec((ROWS, FEAT), lambda i: (i, 0)),
            pl.BlockSpec((ROWS, BOT), lambda i: (i, 0)),
            pl.BlockSpec((ROWS, BOT), lambda i: (i, 0)),
            whole_spec((SLOTS, FEAT)),
            whole_spec((SLOTS, FEAT)),
            whole_spec((SLOTS, ATT)),
            whole_spec((SLOTS, ATT)),
            whole_spec((SLOTS, LANE)),
            whole_spec((40, LANE)),
        ],
        out_shape=[
            jax.ShapeDtypeStruct((SLOTS * POS, FEAT), BF16),
            jax.ShapeDtypeStruct((SLOTS * POS, BOT), BF16),
            jax.ShapeDtypeStruct((SLOTS * POS, BOT), F32),
            jax.ShapeDtypeStruct((SLOTS, FEAT), F32),
            jax.ShapeDtypeStruct((SLOTS, FEAT), F32),
            jax.ShapeDtypeStruct((SLOTS, ATT), F32),
            jax.ShapeDtypeStruct((SLOTS, ATT), F32),
            jax.ShapeDtypeStruct((SLOTS, LANE), F32),
            jax.ShapeDtypeStruct((40, LANE), F32),
        ],
        compiler_params=params(),
        name="encode",
    )(counts, *in_hbm(rows, slide_ids, pooled_cot, w_up, w_down, gu, gd, attn_v, attn_u, aw))

    (pairs,) = call(pair_kernel, [((N_PEERS, 24, LANE), F32)], pack, swap(pack), name="pair")
    got = lax.all_to_all(pairs, PEERS, 0, 0, tiled=True)
    other = swap(got)

    vmem = pl.BlockSpec(memory_space=pltpu.VMEM)
    back, pooled, small, keep_a, send_a = pl.pallas_call(
        middle_kernel,
        in_specs=[smem] + [vmem] * 12,
        out_shape=[
            jax.ShapeDtypeStruct((SLOTS, FEAT), F32),
            jax.ShapeDtypeStruct((4, FEAT), F32),
            jax.ShapeDtypeStruct((16, LANE), F32),
            jax.ShapeDtypeStruct((ATT, FEAT), F32),
            jax.ShapeDtypeStruct((ATT, FEAT), BF16),
        ],
        compiler_params=params(),
        name="middle",
    )(counts, slide_ids, got, other, feat, act, tanh, sigm, weight, attn_v, attn_u, aw, gd)

    got_a = swap(send_a)
    keep_b, send_b, extra = pl.pallas_call(
        backward_kernel,
        grid=(STEPS,),
        in_specs=[
            pl.BlockSpec((ROWS, FEAT), lambda i: (i, 0)),
            pl.BlockSpec((ROWS, FEAT), lambda i: (i, 0)),
            pl.BlockSpec((ROWS, BOT), lambda i: (i, 0)),
            pl.BlockSpec((ROWS, BOT), lambda i: (i, 0)),
            whole_spec((SLOTS, FEAT)),
            whole_spec((16, LANE)),
            whole_spec((BOT, FEAT)),
            whole_spec((1, BOT)),
        ],
        out_specs=[
            whole_spec((BOT, FEAT)),
            whole_spec((BOT + HALF, FEAT)),
            whole_spec((HALF, LANE)),
        ],
        out_shape=[
            jax.ShapeDtypeStruct((BOT, FEAT), F32),
            jax.ShapeDtypeStruct((BOT + HALF, FEAT), BF16),
            jax.ShapeDtypeStruct((HALF, LANE), F32),
        ],
        scratch_shapes=[
            pltpu.VMEM((BOT, FEAT), F32),
            pltpu.VMEM((BOT, FEAT), F32),
            pltpu.VMEM((8, BOT), F32),
        ],
        compiler_params=params(),
        name="backward",
    )(rows, mask, hid, up, back, small, w_down, gu)

    mine = reduce_all(keep_a, got_a, keep_b, swap(send_b), extra)
    other = swap(mine)

    part = pl.BlockSpec((N_PLANE, 2 * PIECE, LANE), lambda i: (0, i, 0))
    tail = pl.BlockSpec((1, HALF, LANE), lambda i: (0, MAIN // HALF, 0))
    wide = pl.BlockSpec((BOT, 2 * LANE), lambda i: (0, i))
    tall = pl.BlockSpec((2 * LANE, BOT), lambda i: (i, 0))
    g_up, g_down, g_v, g_u, g_gu, g_gd, g_aw = pl.pallas_call(
        unpack_kernel,
        grid=(4,),
        in_specs=[part, part, tail, tail],
        out_specs=[
            tall,
            wide,
            tall,
            tall,
            whole_spec((1, BOT)),
            whole_spec((1, FEAT)),
            whole_spec((1, ATT)),
        ],
        out_shape=[
            jax.ShapeDtypeStruct((FEAT, BOT), F32),
            jax.ShapeDtypeStruct((BOT, FEAT), F32),
            jax.ShapeDtypeStruct((FEAT, ATT), F32),
            jax.ShapeDtypeStruct((FEAT, ATT), F32),
            jax.ShapeDtypeStruct((1, BOT), F32),
            jax.ShapeDtypeStruct((1, FEAT), F32),
            jax.ShapeDtypeStruct((1, ATT), F32),
        ],
        compiler_params=params(),
        name="unpack",
    )(mine, other, mine, other)
    return (
        pooled,
        g_up,
        g_down,
        g_gu.reshape(BOT),
        g_gd.reshape(FEAT),
        g_v,
        g_u,
        g_aw.reshape(ATT),
    )


def solution(mesh):
    fine = Mesh(mesh.devices.reshape(2, 4, 2, 8, 2), FINE)
    return jax.shard_map(
        per_device,
        mesh=fine,
        in_specs=(
            P(SLIDE, TILE, None, None),
            P(SLIDE, TILE),
            P(SLIDE, TILE),
            P(SLIDE, TILE),
            P(),
            P(),
            P(),
            P(),
            P(),
            P(),
            P(),
        ),
        out_specs=(P(SLIDE, None), P(), P(), P(), P(), P(), P(), P()),
        check_vma=False,
    )
```

time: 606 us -> 121 us (0.20)
  blocking collectives: 349 us -> 77.8 us
  waiting for transfers between devices: 188 us -> 6.49 us
  Pallas kernels: 0 us -> 23.4 us
  local copies, waits for them, and re-layouts: 22.2 us -> 0.03 us
  matrix products: 16.4 us -> 0 us
  between operations: 15.7 us -> 1.38 us
    psum x2 -> x0, blocking collectives: 203 us -> none  [the longest x1 123 us: per_device(): numerator, denominator = lax.psum((numerator, denominator), 'tile')]
    psum x1 -> x0, waiting for transfers between devices: 188 us -> none  [per_device(): lax.psum((gradients[0], gradients[1], gradients[2], gradients[3], gradien...]
    all_gather x2 -> x0, blocking collectives: 145 us -> none  [the longest x1 127 us: per_device(): lax.all_gather(pooled_cot, 'tile', axis=1, tiled=True).astype(jnp.float32)]
    all_to_all x0 -> x5, blocking collectives: none -> 77.8 us  [the longest x1 22.4 us: reduce_all(): got = lax.all_to_all(paired, PLANE, 0, 0, tiled=True)]
    pallas_call x0 -> x9, Pallas kernels: none -> 23.4 us  [the longest x1 9.56 us: per_device(): pl.pallas_call(forward_kernel, grid=(STEPS,), in_specs=[smem, pl.BlockSpe...]
    dot_general x15 -> x0, matrix products: 16.4 us -> none  [the longest x1 2.91 us: forward(): down_proj = jnp.dot(hidden, w_down, preferred_element_type=jnp.float32)]
    unnamed x39 -> x14, local copies, waits for them, and re-layouts: 14.2 us -> 0.03 us
    ppermute x0 -> x5, starting transfers between devices: none -> 11.5 us  [swap(): return lax.ppermute(v, 'core', [(0, 1), (1, 0)])]
  transfers between devices with their start and end apart: 2 -> 5, of which waited for: 1 -> 4; matrix products, arithmetic and copies ran while one was open for 0% -> 0% of each run, Pallas kernels for 0% -> 0%
where the time goes in v1:
time: 121 us
  blocking collectives  77.8 us (64%)
  Pallas kernels  23.4 us (19%)
  starting transfers between devices  11.5 us (10%)
  waiting for transfers between devices  6.49 us (5%)
  between operations  1.38 us (1%)
    all_to_all x1, blocking collectives, reduce_all(): got = lax.all_to_all(paired, PLANE, 0, 0, tiled=True)  22.4 us
    all_to_all x1, blocking collectives, per_device(): got = lax.all_to_all(pairs, PEERS, 0, 0, tiled=True)  17.9 us
    all_to_all x1, blocking collectives, reduce_all(): return lax.all_to_all(whole, PLANE, 0, 0, tiled=True)  16.1 us
    all_to_all x1, blocking collectives, reduce_all(): got = lax.all_to_all(parts, 'z', 0, 0, tiled=True)  11.7 us
    ppermute x5, starting transfers between devices, swap(): return lax.ppermute(v, 'core', [(0, 1), (1, 0)])  11.5 us
    all_to_all x1, blocking collectives, reduce_all(): got = lax.all_to_all(main, 'z', 0, 0, tiled=True)  9.6 us
    pallas_call x1, Pallas kernels, per_device(): pl.pallas_call(forward_kernel, grid=(STEPS,), in_specs=[smem, pl.BlockSpe...  9.56 us
    pallas_call x1, Pallas kernels, per_device(): pl.pallas_call(backward_kernel, grid=(STEPS,), in_specs=[pl.BlockSpec((RO...  8.63 us
  transfers between devices with their start and end apart: 5, of which 4 were waited for; matrix products, arithmetic and copies ran while one was open for 0% of the time, Pallas kernels for 0%

profile of v1, /device:TPU:1, one launch (start us, length us, event | category | flops | bytes accessed | tf_op | source)
XLA Modules:
  0.0 120.7 jit_solution(10503164924215870072)
XLA Ops:
  1.3 9.6 %encode.1 = (bf16[2048,1024]{1,0:T(8,128)(2,1)}, bf16[2048,256]{1,0:T(8,128)(2,1)S(1)}, f32[2048,256]{1,0:T(8,128)S(1)}, f32[32,1024]{1,0:T(8,128)S(1)}, f32[32,...) custom-call(s32[1,1]{1,0:T(1,128)S(6)} %copy.19.count_ref, ...), custom_call_target="tpu_custom_call" | custom-call | tf_op jit(solution)/shard_map/encode/pallas_call | solution.py:386
  10.9 3.2 %collective-permute-start = (f32[40,128]{1,0:T(8,128)S(1)}, f32[40,128]{1,0:T(8,128)S(1)}, u32[]{:S(2)}, u32[]{:S(2)}) collective-permute-start(f32[40,128]{1,0:T(8,128)S(1)} %get-tuple-element.34.mine_ref), channel_id=1, source_target_pairs={{0,1},{1,0},{2,3},{3,2},{4,5},{5,4},{6,7},{7,6},{8,9},{9,8},{10,11... | collective-permute-start | bytes 61448 | tf_op jit(solution)/shard_map/ppermute | solution.py:350
  14.1 0.8 collective-permute-done.other_ref
  15.0 0.0 copy-start
  15.0 0.0 copy-start.5
  15.0 17.9 %all_to_all.25.got_ref = f32[16,24,128]{2,1,0:T(8,128)S(1)} all-to-all(f32[16,24,128]{2,1,0:T(8,128)S(1)} %pair.1), channel_id=1, replica_groups=mesh['x_lo'=2,'y'=4,'x_hi'=2,'z'=8,'core'=2] {'x_hi','z'}, dimensions={0} | all-to-all | bytes 393216 | tf_op jit(solution)/shard_map/all_to_all | solution.py:429
  32.9 2.2 %collective-permute-start.1 = (f32[16,24,128]{2,1,0:T(8,128)S(1)}, f32[16,24,128]{2,1,0:T(8,128)S(1)}, u32[]{:S(2)}, u32[]{:S(2)}) collective-permute-start(f32[16,24,128]{2,1,0:T(8,128)S(1)} %all_to_all.25.got_ref), channel_id=1, source_target_pairs={{0,1},{1,0},{2,3},{3,2},{4,5},{5,4},{6,7},{7,6},{8,9},{9,8},{10,11... | collective-permute-start | bytes 589832 | tf_op jit(solution)/shard_map/ppermute | solution.py:350
  35.1 1.1 collective-permute-done.1.other_ref
  36.2 1.8 %middle.1 = (f32[32,1024]{1,0:T(8,128)S(1)}, f32[4,1024]{1,0:T(4,128)}, f32[16,128]{1,0:T(8,128)S(1)}, f32[256,1024]{1,0:T(8,128)S(1)}, bf16[256,1024]{1,0:T(8,128)(2,1)S(1)}) custom-call(s32[1,1]{1,0:T(1,128)S(6)} %copy.19.count_ref, s32[1,32]{1,0:T(1,128)S(1)} %copy-done.6, f32[16,24,128]{2,1,0:T(8,128)S(1)} %all_to_all.25.got_ref, ...), custom_call_target="tpu_custom_call" | custom-call | tf_op jit(solution)/shard_map/middle/pallas_call | solution.py:433
  38.0 8.6 %backward.1 = (f32[256,1024]{1,0:T(8,128)S(1)}, bf16[272,1024]{1,0:T(8,128)(2,1)S(1)}, f32[16,128]{1,0:T(8,128)S(1)}) custom-call(bf16[2048,1024]{1,0:T(8,128)(2,1)} %bitcast.14, bf16[2048,1024]{1,0:T(8,128)(2,1)} %get-tuple-element.43.mask_ref, bf16[2048,256]{1,0:T(8,128)(2,1)S(1)} %get-tuple-element.44.hid_ref, f32[2048,256]{1,0:T(8,128)S(1)} %get-tuple-element.45.up_ref, ...), custom_call_target="tpu_custom_call" | custom-call | tf_op jit(solution)/shard_map/backward/pallas_call | solution.py:448
  46.6 0.4 collective-permute-start.3
  47.0 0.2 collective-permute-start.2
  47.2 2.2 %collective-permute-done.2.got_a_ref = bf16[256,1024]{1,0:T(8,128)(2,1)S(1)} collective-permute-done((bf16[256,1024]{1,0:T(8,128)(2,1)S(1)}, bf16[256,1024]{1,0:T(8,128)(2,1)S(1)}, u32[]{:S(2)}, u32[]{:S(2)}) %collective-permute-start.2) | collective-permute-done | bytes 524320 | tf_op jit(solution)/shard_map/ppermute | solution.py:350
  49.4 0.0 collective-permute-done.3.got_b_ref
  49.4 0.2 paired.1
  49.7 22.4 %all_to_all.26.got_ref = bf16[16,272,128]{2,1,0:T(8,128)(2,1)S(1)} all-to-all(bf16[16,272,128]{2,1,0:T(8,128)(2,1)S(1)} %paired.1), channel_id=1, replica_groups=mesh['x_lo'=2,'y'=4,'x_hi'=2,'z'=8,'core'=2] {'x_lo','y','x_hi'}, dimensions={0} | all-to-all | bytes 2228224 | tf_op jit(solution)/shard_map/all_to_all | solution.py:362
  72.1 0.1 plane_sum.1
  72.3 11.7 %all_to_all.27.got_ref = f32[8,48,128]{2,1,0:T(8,128)S(1)} all-to-all(f32[8,48,128]{2,1,0:T(8,128)S(1)} %plane_sum.1), channel_id=1, replica_groups=mesh['x_lo'=2,'y'=4,'x_hi'=2,'z'=8,'core'=2] {'z'}, dimensions={0} | all-to-all | bytes 393216 | tf_op jit(solution)/shard_map/all_to_all | solution.py:366
  84.0 9.6 %all_to_all.28.got_ref = bf16[8,32,128]{2,1,0:T(8,128)(2,1)S(1)} all-to-all(bf16[8,32,128]{2,1,0:T(8,128)(2,1)S(1)} %get-tuple-element.51), channel_id=1, replica_groups=mesh['x_lo'=2,'y'=4,'x_hi'=2,'z'=8,'core'=2] {'z'}, dimensions={0} | all-to-all | bytes 131072 | tf_op jit(solution)/shard_map/all_to_all | solution.py:373
  93.6 0.1 join.1
  93.8 16.1 %all_to_all.29.mine_ref.sm_ref = bf16[16,272,128]{2,1,0:T(8,128)(2,1)S(1)} all-to-all(bf16[16,272,128]{2,1,0:T(8,128)(2,1)S(1)} %join.1), channel_id=1, replica_groups=mesh['x_lo'=2,'y'=4,'x_hi'=2,'z'=8,'core'=2] {'x_lo','y','x_hi'}, dimensions={0} | all-to-all | bytes 2228224 | tf_op jit(solution)/shard_map/all_to_all | solution.py:375
  109.9 5.5 %collective-permute-start.4 = (bf16[16,272,128]{2,1,0:T(8,128)(2,1)S(1)}, bf16[16,272,128]{2,1,0:T(8,128)(2,1)S(1)}, u32[]{:S(2)}, u32[]{:S(2)}) collective-permute-start(bf16[16,272,128]{2,1,0:T(8,128)(2,1)S(1)} %all_to_all.29.mine_ref.sm_ref), channel_id=1, source_target_pairs={{0,1},{1,0},{2,3},{3,2},{4,5},{5,4},{6,7},{7,6},{8,9},{9,8},{10,11... | collective-permute-start | bytes 3342344 | tf_op jit(solution)/shard_map/ppermute | solution.py:350
  115.4 2.4 %collective-permute-done.4.other_ref.so_ref = bf16[16,272,128]{2,1,0:T(8,128)(2,1)S(1)} collective-permute-done((bf16[16,272,128]{2,1,0:T(8,128)(2,1)S(1)}, bf16[16,272,128]{2,1,0:T(8,128)(2,1)S(1)}, u32[]{:S(2)}, u32[]{:S(2)}) %collective-permute-start.4) | collective-permute-done | bytes 1114144 | tf_op jit(solution)/shard_map/ppermute | solution.py:350
  117.8 2.9 %unpack.1 = (f32[1024,256]{1,0:T(8,128)}, f32[256,1024]{1,0:T(8,128)}, f32[1024,256]{1,0:T(8,128)}, f32[1024,256]{1,0:T(8,128)}, f32[1,256]{1,0:T(1,128)}, /*index=5*/f32[1,1024]{1,0:T(1,128)}, f32[1,256]{1,0:T(1,128)}) custom-call(bf16[16,272,128]{2,1,0:T(8,128)(2,1)S(1)} %all_to_all.29.mine_ref.sm_ref, ...), custom_call_target="tpu_custom_call" | custom-call | tf_op jit(solution)/shard_map/unpack/pallas_call | solution.py:487
  (14 shorter events, 0.1 us)
Async XLA Ops:
  1.3 34.9 %copy-start.1 = (bf16[1024,256]{1,0:T(8,128)(2,1)S(1)}, bf16[1024,256]{1,0:T(8,128)(2,1)}, u32[]{:S(2)}) copy-start(bf16[1024,256]{1,0:T(8,128)(2,1)} %av_ref.3) | copy-start | bytes 1572868
  1.3 34.9 %copy-start.2 = (bf16[1024,256]{1,0:T(8,128)(2,1)S(1)}, bf16[1024,256]{1,0:T(8,128)(2,1)}, u32[]{:S(2)}) copy-start(bf16[1024,256]{1,0:T(8,128)(2,1)} %au_ref.3) | copy-start | bytes 1572868
  1.3 34.9 %copy-start.3 = (f32[1024]{0:T(1024)S(1)}, f32[1024]{0:T(1024)}, u32[]{:S(2)}) copy-start(f32[1024]{0:T(1024)} %param.18) | copy-start | bytes 12292
  1.3 34.9 %copy-start.4 = (f32[256]{0:T(256)S(1)}, f32[256]{0:T(256)}, u32[]{:S(2)}) copy-start(f32[256]{0:T(256)} %param.21) | copy-start | bytes 3076
  1.3 34.9 %copy-start.6 = (s32[1,32]{1,0:T(1,128)S(1)}, s32[1,32]{1,0:T(1,128)}, u32[]{:S(2)}) copy-start(s32[1,32]{1,0:T(1,128)} %ids_ref.3) | copy-start | bytes 388
  10.9 4.1 %collective-permute-start = (f32[40,128]{1,0:T(8,128)S(1)}, f32[40,128]{1,0:T(8,128)S(1)}, u32[]{:S(2)}, u32[]{:S(2)}) collective-permute-start(f32[40,128]{1,0:T(8,128)S(1)} %get-tuple-element.34.mine_ref), channel_id=1, source_target_pairs={{0,1},{1,0},{2,3},{3,2},{4,5},{5,4},{6,7},{7,6},{8,9},{9,8},{10,11... | collective-permute-start | bytes 61448 | tf_op jit(solution)/shard_map/ppermute | solution.py:350
  15.0 23.0 %copy-start = (bf16[256,1024]{1,0:T(8,128)(2,1)S(1)}, bf16[256,1024]{1,0:T(8,128)(2,1)}, u32[]{:S(2)}) copy-start(bf16[256,1024]{1,0:T(8,128)(2,1)} %wd_ref.3) | copy-start | bytes 1572868
  15.0 23.0 %copy-start.5 = (f32[256]{0:T(256)S(1)}, f32[256]{0:T(256)}, u32[]{:S(2)}) copy-start(f32[256]{0:T(256)} %param.17) | copy-start | bytes 3076
  32.9 3.2 %collective-permute-start.1 = (f32[16,24,128]{2,1,0:T(8,128)S(1)}, f32[16,24,128]{2,1,0:T(8,128)S(1)}, u32[]{:S(2)}, u32[]{:S(2)}) collective-permute-start(f32[16,24,128]{2,1,0:T(8,128)S(1)} %all_to_all.25.got_ref), channel_id=1, source_target_pairs={{0,1},{1,0},{2,3},{3,2},{4,5},{5,4},{6,7},{7,6},{8,9},{9,8},{10,11... | collective-permute-start | bytes 589832 | tf_op jit(solution)/shard_map/ppermute | solution.py:350
  46.6 2.8 %collective-permute-start.3 = (bf16[272,1024]{1,0:T(8,128)(2,1)S(1)}, bf16[272,1024]{1,0:T(8,128)(2,1)S(1)}, u32[]{:S(2)}, u32[]{:S(2)}) collective-permute-start(bf16[272,1024]{1,0:T(8,128)(2,1)S(1)} %get-tuple-element.49), channel_id=1, source_target_pairs={{0,1},{1,0},{2,3},{3,2},{4,5},{5,4},{6,7},{7,6},{8,9},{9,8},{10,11... | collective-permute-start | bytes 1671176 | tf_op jit(solution)/shard_map/ppermute | solution.py:350
  47.0 2.4 %collective-permute-start.2 = (bf16[256,1024]{1,0:T(8,128)(2,1)S(1)}, bf16[256,1024]{1,0:T(8,128)(2,1)S(1)}, u32[]{:S(2)}, u32[]{:S(2)}) collective-permute-start(bf16[256,1024]{1,0:T(8,128)(2,1)S(1)} %get-tuple-element.42), channel_id=1, source_target_pairs={{0,1},{1,0},{2,3},{3,2},{4,5},{5,4},{6,7},{7,6},{8,9},{9,8},{10,11... | collective-permute-start | bytes 1572872 | tf_op jit(solution)/shard_map/ppermute | solution.py:350
  109.9 7.9 %collective-permute-start.4 = (bf16[16,272,128]{2,1,0:T(8,128)(2,1)S(1)}, bf16[16,272,128]{2,1,0:T(8,128)(2,1)S(1)}, u32[]{:S(2)}, u32[]{:S(2)}) collective-permute-start(bf16[16,272,128]{2,1,0:T(8,128)(2,1)S(1)} %all_to_all.29.mine_ref.sm_ref), channel_id=1, source_target_pairs={{0,1},{1,0},{2,3},{3,2},{4,5},{5,4},{6,7},{7,6},{8,9},{9,8},{10,11... | collective-permute-start | bytes 3342344 | tf_op jit(solution)/shard_map/ppermute | solution.py:350

commit v2 on v1

v2 whole, which is shorter than its diff:
```python
import functools

import jax
import jax.numpy as jnp
from jax import lax
from jax.experimental import pallas as pl
from jax.experimental.pallas import tpu as pltpu
from jax.sharding import Mesh
from jax.sharding import PartitionSpec as P

F32 = jnp.float32
BF16 = jnp.bfloat16

FINE = ("x_lo", "y", "x_hi", "z", "core")
SLIDE = ("x_lo", "y")
TILE = ("x_hi", "z", "core")
PLANE = ("x_lo", "y", "x_hi")
N_PLANE = 16
N_Z = 8

SLOTS = 32
POS = 64
FEAT = 1024
BOT = 256
ATT = 256
LANE = 128
STEPS = 4
GROUP = SLOTS // STEPS
PIECE = 32
HALF = 16
BLOCKS = FEAT // LANE
MAIN = PIECE * BLOCKS
TALL = MAIN + HALF
ROWS = GROUP * POS

CHUNKS = 8
CHUNK = SLOTS * POS // CHUNKS
LOADS = (512, 1536)

VMEM_LIMIT = 24 * 1024 * 1024
VMEM = pl.BlockSpec(memory_space=pltpu.VMEM)


def params():
    return pltpu.CompilerParams(vmem_limit_bytes=VMEM_LIMIT)


def nn(a, b):
    return jnp.dot(a, b, preferred_element_type=F32)


def nt(a, b):
    return lax.dot_general(a, b, (((1,), (1,)), ((), ())), preferred_element_type=F32)


def tn(a, b):
    return lax.dot_general(a, b, (((0,), (0,)), ((), ())), preferred_element_type=F32)


def sigmoid(v):
    return 1.0 / (1.0 + jnp.exp(-v))


def column(row):
    n = row.shape[1]
    i = lax.broadcasted_iota(jnp.int32, (n, n), 0)
    j = lax.broadcasted_iota(jnp.int32, (n, n), 1)
    return jnp.sum(jnp.where(i == j, jnp.broadcast_to(row, (n, n)), 0), axis=1, keepdims=True)


def members(ids_ref):
    ids = column(ids_ref[...])
    return [ids == c for c in range(4)], ids >= 0


def split3(v):
    hi = v.astype(BF16)
    rest = v - hi.astype(F32)
    mid = rest.astype(BF16)
    low = (rest - mid.astype(F32)).astype(BF16)
    return [hi, mid, low]


def slopes(tanh, sigm, aw):
    return aw * sigm * (1.0 - tanh * tanh), aw * tanh * sigm * (1.0 - sigm)


def forward_kernel(
    x_hbm, wu_hbm, wd_hbm, gu_hbm, gd_hbm, av_hbm, au_hbm, aw_hbm, ids_hbm, cot_hbm,
    x_ref, hid_ref, up_ref, feat_ref, tanh_ref, sigm_ref, weight_ref, pack_ref,
    wu_ref, wd_ref, gu_ref, gd_ref, av_ref, au_ref, aw_ref, ids_ref, cot_ref, sems,
):
    starts = [sum(LOADS[:i]) for i in range(len(LOADS))]
    loads = []
    for i, start in enumerate(starts):
        at = pl.ds(start, LOADS[i])
        loads.append(pltpu.make_async_copy(x_hbm.at[at, :], x_ref.at[at, :], sems.at[i]))
    pairs = [
        (wu_hbm, wu_ref),
        (gu_hbm, gu_ref),
        (wd_hbm, wd_ref),
        (gd_hbm, gd_ref),
        (av_hbm, av_ref),
        (au_hbm, au_ref),
        (aw_hbm, aw_ref),
        (ids_hbm, ids_ref),
        (cot_hbm, cot_ref),
    ]
    others = [
        pltpu.make_async_copy(src, dst, sems.at[len(LOADS) + i])
        for i, (src, dst) in enumerate(pairs)
    ]
    others[0].start()
    loads[0].start()
    for copy in others[1:4]:
        copy.start()
    for copy in loads[1:]:
        copy.start()
    for copy in others[4:]:
        copy.start()
    for copy in others[:4]:
        copy.wait()
    for i in range(CHUNKS):
        at = slice(i * CHUNK, (i + 1) * CHUNK)
        if i * CHUNK in starts:
            loads[starts.index(i * CHUNK)].wait()
        x = x_ref[at, :]
        up = nn(x, wu_ref[...])
        up_ref[at, :] = up
        hidden = jnp.maximum(up * gu_ref[...], 0.0).astype(BF16)
        hid_ref[at, :] = hidden
        down = nn(hidden, wd_ref[...])
        res = x.astype(F32) + down * gd_ref[...]
        feats = jnp.sum(jnp.maximum(res, 0.0).reshape(CHUNK // POS, POS, FEAT), axis=1)
        feat_ref[i * CHUNK // POS : (i + 1) * CHUNK // POS, :] = feats * (1.0 / POS)
    for copy in others[4:]:
        copy.wait()
    feat = feat_ref[...]
    feat_b = feat.astype(BF16)
    tanh = jnp.tanh(nn(feat_b, av_ref[...]))
    sigm = sigmoid(nn(feat_b, au_ref[...]))
    tanh_ref[...] = tanh
    sigm_ref[...] = sigm
    weight = sigmoid(jnp.sum(tanh * sigm * aw_ref[...], axis=1, keepdims=True))
    weight_ref[...] = jnp.broadcast_to(weight, (SLOTS, LANE))
    member, _ = members(ids_ref)
    for c in range(4):
        share = jnp.where(member[c], weight, 0.0)
        num = jnp.sum(share * feat, axis=0, keepdims=True)
        den = jnp.sum(share, axis=0, keepdims=True)
        for r in range(8):
            pack_ref[8 * c + r : 8 * c + r + 1, :] = num[:, LANE * r : LANE * (r + 1)]
        pack_ref[36 + c : 37 + c, :] = jnp.broadcast_to(den, (1, LANE))
    quarter = lax.rem(lax.axis_index("z"), 2) * 2 + lax.axis_index("core")
    lane = lax.broadcasted_iota(jnp.int32, (4, LANE), 1)
    mine = jnp.logical_and(lane >= quarter * 32, lane < quarter * 32 + 32)
    cot = cot_ref[...].astype(F32)
    cot = jnp.concatenate([cot, cot, cot, cot], axis=1)
    pack_ref[32:36, :] = jnp.where(mine, cot, 0.0)


def keep_kernel(
    x_ref, hid_ref, wd_ref, gd_ref, tanh_ref, sigm_ref, aw_ref, av_ref, au_ref,
    mask_ref, act_ref, slope_ref,
):
    for i in range(CHUNKS):
        at = slice(i * CHUNK, (i + 1) * CHUNK)
        down = nn(hid_ref[at, :], wd_ref[...])
        positive = x_ref[at, :].astype(F32) + down * gd_ref[...] > 0
        mask_ref[at, :] = jnp.where(positive, 1.0, 0.0).astype(BF16)
        acts = jnp.where(positive, down, 0.0).reshape(CHUNK // POS, POS, FEAT)
        act_ref[i * CHUNK // POS : (i + 1) * CHUNK // POS, :] = jnp.sum(acts, axis=1)
    slope_t, slope_s = slopes(tanh_ref[...], sigm_ref[...], aw_ref[...])
    from_t = nt(jnp.concatenate(split3(slope_t), axis=0), av_ref[...])
    from_s = nt(jnp.concatenate(split3(slope_s), axis=0), au_ref[...])
    total = from_t[0:32] + from_t[32:64] + from_t[64:96]
    slope_ref[...] = total + (from_s[0:32] + from_s[32:64] + from_s[64:96])


def pair_kernel(mine_ref, other_ref, out_ref):
    out_ref[...] = mine_ref[...] + other_ref[...]


def spread_kernel(mine_ref, other_ref, out_ref):
    first = lax.axis_index("x_hi") == 0
    mine = mine_ref[...]
    other = other_ref[...]
    total = mine + other
    row = lax.broadcasted_iota(jnp.int32, (40, LANE), 0)
    cot = jnp.logical_and(row >= 32, row < 36)
    low = jnp.where(cot, jnp.where(first, mine, other), total)
    high = jnp.where(first, other, mine)[32:36]
    for p in range(N_Z):
        out_ref[p, 0:40, :] = low
        out_ref[p, 40:44, :] = high
        out_ref[p, 44:48, :] = high


def middle_kernel(
    ids_ref, got_ref, feat_ref, act_ref, slope_ref, tanh_ref, sigm_ref, weight_ref,
    aw_ref, gd_ref,
    back_ref, pooled_ref, small_ref, keep_ref, send_ref,
):
    core = lax.axis_index("core")
    total = got_ref[0]
    for p in range(1, N_Z):
        total = total + got_ref[p]
    cot = jnp.concatenate(
        [
            got_ref[2 * b, row : row + 4, :] + got_ref[2 * b + 1, row : row + 4, :]
            for row in (32, 40)
            for b in range(N_Z // 2)
        ],
        axis=1,
    )
    member, live = members(ids_ref)
    cot_tile = jnp.zeros((SLOTS, FEAT), F32)
    pooled_tile = jnp.zeros((SLOTS, FEAT), F32)
    den_tile = jnp.where(live, 0.0, 1.0)
    for c in range(4):
        num = jnp.concatenate([total[8 * c + r : 8 * c + r + 1, :] for r in range(8)], axis=1)
        den = total[36 + c : 37 + c, 0:1]
        pooled = num / den
        pooled_ref[c : c + 1, :] = pooled
        cot_tile = jnp.where(member[c], cot[c : c + 1, :], cot_tile)
        pooled_tile = jnp.where(member[c], pooled, pooled_tile)
        den_tile = jnp.where(member[c], den, den_tile)
    feat = feat_ref[...]
    tanh = tanh_ref[...]
    sigm = sigm_ref[...]
    weight = weight_ref[:, 0:1]
    aw = aw_ref[...]
    dweight = jnp.sum(cot_tile * (feat - pooled_tile), axis=1, keepdims=True) / den_tile
    dscore = dweight * weight * (1.0 - weight)
    grad_aw = jnp.sum(dscore * tanh * sigm, axis=0, keepdims=True)
    slope_t, slope_s = slopes(tanh, sigm, aw)
    parts_t = jnp.concatenate(split3(dscore * slope_t), axis=0)
    parts_s = jnp.concatenate(split3(dscore * slope_s), axis=0)
    feat_b = feat.astype(BF16)
    feat_3 = jnp.concatenate([feat_b, feat_b, feat_b], axis=0)
    grad_v = tn(parts_t, feat_3)
    grad_u = tn(parts_s, feat_3)

    @pl.when(core == 0)
    def _():
        keep_ref[...] = grad_v
        send_ref[...] = grad_u.astype(BF16)

    @pl.when(core != 0)
    def _():
        keep_ref[...] = grad_u
        send_ref[...] = grad_v.astype(BF16)

    dfeat = ((weight / den_tile) * cot_tile + dscore * slope_ref[...]) * (1.0 / POS)
    back_ref[...] = (dfeat * gd_ref[...]).astype(BF16).astype(F32)
    grad_gd = jnp.sum(dfeat * act_ref[...], axis=0, keepdims=True)
    for r in range(8):
        small_ref[r : r + 1, :] = grad_gd[:, LANE * r : LANE * (r + 1)]
    for r in range(2):
        small_ref[8 + r : 9 + r, :] = grad_aw[:, LANE * r : LANE * (r + 1)]
    small_ref[10:16, :] = jnp.zeros((6, LANE), F32)


def backward_kernel(
    x_ref, mask_ref, hid_ref, up_ref, back_ref, small_ref, wd_ref, gu_ref,
    keep_ref, send_ref, extra_ref, dback_ref, dup_ref,
):
    gu = gu_ref[...]
    gain = jnp.zeros((8, BOT), F32)
    for i in range(STEPS):
        at = slice(ROWS * i, ROWS * (i + 1))
        for k in range(GROUP):
            tile = GROUP * i + k
            row = back_ref[tile : tile + 1, :].astype(BF16)
            here = slice(POS * tile, POS * (tile + 1))
            dback_ref[here, :] = mask_ref[here, :] * jnp.broadcast_to(row, (POS, FEAT))
        dhid = nt(dback_ref[at, :], wd_ref[...])
        up = up_ref[at, :]
        dscaled = jnp.where(up * gu > 0, dhid, 0.0)
        gain = gain + jnp.sum((dscaled * up).reshape(ROWS // 8, 8, BOT), axis=0)
        dup_ref[at, :] = (dscaled * gu).astype(BF16)
    gain = jnp.sum(gain, axis=0, keepdims=True)
    small = jnp.concatenate(
        [
            small_ref[0:10, :],
            gain[:, 0:LANE],
            gain[:, LANE : 2 * LANE],
            jnp.zeros((HALF - 12, LANE), F32),
        ],
        axis=0,
    )
    first = lax.axis_index("core") == 0
    down = tn(hid_ref[...], dback_ref[...])
    up_grad = tn(dup_ref[...], x_ref[...])

    @pl.when(first)
    def _():
        keep_ref[...] = down
        extra_ref[...] = small
        send_ref[0:BOT, :] = up_grad.astype(BF16)

    @pl.when(jnp.logical_not(first))
    def _():
        keep_ref[...] = up_grad
        extra_ref[...] = jnp.zeros((HALF, LANE), F32)
        send_ref[0:BOT, :] = down.astype(BF16)

    sent = jnp.where(first, 0.0, small)
    high = sent.astype(BF16)
    send_ref[BOT : BOT + HALF, :] = jnp.zeros((HALF, FEAT), BF16)
    send_ref[BOT : BOT + HALF, 0:LANE] = high
    send_ref[BOT : BOT + HALF, LANE : 2 * LANE] = (sent - high.astype(F32)).astype(BF16)


def two_terms(row):
    high = row.astype(BF16).astype(F32)
    rows = lax.broadcasted_iota(jnp.int32, (HALF, LANE), 0)
    block = jnp.where(rows == 0, high, jnp.where(rows == 1, row - high, 0.0))
    return block.astype(BF16)


def paired_kernel(keep_a_ref, got_a_ref, keep_b_ref, got_b_ref, extra_ref, out_ref):
    for p in range(N_PLANE):
        at = slice(HALF * p, HALF * (p + 1))
        for j in range(BLOCKS):
            lanes = slice(LANE * j, LANE * (j + 1))
            sum_a = keep_a_ref[at, lanes] + got_a_ref[at, lanes].astype(F32)
            sum_b = keep_b_ref[at, lanes] + got_b_ref[at, lanes].astype(F32)
            out_ref[p, PIECE * j : PIECE * j + HALF, :] = sum_a.astype(BF16)
            out_ref[p, PIECE * j + HALF : PIECE * (j + 1), :] = sum_b.astype(BF16)
        cols = slice(0, LANE), slice(LANE, 2 * LANE)
        small = extra_ref[p : p + 1, :]
        for col in cols:
            small = small + got_b_ref[BOT : BOT + HALF, col].astype(F32)[p : p + 1, :]
        out_ref[p, MAIN:TALL, :] = two_terms(small)


def small_row(block):
    return block[MAIN : MAIN + 1, :].astype(F32) + block[MAIN + 1 : MAIN + 2, :].astype(F32)


def plane_sum_kernel(got_ref, out_ref):
    total = got_ref[0].astype(F32)
    for p in range(1, N_PLANE):
        total = total + got_ref[p].astype(F32)
    out_ref[0:MAIN, :] = total[0:MAIN].astype(BF16)
    out_ref[MAIN:TALL, :] = two_terms(small_row(total))


def z_pair_kernel(mine_ref, other_ref, out_ref):
    total = mine_ref[0:MAIN, :].astype(F32) + other_ref[0:MAIN, :].astype(F32)
    out_ref[0:MAIN, :] = total.astype(BF16)
    out_ref[MAIN:TALL, :] = two_terms(small_row(mine_ref) + small_row(other_ref))


def z_sum_kernel(mine_ref, near_ref, far_ref, cross_ref, out_ref):
    near = mine_ref[0:MAIN, :].astype(F32) + near_ref[0:MAIN, :].astype(F32)
    far = far_ref[0:MAIN, :].astype(F32) + cross_ref[0:MAIN, :].astype(F32)
    main = (near + far).astype(BF16)
    near = small_row(mine_ref) + small_row(near_ref)
    far = small_row(far_ref) + small_row(cross_ref)
    small = two_terms(near + far)
    for p in range(N_PLANE):
        out_ref[p, 0:MAIN, :] = main
        out_ref[p, MAIN:TALL, :] = small


def unpack_kernel(own, got_ref, *refs):
    up_hbm, down_hbm, v_hbm, u_hbm, gup_hbm, gdown_hbm, aw_hbm = refs[-14:-7]
    attn_ref, down_ref, up_ref, gup_ref, gdown_ref, aw_ref, sems = refs[-7:]
    first = (lax.axis_index("core") == 0) if own else (lax.axis_index("core") != 0)
    to_v = pltpu.make_async_copy(attn_ref, v_hbm, sems.at[0])
    to_u = pltpu.make_async_copy(attn_ref, u_hbm, sems.at[0])
    to_down = pltpu.make_async_copy(down_ref, down_hbm, sems.at[1])
    to_up = pltpu.make_async_copy(up_ref, up_hbm, sems.at[1])
    smalls = [
        pltpu.make_async_copy(gup_ref, gup_hbm, sems.at[2]),
        pltpu.make_async_copy(gdown_ref, gdown_hbm, sems.at[3]),
        pltpu.make_async_copy(aw_ref, aw_hbm, sems.at[4]),
    ]
    for j in range(BLOCKS):
        rows = slice(PIECE * j, PIECE * j + HALF)
        attn = got_ref[:, rows, :].astype(F32).reshape(ATT, LANE)
        attn_ref[LANE * j : LANE * (j + 1), :] = attn.T

    @pl.when(first)
    def _():
        to_v.start()
        for j in range(BLOCKS):
            rows = slice(PIECE * j + HALF, PIECE * (j + 1))
            enc = got_ref[:, rows, :].astype(F32).reshape(BOT, LANE)
            down_ref[:, LANE * j : LANE * (j + 1)] = enc
        to_down.start()
        for r in range(12):
            block = got_ref[r, MAIN:TALL, :].astype(F32)
            small = block[0:1, :] + block[1:2, :]
            if r < 8:
                gdown_ref[:, LANE * r : LANE * (r + 1)] = small
            elif r < 10:
                aw_ref[:, LANE * (r - 8) : LANE * (r - 7)] = small
            else:
                gup_ref[:, LANE * (r - 10) : LANE * (r - 9)] = small
        for copy in smalls:
            copy.start()
        to_v.wait()
        to_down.wait()
        for copy in smalls:
            copy.wait()

    @pl.when(jnp.logical_not(first))
    def _():
        to_u.start()
        for j in range(BLOCKS):
            rows = slice(PIECE * j + HALF, PIECE * (j + 1))
            enc = got_ref[:, rows, :].astype(F32).reshape(BOT, LANE)
            up_ref[LANE * j : LANE * (j + 1), :] = enc.T
        to_up.start()
        to_u.wait()
        to_up.wait()


def whole_spec(shape):
    return pl.BlockSpec(shape, lambda *_: (0,) * len(shape))


def call(body, outs, *args, name):
    return pl.pallas_call(
        body,
        out_shape=[jax.ShapeDtypeStruct(s, d) for s, d in outs],
        compiler_params=params(),
        name=name,
    )(*args)


def swap(v, axis):
    return lax.ppermute(v, axis, [(0, 1), (1, 0)])


def in_hbm(*arrays):
    return [pltpu.with_memory_space_constraint(v, pltpu.HBM) for v in arrays]


def reduce_all(keep_a, got_a, keep_b, got_b, extra):
    pieces = (N_PLANE, TALL, LANE)
    (paired,) = call(
        paired_kernel, [(pieces, BF16)], keep_a, got_a, keep_b, got_b, extra, name="paired"
    )
    got = lax.all_to_all(paired, PLANE, 0, 0, tiled=True)
    flat = [(pieces[1:], BF16)]
    (part,) = call(plane_sum_kernel, flat, got, name="plane_sum")
    (pair,) = call(z_pair_kernel, flat, part, cross_z(part, 1), name="z_pair")
    (whole,) = call(
        z_sum_kernel,
        [(pieces, BF16)],
        pair, cross_z(pair, 2), cross_z(pair, 4), cross_z(pair, 6),
        name="z_sum",
    )
    return lax.all_to_all(whole, PLANE, 0, 0, tiled=True)


def cross_z(v, bits):
    return lax.ppermute(v, "z", [(i, i ^ bits) for i in range(N_Z)])


def unpack(got, *before):
    hbm = pl.BlockSpec(memory_space=pltpu.HBM)
    shapes = [
        (FEAT, BOT), (BOT, FEAT), (FEAT, ATT), (FEAT, ATT), (1, BOT), (1, FEAT), (1, ATT)
    ]
    return pl.pallas_call(
        functools.partial(unpack_kernel, not before),
        in_specs=[VMEM] + [hbm] * len(before),
        out_specs=[hbm] * len(shapes),
        out_shape=[jax.ShapeDtypeStruct(v, F32) for v in shapes],
        input_output_aliases={1 + i: i for i in range(len(before))},
        scratch_shapes=[
            pltpu.VMEM((FEAT, ATT), F32),
            pltpu.VMEM((BOT, FEAT), F32),
            pltpu.VMEM((FEAT, BOT), F32),
            pltpu.VMEM((1, BOT), F32),
            pltpu.VMEM((1, FEAT), F32),
            pltpu.VMEM((1, ATT), F32),
            pltpu.SemaphoreType.DMA((5,)),
        ],
        compiler_params=params(),
        name="unpack_other" if before else "unpack_own",
    )(got, *before)


def encode(
    rows, ids, pooled_cot, w_up, w_down, gu, gd, attn_v, attn_u, aw
):
    hbm = pl.BlockSpec(memory_space=pltpu.HBM)
    outs = [
        ((SLOTS * POS, FEAT), BF16),
        ((SLOTS * POS, BOT), BF16),
        ((SLOTS * POS, BOT), F32),
        ((SLOTS, FEAT), F32),
        ((SLOTS, ATT), F32),
        ((SLOTS, ATT), F32),
        ((SLOTS, LANE), F32),
        ((40, LANE), F32),
    ]
    return pl.pallas_call(
        forward_kernel,
        in_specs=[hbm] * 10,
        out_specs=[VMEM] * len(outs),
        out_shape=[jax.ShapeDtypeStruct(s, d) for s, d in outs],
        scratch_shapes=[
            pltpu.VMEM((FEAT, BOT), BF16),
            pltpu.VMEM((BOT, FEAT), BF16),
            pltpu.VMEM((1, BOT), F32),
            pltpu.VMEM((1, FEAT), F32),
            pltpu.VMEM((FEAT, ATT), BF16),
            pltpu.VMEM((FEAT, ATT), BF16),
            pltpu.VMEM((1, ATT), F32),
            pltpu.VMEM((1, SLOTS), jnp.int32),
            pltpu.VMEM((4, 32), BF16),
            pltpu.SemaphoreType.DMA((len(LOADS) + 9,)),
        ],
        compiler_params=params(),
        name="encode",
    )(*in_hbm(rows, w_up, w_down, gu, gd, attn_v, attn_u, aw, ids, pooled_cot))


def backward(x, mask, hid, up, back, small, w_down, gu):
    return pl.pallas_call(
        backward_kernel,
        in_specs=[VMEM] * 8,
        out_shape=[
            jax.ShapeDtypeStruct((BOT, FEAT), F32),
            jax.ShapeDtypeStruct((BOT + HALF, FEAT), BF16),
            jax.ShapeDtypeStruct((HALF, LANE), F32),
        ],
        scratch_shapes=[
            pltpu.VMEM((SLOTS * POS, FEAT), BF16),
            pltpu.VMEM((SLOTS * POS, BOT), BF16),
        ],
        compiler_params=params(),
        name="backward",
    )(x, mask, hid, up, back, small, w_down, gu)


def per_device(
    tiles, counts, slide_ids, pooled_cot, w_up, w_down, gain_up, gain_down, attn_v, attn_u, attn_w
):
    rows = tiles.reshape(SLOTS * POS, FEAT)
    gu = gain_up.reshape(1, BOT)
    gd = gain_down.reshape(1, FEAT)
    aw = attn_w.reshape(1, ATT)
    slot = lax.broadcasted_iota(jnp.int32, (1, SLOTS), 1)
    ids = jnp.where(slot < counts, slide_ids, -1)
    x, hid, up, feat, tanh, sigm, weight, pack = encode(
        rows, ids, pooled_cot, w_up, w_down, gu, gd, attn_v, attn_u, aw
    )
    (half,) = call(pair_kernel, [((40, LANE), F32)], pack, swap(pack, "core"), name="pair")
    mask, act, slope = call(
        keep_kernel,
        [((SLOTS * POS, FEAT), BF16), ((SLOTS, FEAT), F32), ((SLOTS, FEAT), F32)],
        x, hid, w_down, gd, tanh, sigm, aw, attn_v, attn_u,
        name="keep",
    )
    across, mask, act, slope = lax.optimization_barrier((swap(half, "x_hi"), mask, act, slope))
    (spread,) = call(spread_kernel, [((N_Z, 48, LANE), F32)], half, across, name="spread")
    got = lax.all_to_all(spread, "z", 0, 0, tiled=True)

    back, pooled, small, keep_a, send_a = pl.pallas_call(
        middle_kernel,
        in_specs=[VMEM] * 10,
        out_shape=[
            jax.ShapeDtypeStruct((SLOTS, FEAT), F32),
            jax.ShapeDtypeStruct((4, FEAT), F32),
            jax.ShapeDtypeStruct((16, LANE), F32),
            jax.ShapeDtypeStruct((ATT, FEAT), F32),
            jax.ShapeDtypeStruct((ATT, FEAT), BF16),
        ],
        compiler_params=params(),
        name="middle",
    )(ids, got, feat, act, slope, tanh, sigm, weight, aw, gd)

    got_a = swap(send_a, "core")
    keep_b, send_b, extra = backward(x, mask, hid, up, back, small, w_down, gu)
    got_b = swap(send_b, "core")

    mine = reduce_all(keep_a, got_a, keep_b, got_b, extra)
    other = swap(mine, "core")
    g_up, g_down, g_v, g_u, g_gu, g_gd, g_aw = unpack(other, *unpack(mine))
    return (
        pooled,
        g_up,
        g_down,
        g_gu.reshape(BOT),
        g_gd.reshape(FEAT),
        g_v,
        g_u,
        g_aw.reshape(ATT),
    )


def solution(mesh):
    fine = Mesh(mesh.devices.reshape(2, 4, 2, 8, 2), FINE)
    return jax.shard_map(
        per_device,
        mesh=fine,
        in_specs=(
            P(SLIDE, TILE, None, None),
            P(SLIDE, TILE),
            P(SLIDE, TILE),
            P(SLIDE, TILE),
            P(),
            P(),
            P(),
            P(),
            P(),
            P(),
            P(),
        ),
        out_specs=(P(SLIDE, None), P(), P(), P(), P(), P(), P(), P()),
        check_vma=False,
    )
```

time: 121 us -> 106 us (0.88)
  blocking collectives: 77.8 us -> 56.1 us
  starting transfers between devices: 11.5 us -> 18.1 us
  Pallas kernels: 23.4 us -> 18.2 us
  waiting for transfers between devices: 6.49 us -> 10.6 us
    all_to_all x3 -> x1, blocking collectives: 39.3 us -> 16.6 us  [per_device(): got = lax.all_to_all(spread, 'z', 0, 0, tiled=True)]
    pallas_call x4 -> x5, Pallas kernels: 22.9 us -> 14.5 us  [the longest x1 5.99 us: encode(): pl.pallas_call(forward_kernel, in_specs=[hbm] * 10, out_specs=[VMEM] * le...]
    ppermute x5 -> x9, starting transfers between devices: 11.5 us -> 18.1 us  [the longest x5 12 us: swap(): return lax.ppermute(v, axis, [(0, 1), (1, 0)])]
    ppermute x5 -> x9, waiting for transfers between devices: 6.49 us -> 10.6 us  [the longest x4 6.81 us: cross_z(): return lax.ppermute(v, 'z', [(i, i ^ bits) for i in range(N_Z)])]
    pallas_call x5 -> x7, Pallas kernels: 0.57 us -> 3.64 us  [call(): pl.pallas_call(body, out_shape=[jax.ShapeDtypeStruct(s, d) for s, d in ou...]
  transfers between devices with their start and end apart: 5 -> 9, of which waited for: 4 -> 6; matrix products, arithmetic and copies ran while one was open for 0% -> 0% of each run, Pallas kernels for 0% -> 5%
where the time goes in v2:
time: 106 us
  blocking collectives  56.1 us (53%)
  Pallas kernels  18.2 us (17%)
  starting transfers between devices  18.1 us (17%)
  waiting for transfers between devices  10.6 us (10%)
  between operations  1.53 us (1%)
  other arithmetic  1.17 us (1%)
    all_to_all x1, blocking collectives, reduce_all(): got = lax.all_to_all(paired, PLANE, 0, 0, tiled=True)  22.3 us
    all_to_all x1, blocking collectives, reduce_all(): return lax.all_to_all(whole, PLANE, 0, 0, tiled=True)  17.3 us
    all_to_all x1, blocking collectives, per_device(): got = lax.all_to_all(spread, 'z', 0, 0, tiled=True)  16.6 us
    ppermute x5, starting transfers between devices, swap(): return lax.ppermute(v, axis, [(0, 1), (1, 0)])  12 us
    ppermute x4, waiting for transfers between devices, cross_z(): return lax.ppermute(v, 'z', [(i, i ^ bits) for i in range(N_Z)])  6.81 us
    ppermute x4, starting transfers between devices, cross_z(): return lax.ppermute(v, 'z', [(i, i ^ bits) for i in range(N_Z)])  6.09 us
    pallas_call x1, Pallas kernels, encode(): pl.pallas_call(forward_kernel, in_specs=[hbm] * 10, out_specs=[VMEM] * le...  5.99 us
    ppermute x5, waiting for transfers between devices, swap(): return lax.ppermute(v, axis, [(0, 1), (1, 0)])  3.81 us
  transfers between devices with their start and end apart: 9, of which 6 were waited for; matrix products, arithmetic and copies ran while one was open for 0% of the time, Pallas kernels for 5%

profile of v2, /device:TPU:1, one launch (start us, length us, event | category | flops | bytes accessed | tf_op | source)
XLA Modules:
  0.0 105.7 jit_solution(15435640340900752792)
XLA Ops:
  1.3 1.2 %compare_select_fusion.ids_hbm.ids_ref = s32[1,32]{1,0:T(1,128)} fusion(s32[1,32]{1,0:T(1,128)} %param.13, s32[]{:T(128)} %bitcast.8), kind=kLoop, calls=%fused_computation | loop fusion | flops 64 | bytes 260 | tf_op jit(solution)/shard_map/jit(_where)/select_n | solution.py:552
  2.5 6.0 %encode.1 = (bf16[2048,1024]{1,0:T(8,128)(2,1)S(1)}, bf16[2048,256]{1,0:T(8,128)(2,1)S(1)}, f32[2048,256]{1,0:T(8,128)S(1)}, f32[32,1024]{1,0:T(8,128)S(1)}, f32...) custom-call(bf16[2048,1024]{1,0:T(8,128)(2,1)} %bitcast.17, ...), custom_call_target="tpu_custom_call" | custom-call | tf_op jit(solution)/shard_map/encode/pallas_call | solution.py:504
  8.5 3.3 %collective-permute-start = (f32[40,128]{1,0:T(8,128)S(1)}, f32[40,128]{1,0:T(8,128)S(1)}, u32[]{:S(2)}, u32[]{:S(2)}) collective-permute-start(f32[40,128]{1,0:T(8,128)S(1)} %get-tuple-element.45.mine_ref), channel_id=1, source_target_pairs={{0,1},{1,0},{2,3},{3,2},{4,5},{5,4},{6,7},{7,6},{8,9},{9,8},{10,11... | collective-permute-start | bytes 61448 | tf_op jit(solution)/shard_map/ppermute | solution.py:436
  11.8 0.8 collective-permute-done.other_ref
  12.6 1.0 collective-permute-start.1
  13.7 3.1 %keep.1 = (bf16[2048,1024]{1,0:T(8,128)(2,1)S(1)}, f32[32,1024]{1,0:T(8,128)S(1)}, f32[32,1024]{1,0:T(8,128)S(1)}) custom-call(bf16[2048,1024]{1,0:T(8,128)(2,1)S(1)} %get-tuple-element.46.x_ref, bf16[2048,256]{1,0:T(8,128)(2,1)S(1)} %get-tuple-element.47.hid_ref, bf16[256,1024]{1,0:T(8,128)(2,1)S(1)} %copy-done, f32[1,1024]{1,0:T(1,128)S(1)} %bitcast.10, ...), custom_call_target="tpu_custom_call" | custom-call | tf_op jit(solution)/shard_map/keep/pallas_call | solution.py:427
  16.9 16.6 %all_to_all.15.got_ref = f32[8,48,128]{2,1,0:T(8,128)S(1)} all-to-all(f32[8,48,128]{2,1,0:T(8,128)S(1)} %spread.1), channel_id=1, replica_groups=mesh['x_lo'=2,'y'=4,'x_hi'=2,'z'=8,'core'=2] {'z'}, dimensions={0} | all-to-all | bytes 393216 | tf_op jit(solution)/shard_map/all_to_all | solution.py:565
  33.5 1.5 %middle.1 = (f32[32,1024]{1,0:T(8,128)S(1)}, f32[4,1024]{1,0:T(4,128)}, f32[16,128]{1,0:T(8,128)S(1)}, f32[256,1024]{1,0:T(8,128)S(1)}, bf16[256,1024]{1,0:T(8,128)(2,1)S(1)}) custom-call(s32[1,32]{1,0:T(1,128)S(1)} %copy-done.6, f32[8,48,128]{2,1,0:T(8,128)S(1)} %all_to_all.15.got_ref, f32[32,1024]{1,0:T(8,128)S(1)} %get-tuple-element.54.feat_ref, ...), custom_call_target="tpu_custom_call" | custom-call | tf_op jit(solution)/shard_map/middle/pallas_call | solution.py:567
  34.9 3.8 %backward.1 = (f32[256,1024]{1,0:T(8,128)S(1)}, bf16[272,1024]{1,0:T(8,128)(2,1)S(1)}, f32[16,128]{1,0:T(8,128)S(1)}) custom-call(bf16[2048,1024]{1,0:T(8,128)(2,1)S(1)} %get-tuple-element.46.x_ref, bf16[2048,1024]{1,0:T(8,128)(2,1)S(1)} %get-tuple-element.61.mask_ref, bf16[2048,256]{1,0:T(8,128)(2,1)S(1)} %get-tuple-element.47.hid_ref, ...), custom_call_target="tpu_custom_call" | custom-call | tf_op jit(solution)/shard_map/backward/pallas_call | solution.py:527
  38.7 3.0 %collective-permute-start.3 = (bf16[272,1024]{1,0:T(8,128)(2,1)S(1)}, bf16[272,1024]{1,0:T(8,128)(2,1)S(1)}, u32[]{:S(2)}, u32[]{:S(2)}) collective-permute-start(bf16[272,1024]{1,0:T(8,128)(2,1)S(1)} %get-tuple-element.66), channel_id=1, source_target_pairs={{0,1},{1,0},{2,3},{3,2},{4,5},{5,4},{6,7},{7,6},{8,9},{9,8},{10,11... | collective-permute-start | bytes 1671176 | tf_op jit(solution)/shard_map/ppermute | solution.py:436
  41.9 2.2 %collective-permute-done.2.got_a_ref = bf16[256,1024]{1,0:T(8,128)(2,1)S(1)} collective-permute-done((bf16[256,1024]{1,0:T(8,128)(2,1)S(1)}, bf16[256,1024]{1,0:T(8,128)(2,1)S(1)}, u32[]{:S(2)}, u32[]{:S(2)}) %collective-permute-start.2) | collective-permute-done | bytes 524320 | tf_op jit(solution)/shard_map/ppermute | solution.py:436
  44.4 22.3 %all_to_all.16.got_ref = bf16[16,272,128]{2,1,0:T(8,128)(2,1)S(1)} all-to-all(bf16[16,272,128]{2,1,0:T(8,128)(2,1)S(1)} %paired.1), channel_id=1, replica_groups=mesh['x_lo'=2,'y'=4,'x_hi'=2,'z'=8,'core'=2] {'x_lo','y','x_hi'}, dimensions={0} | all-to-all | bytes 2228224 | tf_op jit(solution)/shard_map/all_to_all | solution.py:448
  66.8 0.3 collective-permute-start.4
  67.1 2.9 %collective-permute-done.4.other_ref = bf16[272,128]{1,0:T(8,128)(2,1)S(1)} collective-permute-done((bf16[272,128]{1,0:T(8,128)(2,1)S(1)}, bf16[272,128]{1,0:T(8,128)(2,1)S(1)}, u32[]{:S(2)}, u32[]{:S(2)}) %collective-permute-start.4) | collective-permute-done | bytes 69664 | tf_op jit(solution)/shard_map/ppermute | solution.py:462
  70.1 0.3 collective-permute-start.5
  70.4 1.9 %collective-permute-start.6 = (bf16[272,128]{1,0:T(8,128)(2,1)S(1)}, bf16[272,128]{1,0:T(8,128)(2,1)S(1)}, u32[]{:S(2)}, u32[]{:S(2)}) collective-permute-start(bf16[272,128]{1,0:T(8,128)(2,1)S(1)} %z_pair.1.mine_ref), channel_id=1, source_target_pairs={{0,8},{2,10},{4,12},{6,14},{8,0},{10,2},{12,4},{14,6},{1,9},{3,11}... | collective-permute-start | bytes 208904 | tf_op jit(solution)/shard_map/ppermute | solution.py:462
  72.3 3.5 %collective-permute-start.7 = (bf16[272,128]{1,0:T(8,128)(2,1)S(1)}, bf16[272,128]{1,0:T(8,128)(2,1)S(1)}, u32[]{:S(2)}, u32[]{:S(2)}) collective-permute-start(bf16[272,128]{1,0:T(8,128)(2,1)S(1)} %z_pair.1.mine_ref), channel_id=1, source_target_pairs={{0,12},{2,14},{4,8},{6,10},{8,4},{10,6},{12,0},{14,2},{1,13},{3,15... | collective-permute-start | bytes 208904 | tf_op jit(solution)/shard_map/ppermute | solution.py:462
  75.8 3.1 %collective-permute-done.6.far_ref = bf16[272,128]{1,0:T(8,128)(2,1)S(1)} collective-permute-done((bf16[272,128]{1,0:T(8,128)(2,1)S(1)}, bf16[272,128]{1,0:T(8,128)(2,1)S(1)}, u32[]{:S(2)}, u32[]{:S(2)}) %collective-permute-start.6) | collective-permute-done | bytes 69664 | tf_op jit(solution)/shard_map/ppermute | solution.py:462
  78.9 0.8 collective-permute-done.7.cross_ref
  79.8 17.3 %all_to_all.17.got_ref = bf16[16,272,128]{2,1,0:T(8,128)(2,1)S(1)} all-to-all(bf16[16,272,128]{2,1,0:T(8,128)(2,1)S(1)} %z_sum.1), channel_id=1, replica_groups=mesh['x_lo'=2,'y'=4,'x_hi'=2,'z'=8,'core'=2] {'x_lo','y','x_hi'}, dimensions={0} | all-to-all | bytes 2228224 | tf_op jit(solution)/shard_map/all_to_all | solution.py:458
  97.1 4.5 %collective-permute-start.8 = (bf16[16,272,128]{2,1,0:T(8,128)(2,1)S(1)}, bf16[16,272,128]{2,1,0:T(8,128)(2,1)S(1)}, u32[]{:S(2)}, u32[]{:S(2)}) collective-permute-start(bf16[16,272,128]{2,1,0:T(8,128)(2,1)S(1)} %all_to_all.17.got_ref), channel_id=1, source_target_pairs={{0,1},{1,0},{2,3},{3,2},{4,5},{5,4},{6,7},{7,6},{8,9},{9,8},{10,11... | collective-permute-start | bytes 3342344 | tf_op jit(solution)/shard_map/ppermute | solution.py:436
  101.6 1.7 %unpack_own.1 = (f32[1024,256]{1,0:T(8,128)}, f32[256,1024]{1,0:T(8,128)}, f32[1024,256]{1,0:T(8,128)}, f32[1024,256]{1,0:T(8,128)}, f32[1,256]{1,0:T(1,128)}, /*index=5*/f32[1,1024]{1,0:T(1,128)}, f32[1,256]{1,0:T(1,128)}) custom-call(bf16[16,272,128]{2,1,0:T(8,128)(2,1)S(1)} %all_to_all.17.got_ref), custom_call_target="tpu_custom_call" | custom-call | tf_op jit(solution)/shard_map/unpack_own/pallas_call | solution.py:470
  103.3 0.7 collective-permute-done.8.got_ref
  104.0 1.6 %unpack_other.1 = (f32[1024,256]{1,0:T(8,128)}, f32[256,1024]{1,0:T(8,128)}, f32[1024,256]{1,0:T(8,128)}, f32[1024,256]{1,0:T(8,128)}, f32[1,256]{1,0:T(1,128)}, /*index=5*/f32[1,1024]{1,0:T(1,128)}, f32[1,256]{1,0:T(1,128)}) custom-call(bf16[16,272,128]{2,1,0:T(8,128)(2,1)S(1)} %collective-pe, ...), custom_call_target="tpu_custom_call", output_to_operand_aliasing={{0}: (1, {}), {1}: (2, {}), {2}: (3, {}), {3}: (4, {}), {4}... | custom-call | tf_op jit(solution)/shard_map/unpack_other/pallas_call | solution.py:470
  (24 shorter events, 0.7 us)
Async XLA Ops:
  2.4 11.2 %copy-start = (bf16[256,1024]{1,0:T(8,128)(2,1)S(1)}, bf16[256,1024]{1,0:T(8,128)(2,1)}, u32[]{:S(2)}) copy-start(bf16[256,1024]{1,0:T(8,128)(2,1)} %wd_ref.3) | copy-start | bytes 1572868
  2.5 11.2 %copy-start.1 = (bf16[1024,256]{1,0:T(8,128)(2,1)S(1)}, bf16[1024,256]{1,0:T(8,128)(2,1)}, u32[]{:S(2)}) copy-start(bf16[1024,256]{1,0:T(8,128)(2,1)} %av_ref.1) | copy-start | bytes 1572868
  2.5 11.2 %copy-start.2 = (bf16[1024,256]{1,0:T(8,128)(2,1)S(1)}, bf16[1024,256]{1,0:T(8,128)(2,1)}, u32[]{:S(2)}) copy-start(bf16[1024,256]{1,0:T(8,128)(2,1)} %au_ref.1) | copy-start | bytes 1572868
  2.5 11.2 %copy-start.3 = (f32[1024]{0:T(1024)S(1)}, f32[1024]{0:T(1024)}, u32[]{:S(2)}) copy-start(f32[1024]{0:T(1024)} %param.18) | copy-start | bytes 12292
  2.5 11.2 %copy-start.4 = (f32[256]{0:T(256)S(1)}, f32[256]{0:T(256)}, u32[]{:S(2)}) copy-start(f32[256]{0:T(256)} %param.21) | copy-start | bytes 3076
  8.5 4.2 %collective-permute-start = (f32[40,128]{1,0:T(8,128)S(1)}, f32[40,128]{1,0:T(8,128)S(1)}, u32[]{:S(2)}, u32[]{:S(2)}) collective-permute-start(f32[40,128]{1,0:T(8,128)S(1)} %get-tuple-element.45.mine_ref), channel_id=1, source_target_pairs={{0,1},{1,0},{2,3},{3,2},{4,5},{5,4},{6,7},{7,6},{8,9},{9,8},{10,11... | collective-permute-start | bytes 61448 | tf_op jit(solution)/shard_map/ppermute | solution.py:436
  12.6 4.2 %collective-permute-start.1 = (f32[40,128]{1,0:T(8,128)S(1)}, f32[40,128]{1,0:T(8,128)S(1)}, u32[]{:S(2)}, u32[]{:S(2)}) collective-permute-start(f32[40,128]{1,0:T(8,128)S(1)} %pair.1.mine_ref), channel_id=1, source_target_pairs={{0,16},{16,0},{1,17},{17,1},{2,18},{18,2},{3,19},{19,3},{4,20},{20... | collective-permute-start | bytes 61448 | tf_op jit(solution)/shard_map/ppermute | solution.py:436
  13.7 19.8 %copy-start.6 = (s32[1,32]{1,0:T(1,128)S(1)}, s32[1,32]{1,0:T(1,128)}, u32[]{:S(2)}) copy-start(s32[1,32]{1,0:T(1,128)} %compare_select_fusion.ids_hbm.ids_ref) | copy-start | bytes 388
  16.8 18.2 %copy-start.5 = (f32[256]{0:T(256)S(1)}, f32[256]{0:T(256)}, u32[]{:S(2)}) copy-start(f32[256]{0:T(256)} %param.17) | copy-start | bytes 3076
  38.7 5.4 %collective-permute-start.3 = (bf16[272,1024]{1,0:T(8,128)(2,1)S(1)}, bf16[272,1024]{1,0:T(8,128)(2,1)S(1)}, u32[]{:S(2)}, u32[]{:S(2)}) collective-permute-start(bf16[272,1024]{1,0:T(8,128)(2,1)S(1)} %get-tuple-element.66), channel_id=1, source_target_pairs={{0,1},{1,0},{2,3},{3,2},{4,5},{5,4},{6,7},{7,6},{8,9},{9,8},{10,11... | collective-permute-start | bytes 1671176 | tf_op jit(solution)/shard_map/ppermute | solution.py:436
  41.8 2.3 %collective-permute-start.2 = (bf16[256,1024]{1,0:T(8,128)(2,1)S(1)}, bf16[256,1024]{1,0:T(8,128)(2,1)S(1)}, u32[]{:S(2)}, u32[]{:S(2)}) collective-permute-start(bf16[256,1024]{1,0:T(8,128)(2,1)S(1)} %get-tuple-element.60), channel_id=1, source_target_pairs={{0,1},{1,0},{2,3},{3,2},{4,5},{5,4},{6,7},{7,6},{8,9},{9,8},{10,11... | collective-permute-start | bytes 1572872 | tf_op jit(solution)/shard_map/ppermute | solution.py:436
  66.8 3.2 %collective-permute-start.4 = (bf16[272,128]{1,0:T(8,128)(2,1)S(1)}, bf16[272,128]{1,0:T(8,128)(2,1)S(1)}, u32[]{:S(2)}, u32[]{:S(2)}) collective-permute-start(bf16[272,128]{1,0:T(8,128)(2,1)S(1)} %plane_sum.1.mine_ref), channel_id=1, source_target_pairs={{0,2},{2,0},{4,6},{6,4},{8,10},{10,8},{12,14},{14,12},{1,3},{3,1},... | collective-permute-start | bytes 208904 | tf_op jit(solution)/shard_map/ppermute | solution.py:462
  70.1 5.7 %collective-permute-start.5 = (bf16[272,128]{1,0:T(8,128)(2,1)S(1)}, bf16[272,128]{1,0:T(8,128)(2,1)S(1)}, u32[]{:S(2)}, u32[]{:S(2)}) collective-permute-start(bf16[272,128]{1,0:T(8,128)(2,1)S(1)} %z_pair.1.mine_ref), channel_id=1, source_target_pairs={{0,4},{2,6},{4,0},{6,2},{8,12},{10,14},{12,8},{14,10},{1,5},{3,7},... | collective-permute-start | bytes 208904 | tf_op jit(solution)/shard_map/ppermute | solution.py:462
  70.4 8.5 %collective-permute-start.6 = (bf16[272,128]{1,0:T(8,128)(2,1)S(1)}, bf16[272,128]{1,0:T(8,128)(2,1)S(1)}, u32[]{:S(2)}, u32[]{:S(2)}) collective-permute-start(bf16[272,128]{1,0:T(8,128)(2,1)S(1)} %z_pair.1.mine_ref), channel_id=1, source_target_pairs={{0,8},{2,10},{4,12},{6,14},{8,0},{10,2},{12,4},{14,6},{1,9},{3,11}... | collective-permute-start | bytes 208904 | tf_op jit(solution)/shard_map/ppermute | solution.py:462
  72.3 7.4 %collective-permute-start.7 = (bf16[272,128]{1,0:T(8,128)(2,1)S(1)}, bf16[272,128]{1,0:T(8,128)(2,1)S(1)}, u32[]{:S(2)}, u32[]{:S(2)}) collective-permute-start(bf16[272,128]{1,0:T(8,128)(2,1)S(1)} %z_pair.1.mine_ref), channel_id=1, source_target_pairs={{0,12},{2,14},{4,8},{6,10},{8,4},{10,6},{12,0},{14,2},{1,13},{3,15... | collective-permute-start | bytes 208904 | tf_op jit(solution)/shard_map/ppermute | solution.py:462
  97.1 6.9 %collective-permute-start.8 = (bf16[16,272,128]{2,1,0:T(8,128)(2,1)S(1)}, bf16[16,272,128]{2,1,0:T(8,128)(2,1)S(1)}, u32[]{:S(2)}, u32[]{:S(2)}) collective-permute-start(bf16[16,272,128]{2,1,0:T(8,128)(2,1)S(1)} %all_to_all.17.got_ref), channel_id=1, source_target_pairs={{0,1},{1,0},{2,3},{3,2},{4,5},{5,4},{6,7},{7,6},{8,9},{9,8},{10,11... | collective-permute-start | bytes 3342344 | tf_op jit(solution)/shard_map/ppermute | solution.py:436

commit v3 on v2

--- a/solution.py
+++ b/solution.py
@@ -86,9 +86,9 @@
 
 
 def forward_kernel(
-    x_hbm, wu_hbm, wd_hbm, gu_hbm, gd_hbm, av_hbm, au_hbm, aw_hbm, ids_hbm, cot_hbm,
-    x_ref, hid_ref, up_ref, feat_ref, tanh_ref, sigm_ref, weight_ref, pack_ref,
-    wu_ref, wd_ref, gu_ref, gd_ref, av_ref, au_ref, aw_ref, ids_ref, cot_ref, sems,
+    x_hbm, wu_hbm, wd_hbm, gu_hbm, gd_hbm, av_hbm, au_hbm, aw_hbm, ids_hbm, cot_hbm, count_ref,
+    x_ref, hid_ref, up_ref, feat_ref, tanh_ref, sigm_ref, weight_ref, pack_ref, live_ref,
+    wd_ref, gu_ref, gd_ref, av_ref, au_ref, aw_ref, wu_ref, ids_ref, cot_ref, sems,
 ):
     starts = [sum(LOADS[:i]) for i in range(len(LOADS))]
     loads = []
@@ -143,7 +143,9 @@
     sigm_ref[...] = sigm
     weight = sigmoid(jnp.sum(tanh * sigm * aw_ref[...], axis=1, keepdims=True))
     weight_ref[...] = jnp.broadcast_to(weight, (SLOTS, LANE))
-    member, _ = members(ids_ref)
+    slot = lax.broadcasted_iota(jnp.int32, (1, SLOTS), 1)
+    live_ref[...] = jnp.where(slot < count_ref[0, 0], ids_ref[...], -1)
+    member, _ = members(live_ref)
     for c in range(4):
         share = jnp.where(member[c], weight, 0.0)
         num = jnp.sum(share * feat, axis=0, keepdims=True)
@@ -199,7 +201,7 @@
 def middle_kernel(
     ids_ref, got_ref, feat_ref, act_ref, slope_ref, tanh_ref, sigm_ref, weight_ref,
     aw_ref, gd_ref,
-    back_ref, pooled_ref, small_ref, keep_ref, send_ref,
+    back_ref, pooled_ref, small_ref, keep_ref, send_ref, keep_sum_ref, profile_ref,
 ):
     core = lax.axis_index("core")
     total = got_ref[0]
@@ -217,11 +219,13 @@
     cot_tile = jnp.zeros((SLOTS, FEAT), F32)
     pooled_tile = jnp.zeros((SLOTS, FEAT), F32)
     den_tile = jnp.where(live, 0.0, 1.0)
+    profile = jnp.zeros((1, FEAT), F32)
     for c in range(4):
         num = jnp.concatenate([total[8 * c + r : 8 * c + r + 1, :] for r in range(8)], axis=1)
         den = total[36 + c : 37 + c, 0:1]
         pooled = num / den
         pooled_ref[c : c + 1, :] = pooled
+        profile = profile + pooled
         cot_tile = jnp.where(member[c], cot[c : c + 1, :], cot_tile)
         pooled_tile = jnp.where(member[c], pooled, pooled_tile)
         den_tile = jnp.where(member[c], den, den_tile)
@@ -234,22 +238,40 @@
     dscore = dweight * weight * (1.0 - weight)
     grad_aw = jnp.sum(dscore * tanh * sigm, axis=0, keepdims=True)
     slope_t, slope_s = slopes(tanh, sigm, aw)
-    parts_t = jnp.concatenate(split3(dscore * slope_t), axis=0)
-    parts_s = jnp.concatenate(split3(dscore * slope_s), axis=0)
-    feat_b = feat.astype(BF16)
-    feat_3 = jnp.concatenate([feat_b, feat_b, feat_b], axis=0)
-    grad_v = tn(parts_t, feat_3)
-    grad_u = tn(parts_s, feat_3)
+    grad_t = dscore * slope_t
+    grad_s = dscore * slope_s
+    profile = (profile * 0.25).astype(BF16).astype(F32)
+    norm = jnp.maximum(jnp.sum(profile * profile, axis=1, keepdims=True), 1e-30)
+    feat_b = feat.astype(BF16).astype(F32)
+    along = jnp.sum(feat_b * profile, axis=1, keepdims=True) / norm
+    rest = feat_b - along * profile
+    rest_0, rest_1, _ = split3(rest)
+    rest_3 = jnp.concatenate([rest_0, rest_0, rest_1], axis=0)
+    grad_t0, grad_t1, _ = split3(grad_t)
+    grad_s0, grad_s1, _ = split3(grad_s)
+    grad_v = tn(jnp.concatenate([grad_t0, grad_t1, grad_t0], axis=0), rest_3)
+    grad_u = tn(jnp.concatenate([grad_s0, grad_s1, grad_s0], axis=0), rest_3)
+    sum_t = jnp.sum(along * grad_t, axis=0, keepdims=True)
+    sum_s = jnp.sum(along * grad_s, axis=0, keepdims=True)
+    for r in range(8):
+        profile_ref[r : r + 1, :] = profile[:, LANE * r : LANE * (r + 1)]
+    keep_sum_ref[...] = jnp.where(core == 0, sum_t, sum_s)
+    sent = jnp.where(core == 0, sum_s, sum_t)
+    high = sent.astype(BF16)
+    send_ref[ATT : ATT + HALF, :] = jnp.zeros((HALF, FEAT), BF16)
+    send_ref[ATT : ATT + HALF, 0:ATT] = jnp.broadcast_to(high, (HALF, ATT))
+    low = (sent - high.astype(F32)).astype(BF16)
+    send_ref[ATT : ATT + HALF, ATT : 2 * ATT] = jnp.broadcast_to(low, (HALF, ATT))
 
     @pl.when(core == 0)
     def _():
         keep_ref[...] = grad_v
-        send_ref[...] = grad_u.astype(BF16)
+        send_ref[0:ATT, :] = grad_u.astype(BF16)
 
     @pl.when(core != 0)
     def _():
         keep_ref[...] = grad_u
-        send_ref[...] = grad_v.astype(BF16)
+        send_ref[0:ATT, :] = grad_v.astype(BF16)
 
     dfeat = ((weight / den_tile) * cot_tile + dscore * slope_ref[...]) * (1.0 / POS)
     back_ref[...] = (dfeat * gd_ref[...]).astype(BF16).astype(F32)
@@ -261,9 +283,8 @@
     small_ref[10:16, :] = jnp.zeros((6, LANE), F32)
 
 
-def backward_kernel(
-    x_ref, mask_ref, hid_ref, up_ref, back_ref, small_ref, wd_ref, gu_ref,
-    keep_ref, send_ref, extra_ref, dback_ref, dup_ref,
+def rows_kernel(
+    mask_ref, up_ref, back_ref, small_ref, wd_ref, gu_ref, dback_ref, dup_ref, out_ref
 ):
     gu = gu_ref[...]
     gain = jnp.zeros((8, BOT), F32)
@@ -280,15 +301,14 @@
         gain = gain + jnp.sum((dscaled * up).reshape(ROWS // 8, 8, BOT), axis=0)
         dup_ref[at, :] = (dscaled * gu).astype(BF16)
     gain = jnp.sum(gain, axis=0, keepdims=True)
-    small = jnp.concatenate(
-        [
-            small_ref[0:10, :],
-            gain[:, 0:LANE],
-            gain[:, LANE : 2 * LANE],
-            jnp.zeros((HALF - 12, LANE), F32),
-        ],
-        axis=0,
-    )
+    out_ref[0:10, :] = small_ref[0:10, :]
+    out_ref[10:11, :] = gain[:, 0:LANE]
+    out_ref[11:12, :] = gain[:, LANE : 2 * LANE]
+    out_ref[12:HALF, :] = jnp.zeros((HALF - 12, LANE), F32)
+
+
+def sums_kernel(x_ref, hid_ref, dback_ref, dup_ref, small_ref, keep_ref, send_ref, extra_ref):
+    small = small_ref[...]
     first = lax.axis_index("core") == 0
     down = tn(hid_ref[...], dback_ref[...])
     up_grad = tn(dup_ref[...], x_ref[...])
@@ -319,7 +339,16 @@
     return block.astype(BF16)
 
 
-def paired_kernel(keep_a_ref, got_a_ref, keep_b_ref, got_b_ref, extra_ref, out_ref):
+def paired_kernel(
+    keep_a_ref, got_a_ref, keep_b_ref, got_b_ref, extra_ref, keep_sum_ref, out_ref, sum_ref
+):
+    total = keep_sum_ref[...]
+    for start in (0, ATT):
+        term = got_a_ref[ATT : ATT + HALF, start : start + ATT].astype(F32)
+        total = total + term[0:1, :]
+    sum_ref[0:1, :] = total[:, 0:LANE]
+    sum_ref[1:2, :] = total[:, LANE : 2 * LANE]
+    sum_ref[2:8, :] = jnp.zeros((6, LANE), F32)
     for p in range(N_PLANE):
         at = slice(HALF * p, HALF * (p + 1))
         for j in range(BLOCKS):
@@ -339,30 +368,47 @@
     return block[MAIN : MAIN + 1, :].astype(F32) + block[MAIN + 1 : MAIN + 2, :].astype(F32)
 
 
-def plane_sum_kernel(got_ref, out_ref):
+def tail_parts(ref):
+    tail = ref[MAIN:TALL, :].astype(F32)
+    return tail[0:1] + tail[1:2], tail[2:10], tail[10:12] + tail[12:14]
+
+
+def tail_block(small, profile, sums):
+    high = small.astype(BF16).astype(F32)
+    sums_high = sums.astype(BF16).astype(F32)
+    rows = [high, small - high, profile, sums_high, sums - sums_high, jnp.zeros((2, LANE), F32)]
+    return jnp.concatenate(rows, axis=0).astype(BF16)
+
+
+def plane_sum_kernel(got_ref, profile_ref, sum_ref, out_ref):
     total = got_ref[0].astype(F32)
     for p in range(1, N_PLANE):
         total = total + got_ref[p].astype(F32)
     out_ref[0:MAIN, :] = total[0:MAIN].astype(BF16)
-    out_ref[MAIN:TALL, :] = two_terms(small_row(total))
+    out_ref[MAIN:TALL, :] = tail_block(small_row(total), profile_ref[...], sum_ref[0:2, :])
 
 
 def z_pair_kernel(mine_ref, other_ref, out_ref):
     total = mine_ref[0:MAIN, :].astype(F32) + other_ref[0:MAIN, :].astype(F32)
     out_ref[0:MAIN, :] = total.astype(BF16)
-    out_ref[MAIN:TALL, :] = two_terms(small_row(mine_ref) + small_row(other_ref))
+    small, profile, sums = tail_parts(mine_ref)
+    small_o, _, sums_o = tail_parts(other_ref)
+    out_ref[MAIN:TALL, :] = tail_block(small + small_o, profile, sums + sums_o)
 
 
 def z_sum_kernel(mine_ref, near_ref, far_ref, cross_ref, out_ref):
     near = mine_ref[0:MAIN, :].astype(F32) + near_ref[0:MAIN, :].astype(F32)
     far = far_ref[0:MAIN, :].astype(F32) + cross_ref[0:MAIN, :].astype(F32)
     main = (near + far).astype(BF16)
-    near = small_row(mine_ref) + small_row(near_ref)
-    far = small_row(far_ref) + small_row(cross_ref)
-    small = two_terms(near + far)
+    small, profile, sums = tail_parts(mine_ref)
+    small_n, _, sums_n = tail_parts(near_ref)
+    small_f, _, sums_f = tail_parts(far_ref)
+    small_c, _, sums_c = tail_parts(cross_ref)
+    small = (small + small_n) + (small_f + small_c)
+    tail = tail_block(small, profile, (sums + sums_n) + (sums_f + sums_c))
     for p in range(N_PLANE):
         out_ref[p, 0:MAIN, :] = main
-        out_ref[p, MAIN:TALL, :] = small
+        out_ref[p, MAIN:TALL, :] = tail
 
 
 def unpack_kernel(own, got_ref, *refs):
@@ -378,10 +424,16 @@
         pltpu.make_async_copy(gdown_ref, gdown_hbm, sems.at[3]),
         pltpu.make_async_copy(aw_ref, aw_hbm, sems.at[4]),
     ]
+    tails = [got_ref[p, MAIN:TALL, :].astype(F32) for p in range(N_PLANE)]
+    sums = [tail[10:12] + tail[12:14] for tail in tails]
+    sums = [jnp.concatenate([v[0:1], v[1:2]], axis=1) for v in sums]
+    sums = jnp.concatenate(split3(jnp.concatenate(sums, axis=0)), axis=0)
     for j in range(BLOCKS):
         rows = slice(PIECE * j, PIECE * j + HALF)
         attn = got_ref[:, rows, :].astype(F32).reshape(ATT, LANE)
-        attn_ref[LANE * j : LANE * (j + 1), :] = attn.T
+        profile = jnp.concatenate([tail[2 + j : 3 + j] for tail in tails], axis=0).astype(BF16)
+        outer = tn(jnp.concatenate([profile, profile, profile], axis=0), sums)
+        attn_ref[LANE * j : LANE * (j + 1), :] = attn.T + outer
 
     @pl.when(first)
     def _():
@@ -440,14 +492,17 @@
     return [pltpu.with_memory_space_constraint(v, pltpu.HBM) for v in arrays]
 
 
-def reduce_all(keep_a, got_a, keep_b, got_b, extra):
+def reduce_all(keep_a, got_a, keep_b, got_b, extra, keep_sum, profile):
     pieces = (N_PLANE, TALL, LANE)
-    (paired,) = call(
-        paired_kernel, [(pieces, BF16)], keep_a, got_a, keep_b, got_b, extra, name="paired"
+    paired, sums = call(
+        paired_kernel,
+        [(pieces, BF16), ((8, LANE), F32)],
+        keep_a, got_a, keep_b, got_b, extra, keep_sum,
+        name="paired",
     )
     got = lax.all_to_all(paired, PLANE, 0, 0, tiled=True)
     flat = [(pieces[1:], BF16)]
-    (part,) = call(plane_sum_kernel, flat, got, name="plane_sum")
+    (part,) = call(plane_sum_kernel, flat, got, profile, sums, name="plane_sum")
     (pair,) = call(z_pair_kernel, flat, part, cross_z(part, 1), name="z_pair")
     (whole,) = call(
         z_sum_kernel,
@@ -488,7 +543,7 @@
 
 
 def encode(
-    rows, ids, pooled_cot, w_up, w_down, gu, gd, attn_v, attn_u, aw
+    rows, slide_ids, counts, pooled_cot, w_up, w_down, gu, gd, attn_v, attn_u, aw
 ):
     hbm = pl.BlockSpec(memory_space=pltpu.HBM)
     outs = [
@@ -500,45 +555,38 @@
         ((SLOTS, ATT), F32),
         ((SLOTS, LANE), F32),
         ((40, LANE), F32),
+        ((1, SLOTS), jnp.int32),
+        ((BOT, FEAT), BF16),
+        ((1, BOT), F32),
+        ((1, FEAT), F32),
+        ((FEAT, ATT), BF16),
+        ((FEAT, ATT), BF16),
+        ((1, ATT), F32),
     ]
     return pl.pallas_call(
         forward_kernel,
-        in_specs=[hbm] * 10,
+        in_specs=[hbm] * 10 + [pl.BlockSpec(memory_space=pltpu.SMEM)],
         out_specs=[VMEM] * len(outs),
         out_shape=[jax.ShapeDtypeStruct(s, d) for s, d in outs],
         scratch_shapes=[
             pltpu.VMEM((FEAT, BOT), BF16),
-            pltpu.VMEM((BOT, FEAT), BF16),
-            pltpu.VMEM((1, BOT), F32),
-            pltpu.VMEM((1, FEAT), F32),
-            pltpu.VMEM((FEAT, ATT), BF16),
-            pltpu.VMEM((FEAT, ATT), BF16),
-            pltpu.VMEM((1, ATT), F32),
             pltpu.VMEM((1, SLOTS), jnp.int32),
             pltpu.VMEM((4, 32), BF16),
             pltpu.SemaphoreType.DMA((len(LOADS) + 9,)),
         ],
         compiler_params=params(),
         name="encode",
-    )(*in_hbm(rows, w_up, w_down, gu, gd, attn_v, attn_u, aw, ids, pooled_cot))
-
-
-def backward(x, mask, hid, up, back, small, w_down, gu):
-    return pl.pallas_call(
-        backward_kernel,
-        in_specs=[VMEM] * 8,
-        out_shape=[
-            jax.ShapeDtypeStruct((BOT, FEAT), F32),
-            jax.ShapeDtypeStruct((BOT + HALF, FEAT), BF16),
-            jax.ShapeDtypeStruct((HALF, LANE), F32),
-        ],
-        scratch_shapes=[
-            pltpu.VMEM((SLOTS * POS, FEAT), BF16),
-            pltpu.VMEM((SLOTS * POS, BOT), BF16),
-        ],
-        compiler_params=params(),
-        name="backward",
-    )(x, mask, hid, up, back, small, w_down, gu)
+    )(*in_hbm(rows, w_up, w_down, gu, gd, attn_v, attn_u, aw, slide_ids, pooled_cot), counts)
+
+
+def backward_rows(mask, up, back, small, w_down, gu):
+    outs = [((SLOTS * POS, FEAT), BF16), ((SLOTS * POS, BOT), BF16), ((HALF, LANE), F32)]
+    return call(rows_kernel, outs, mask, up, back, small, w_down, gu, name="backward_rows")
+
+
+def backward_sums(x, hid, dback, dup, small):
+    outs = [((BOT, FEAT), F32), ((BOT + HALF, FEAT), BF16), ((HALF, LANE), F32)]
+    return call(sums_kernel, outs, x, hid, dback, dup, small, name="backward_sums")
 
 
 def per_device(
@@ -548,11 +596,10 @@
     gu = gain_up.reshape(1, BOT)
     gd = gain_down.reshape(1, FEAT)
     aw = attn_w.reshape(1, ATT)
-    slot = lax.broadcasted_iota(jnp.int32, (1, SLOTS), 1)
-    ids = jnp.where(slot < counts, slide_ids, -1)
-    x, hid, up, feat, tanh, sigm, weight, pack = encode(
-        rows, ids, pooled_cot, w_up, w_down, gu, gd, attn_v, attn_u, aw
+    x, hid, up, feat, tanh, sigm, weight, pack, ids, *loaded = encode(
+        rows, slide_ids, counts, pooled_cot, w_up, w_down, gu, gd, attn_v, attn_u, aw
     )
+    w_down, gu, gd, attn_v, attn_u, aw = loaded
     (half,) = call(pair_kernel, [((40, LANE), F32)], pack, swap(pack, "core"), name="pair")
     mask, act, slope = call(
         keep_kernel,
@@ -564,7 +611,7 @@
     (spread,) = call(spread_kernel, [((N_Z, 48, LANE), F32)], half, across, name="spread")
     got = lax.all_to_all(spread, "z", 0, 0, tiled=True)
 
-    back, pooled, small, keep_a, send_a = pl.pallas_call(
+    back, pooled, small, keep_a, send_a, keep_sum, profile = pl.pallas_call(
         middle_kernel,
         in_specs=[VMEM] * 10,
         out_shape=[
@@ -572,17 +619,20 @@
             jax.ShapeDtypeStruct((4, FEAT), F32),
             jax.ShapeDtypeStruct((16, LANE), F32),
             jax.ShapeDtypeStruct((ATT, FEAT), F32),
-            jax.ShapeDtypeStruct((ATT, FEAT), BF16),
+            jax.ShapeDtypeStruct((ATT + HALF, FEAT), BF16),
+            jax.ShapeDtypeStruct((1, ATT), F32),
+            jax.ShapeDtypeStruct((8, LANE), F32),
         ],
         compiler_params=params(),
         name="middle",
     )(ids, got, feat, act, slope, tanh, sigm, weight, aw, gd)
 
-    got_a = swap(send_a, "core")
-    keep_b, send_b, extra = backward(x, mask, hid, up, back, small, w_down, gu)
+    dback, dup, small = backward_rows(mask, up, back, small, w_down, gu)
+    got_a, dback = lax.optimization_barrier((swap(send_a, "core"), dback))
+    keep_b, send_b, extra = backward_sums(x, hid, dback, dup, small)
     got_b = swap(send_b, "core")
 
-    mine = reduce_all(keep_a, got_a, keep_b, got_b, extra)
+    mine = reduce_all(keep_a, got_a, keep_b, got_b, extra, keep_sum, profile)
     other = swap(mine, "core")
     g_up, g_down, g_v, g_u, g_gu, g_gd, g_aw = unpack(other, *unpack(mine))
     return (

time: 106 us -> 104 us (0.981)
  starting transfers between devices: 18.1 us -> 19.8 us
  blocking collectives: 56.1 us -> 54.5 us
  other arithmetic: 1.17 us -> 0 us
  waiting for transfers between devices: 10.6 us -> 9.47 us
    pallas_call x7 -> x9, Pallas kernels: 3.64 us -> 7.98 us  [call(): pl.pallas_call(body, out_shape=[jax.ShapeDtypeStruct(s, d) for s, d in ou...]
    pallas_call x2 -> x1, Pallas kernels: 9.78 us -> 5.61 us  [encode(): pl.pallas_call(forward_kernel, in_specs=[hbm] * 10 + [pl.BlockSpec(memory...]
    all_to_all x1, blocking collectives: 17.3 us -> 15.6 us  [reduce_all(): return lax.all_to_all(whole, PLANE, 0, 0, tiled=True)]
    ppermute x5, starting transfers between devices: 12 us -> 13.7 us  [swap(): return lax.ppermute(v, axis, [(0, 1), (1, 0)])]
    select_n x1 -> x0, other arithmetic: 1.17 us -> none  [per_device(): ids = jnp.where(slot < counts, slide_ids, -1)]
  transfers between devices with their start and end apart: 9 -> 9, of which waited for: 6 -> 6; matrix products, arithmetic and copies ran while one was open for 0% -> 0% of each run, Pallas kernels for 5% -> 6%
where the time goes in v3:
time: 104 us
  blocking collectives  54.5 us (52%)
  starting transfers between devices  19.8 us (19%)
  Pallas kernels  18.8 us (18%)
  waiting for transfers between devices  9.47 us (9%)
  between operations  1.5 us (1%)
    all_to_all x1, blocking collectives, reduce_all(): got = lax.all_to_all(paired, PLANE, 0, 0, tiled=True)  22.3 us
    all_to_all x1, blocking collectives, per_device(): got = lax.all_to_all(spread, 'z', 0, 0, tiled=True)  16.6 us
    all_to_all x1, blocking collectives, reduce_all(): return lax.all_to_all(whole, PLANE, 0, 0, tiled=True)  15.6 us
    ppermute x5, starting transfers between devices, swap(): return lax.ppermute(v, axis, [(0, 1), (1, 0)])  13.7 us
    pallas_call x9, Pallas kernels, call(): pl.pallas_call(body, out_shape=[jax.ShapeDtypeStruct(s, d) for s, d in ou...  7.98 us
    ppermute x4, waiting for transfers between devices, cross_z(): return lax.ppermute(v, 'z', [(i, i ^ bits) for i in range(N_Z)])  6.52 us
    ppermute x4, starting transfers between devices, cross_z(): return lax.ppermute(v, 'z', [(i, i ^ bits) for i in range(N_Z)])  6.12 us
    pallas_call x1, Pallas kernels, encode(): pl.pallas_call(forward_kernel, in_specs=[hbm] * 10 + [pl.BlockSpec(memory...  5.61 us
  transfers between devices with their start and end apart: 9, of which 6 were waited for; matrix products, arithmetic and copies ran while one was open for 0% of the time, Pallas kernels for 6%

profile of v3, /device:TPU:1, one launch (start us, length us, event | category | flops | bytes accessed | tf_op | source)
XLA Modules:
  0.0 104.0 jit_solution(12920159310876108108)
XLA Ops:
  1.3 5.6 %encode.1 = (bf16[2048,1024]{1,0:T(8,128)(2,1)S(1)}, bf16[2048,256]{1,0:T(8,128)(2,1)S(1)}, f32[2048,256]{1,0:T(8,128)S(1)}, f32[32,1024]{1,0:T(8,128)S(1)}, f32...) custom-call(bf16[2048,1024]{1,0:T(8,128)(2,1)} %bitcast.7, ...), custom_call_target="tpu_custom_call" | custom-call | tf_op jit(solution)/shard_map/encode/pallas_call | solution.py:566
  6.9 3.3 %collective-permute-start = (f32[40,128]{1,0:T(8,128)S(1)}, f32[40,128]{1,0:T(8,128)S(1)}, u32[]{:S(2)}, u32[]{:S(2)}) collective-permute-start(f32[40,128]{1,0:T(8,128)S(1)} %get-tuple-element.62.mine_ref), channel_id=1, source_target_pairs={{0,1},{1,0},{2,3},{3,2},{4,5},{5,4},{6,7},{7,6},{8,9},{9,8},{10,11... | collective-permute-start | bytes 61448 | tf_op jit(solution)/shard_map/ppermute | solution.py:488
  10.2 0.8 collective-permute-done.other_ref
  11.1 1.0 collective-permute-start.1
  12.1 3.1 %keep.1 = (bf16[2048,1024]{1,0:T(8,128)(2,1)S(1)}, f32[32,1024]{1,0:T(8,128)S(1)}, f32[32,1024]{1,0:T(8,128)S(1)}) custom-call(bf16[2048,1024]{1,0:T(8,128)(2,1)S(1)} %get-tuple-element.63.x_ref, bf16[2048,256]{1,0:T(8,128)(2,1)S(1)} %get-tuple-element.64.hid_ref, bf16[256,1024]{1,0:T(8,128)(2,1)S(1)} %get-tuple-element.65.wd_ref, ...), custom_call_target="tpu_custom_call" | custom-call | tf_op jit(solution)/shard_map/keep/pallas_call | solution.py:479
  15.3 16.6 %all_to_all.15.got_ref = f32[8,48,128]{2,1,0:T(8,128)S(1)} all-to-all(f32[8,48,128]{2,1,0:T(8,128)S(1)} %spread.1), channel_id=1, replica_groups=mesh['x_lo'=2,'y'=4,'x_hi'=2,'z'=8,'core'=2] {'z'}, dimensions={0} | all-to-all | bytes 393216 | tf_op jit(solution)/shard_map/all_to_all | solution.py:612
  31.8 1.5 %middle.1 = (f32[32,1024]{1,0:T(8,128)S(1)}, f32[4,1024]{1,0:T(4,128)}, f32[16,128]{1,0:T(8,128)S(1)}, f32[256,1024]{1,0:T(8,128)S(1)}, bf16[272,1024]{1,0:T(8,1...) custom-call(s32[1,32]{1,0:T(1,128)S(1)} %get-tuple-element.61.ids_ref, f32[8,48,128]{2,1,0:T(8,128)S(1)} %all_to_all.15.got_ref, ...), custom_call_target="tpu_custom_call" | custom-call | tf_op jit(solution)/shard_map/middle/pallas_call | solution.py:614
  33.4 2.7 %collective-permute-start.2 = (bf16[272,1024]{1,0:T(8,128)(2,1)S(1)}, bf16[272,1024]{1,0:T(8,128)(2,1)S(1)}, u32[]{:S(2)}, u32[]{:S(2)}) collective-permute-start(bf16[272,1024]{1,0:T(8,128)(2,1)S(1)} %get-tuple-element.82), channel_id=1, source_target_pairs={{0,1},{1,0},{2,3},{3,2},{4,5},{5,4},{6,7},{7,6},{8,9},{9,8},{10,11... | collective-permute-start | bytes 1671176 | tf_op jit(solution)/shard_map/ppermute | solution.py:488
  36.1 1.6 %backward_rows.1 = (bf16[2048,1024]{1,0:T(8,128)(2,1)S(1)}, bf16[2048,256]{1,0:T(8,128)(2,1)S(1)}, f32[16,128]{1,0:T(8,128)S(1)}) custom-call(bf16[2048,1024]{1,0:T(8,128)(2,1)S(1)} %get-tuple-element.83.mask_ref, f32[2048,256]{1,0:T(8,128)S(1)} %get-tuple-element.84.up_ref, f32[32,1024]{1,0:T(8,128)S(1)} %get-tuple-element.85.back_ref, ...), custom_call_target="tpu_custom_call" | custom-call | tf_op jit(solution)/shard_map/backward_rows/pallas_call | solution.py:479
  37.7 2.7 %backward_sums.1 = (f32[256,1024]{1,0:T(8,128)S(1)}, bf16[272,1024]{1,0:T(8,128)(2,1)S(1)}, f32[16,128]{1,0:T(8,128)S(1)}) custom-call(bf16[2048,1024]{1,0:T(8,128)(2,1)S(1)} %get-tuple-element.63.x_ref, bf16[2048,256]{1,0:T(8,128)(2,1)S(1)} %get-tuple-element.64.hid_ref, bf16[2048,1024]{1,0:T(8,128)(2,1)S(1)} %get-tuple-element.90.dback_ref, ...), custom_call_target="tpu_custom_call" | custom-call | tf_op jit(solution)/shard_map/backward_sums/pallas_call | solution.py:479
  40.4 0.4 collective-permute-start.3
  40.8 1.6 %collective-permute-done.3.got_b_ref = bf16[272,1024]{1,0:T(8,128)(2,1)S(1)} collective-permute-done((bf16[272,1024]{1,0:T(8,128)(2,1)S(1)}, bf16[272,1024]{1,0:T(8,128)(2,1)S(1)}, u32[]{:S(2)}, u32[]{:S(2)}) %collective-permute-start.3) | collective-permute-done | bytes 557088 | tf_op jit(solution)/shard_map/ppermute | solution.py:488
  42.7 22.3 %all_to_all.16.got_ref = bf16[16,272,128]{2,1,0:T(8,128)(2,1)S(1)} all-to-all(bf16[16,272,128]{2,1,0:T(8,128)(2,1)S(1)} %get-tuple-element.97), channel_id=1, replica_groups=mesh['x_lo'=2,'y'=4,'x_hi'=2,'z'=8,'core'=2] {'x_lo','y','x_hi'}, dimensions={0} | all-to-all | bytes 2228224 | tf_op jit(solution)/shard_map/all_to_all | solution.py:503
  65.2 0.4 collective-permute-start.4
  65.6 2.9 %collective-permute-done.4.other_ref = bf16[272,128]{1,0:T(8,128)(2,1)S(1)} collective-permute-done((bf16[272,128]{1,0:T(8,128)(2,1)S(1)}, bf16[272,128]{1,0:T(8,128)(2,1)S(1)}, u32[]{:S(2)}, u32[]{:S(2)}) %collective-permute-start.4) | collective-permute-done | bytes 69664 | tf_op jit(solution)/shard_map/ppermute | solution.py:517
  68.7 3.4 %collective-permute-start.6 = (bf16[272,128]{1,0:T(8,128)(2,1)S(1)}, bf16[272,128]{1,0:T(8,128)(2,1)S(1)}, u32[]{:S(2)}, u32[]{:S(2)}) collective-permute-start(bf16[272,128]{1,0:T(8,128)(2,1)S(1)} %z_pair.1.mine_ref), channel_id=1, source_target_pairs={{0,8},{2,10},{4,12},{6,14},{8,0},{10,2},{12,4},{14,6},{1,9},{3,11}... | collective-permute-start | bytes 208904 | tf_op jit(solution)/shard_map/ppermute | solution.py:517
  72.1 2.1 %collective-permute-start.5 = (bf16[272,128]{1,0:T(8,128)(2,1)S(1)}, bf16[272,128]{1,0:T(8,128)(2,1)S(1)}, u32[]{:S(2)}, u32[]{:S(2)}) collective-permute-start(bf16[272,128]{1,0:T(8,128)(2,1)S(1)} %z_pair.1.mine_ref), channel_id=1, source_target_pairs={{0,4},{2,6},{4,0},{6,2},{8,12},{10,14},{12,8},{14,10},{1,5},{3,7},... | collective-permute-start | bytes 208904 | tf_op jit(solution)/shard_map/ppermute | solution.py:517
  74.2 1.6 %collective-permute-done.6.far_ref = bf16[272,128]{1,0:T(8,128)(2,1)S(1)} collective-permute-done((bf16[272,128]{1,0:T(8,128)(2,1)S(1)}, bf16[272,128]{1,0:T(8,128)(2,1)S(1)}, u32[]{:S(2)}, u32[]{:S(2)}) %collective-permute-start.6) | collective-permute-done | bytes 69664 | tf_op jit(solution)/shard_map/ppermute | solution.py:517
  75.8 2.1 %collective-permute-done.5.near_ref = bf16[272,128]{1,0:T(8,128)(2,1)S(1)} collective-permute-done((bf16[272,128]{1,0:T(8,128)(2,1)S(1)}, bf16[272,128]{1,0:T(8,128)(2,1)S(1)}, u32[]{:S(2)}, u32[]{:S(2)}) %collective-permute-start.5) | collective-permute-done | bytes 69664 | tf_op jit(solution)/shard_map/ppermute | solution.py:517
  77.9 15.6 %all_to_all.17.got_ref = bf16[16,272,128]{2,1,0:T(8,128)(2,1)S(1)} all-to-all(bf16[16,272,128]{2,1,0:T(8,128)(2,1)S(1)} %z_sum.1), channel_id=1, replica_groups=mesh['x_lo'=2,'y'=4,'x_hi'=2,'z'=8,'core'=2] {'x_lo','y','x_hi'}, dimensions={0} | all-to-all | bytes 2228224 | tf_op jit(solution)/shard_map/all_to_all | solution.py:513
  93.5 6.2 %collective-permute-start.8 = (bf16[16,272,128]{2,1,0:T(8,128)(2,1)S(1)}, bf16[16,272,128]{2,1,0:T(8,128)(2,1)S(1)}, u32[]{:S(2)}, u32[]{:S(2)}) collective-permute-start(bf16[16,272,128]{2,1,0:T(8,128)(2,1)S(1)} %all_to_all.17.got_ref), channel_id=1, source_target_pairs={{0,1},{1,0},{2,3},{3,2},{4,5},{5,4},{6,7},{7,6},{8,9},{9,8},{10,11... | collective-permute-start | bytes 3342344 | tf_op jit(solution)/shard_map/ppermute | solution.py:488
  99.7 1.9 %unpack_own.1 = (f32[1024,256]{1,0:T(8,128)}, f32[256,1024]{1,0:T(8,128)}, f32[1024,256]{1,0:T(8,128)}, f32[1024,256]{1,0:T(8,128)}, f32[1,256]{1,0:T(1,128)}, /*index=5*/f32[1,1024]{1,0:T(1,128)}, f32[1,256]{1,0:T(1,128)}) custom-call(bf16[16,272,128]{2,1,0:T(8,128)(2,1)S(1)} %all_to_all.17.got_ref), custom_call_target="tpu_custom_call" | custom-call | tf_op jit(solution)/shard_map/unpack_own/pallas_call | solution.py:525
  101.6 0.5 collective-permute-done.8.got_ref
  102.0 1.8 %unpack_other.1 = (f32[1024,256]{1,0:T(8,128)}, f32[256,1024]{1,0:T(8,128)}, f32[1024,256]{1,0:T(8,128)}, f32[1024,256]{1,0:T(8,128)}, f32[1,256]{1,0:T(1,128)}, /*index=5*/f32[1,1024]{1,0:T(1,128)}, f32[1,256]{1,0:T(1,128)}) custom-call(bf16[16,272,128]{2,1,0:T(8,128)(2,1)S(1)} %collective-pe, ...), custom_call_target="tpu_custom_call", output_to_operand_aliasing={{0}: (1, {}), {1}: (2, {}), {2}: (3, {}), {3}: (4, {}), {4}... | custom-call | tf_op jit(solution)/shard_map/unpack_other/pallas_call | solution.py:525
  (10 shorter events, 0.8 us)
Async XLA Ops:
  6.9 4.2 %collective-permute-start = (f32[40,128]{1,0:T(8,128)S(1)}, f32[40,128]{1,0:T(8,128)S(1)}, u32[]{:S(2)}, u32[]{:S(2)}) collective-permute-start(f32[40,128]{1,0:T(8,128)S(1)} %get-tuple-element.62.mine_ref), channel_id=1, source_target_pairs={{0,1},{1,0},{2,3},{3,2},{4,5},{5,4},{6,7},{7,6},{8,9},{9,8},{10,11... | collective-permute-start | bytes 61448 | tf_op jit(solution)/shard_map/ppermute | solution.py:488
  11.1 4.1 %collective-permute-start.1 = (f32[40,128]{1,0:T(8,128)S(1)}, f32[40,128]{1,0:T(8,128)S(1)}, u32[]{:S(2)}, u32[]{:S(2)}) collective-permute-start(f32[40,128]{1,0:T(8,128)S(1)} %pair.1.mine_ref), channel_id=1, source_target_pairs={{0,16},{16,0},{1,17},{17,1},{2,18},{18,2},{3,19},{19,3},{4,20},{20... | collective-permute-start | bytes 61448 | tf_op jit(solution)/shard_map/ppermute | solution.py:488
  33.4 4.4 %collective-permute-start.2 = (bf16[272,1024]{1,0:T(8,128)(2,1)S(1)}, bf16[272,1024]{1,0:T(8,128)(2,1)S(1)}, u32[]{:S(2)}, u32[]{:S(2)}) collective-permute-start(bf16[272,1024]{1,0:T(8,128)(2,1)S(1)} %get-tuple-element.82), channel_id=1, source_target_pairs={{0,1},{1,0},{2,3},{3,2},{4,5},{5,4},{6,7},{7,6},{8,9},{9,8},{10,11... | collective-permute-start | bytes 1671176 | tf_op jit(solution)/shard_map/ppermute | solution.py:488
  40.4 2.0 %collective-permute-start.3 = (bf16[272,1024]{1,0:T(8,128)(2,1)S(1)}, bf16[272,1024]{1,0:T(8,128)(2,1)S(1)}, u32[]{:S(2)}, u32[]{:S(2)}) collective-permute-start(bf16[272,1024]{1,0:T(8,128)(2,1)S(1)} %get-tuple-element.94), channel_id=1, source_target_pairs={{0,1},{1,0},{2,3},{3,2},{4,5},{5,4},{6,7},{7,6},{8,9},{9,8},{10,11... | collective-permute-start | bytes 1671176 | tf_op jit(solution)/shard_map/ppermute | solution.py:488
  65.2 3.2 %collective-permute-start.4 = (bf16[272,128]{1,0:T(8,128)(2,1)S(1)}, bf16[272,128]{1,0:T(8,128)(2,1)S(1)}, u32[]{:S(2)}, u32[]{:S(2)}) collective-permute-start(bf16[272,128]{1,0:T(8,128)(2,1)S(1)} %plane_sum.1.mine_ref), channel_id=1, source_target_pairs={{0,2},{2,0},{4,6},{6,4},{8,10},{10,8},{12,14},{14,12},{1,3},{3,1},... | collective-permute-start | bytes 208904 | tf_op jit(solution)/shard_map/ppermute | solution.py:517
  68.5 5.7 %collective-permute-start.7 = (bf16[272,128]{1,0:T(8,128)(2,1)S(1)}, bf16[272,128]{1,0:T(8,128)(2,1)S(1)}, u32[]{:S(2)}, u32[]{:S(2)}) collective-permute-start(bf16[272,128]{1,0:T(8,128)(2,1)S(1)} %z_pair.1.mine_ref), channel_id=1, source_target_pairs={{0,12},{2,14},{4,8},{6,10},{8,4},{10,6},{12,0},{14,2},{1,13},{3,15... | collective-permute-start | bytes 208904 | tf_op jit(solution)/shard_map/ppermute | solution.py:517
  68.7 7.1 %collective-permute-start.6 = (bf16[272,128]{1,0:T(8,128)(2,1)S(1)}, bf16[272,128]{1,0:T(8,128)(2,1)S(1)}, u32[]{:S(2)}, u32[]{:S(2)}) collective-permute-start(bf16[272,128]{1,0:T(8,128)(2,1)S(1)} %z_pair.1.mine_ref), channel_id=1, source_target_pairs={{0,8},{2,10},{4,12},{6,14},{8,0},{10,2},{12,4},{14,6},{1,9},{3,11}... | collective-permute-start | bytes 208904 | tf_op jit(solution)/shard_map/ppermute | solution.py:517
  72.1 5.8 %collective-permute-start.5 = (bf16[272,128]{1,0:T(8,128)(2,1)S(1)}, bf16[272,128]{1,0:T(8,128)(2,1)S(1)}, u32[]{:S(2)}, u32[]{:S(2)}) collective-permute-start(bf16[272,128]{1,0:T(8,128)(2,1)S(1)} %z_pair.1.mine_ref), channel_id=1, source_target_pairs={{0,4},{2,6},{4,0},{6,2},{8,12},{10,14},{12,8},{14,10},{1,5},{3,7},... | collective-permute-start | bytes 208904 | tf_op jit(solution)/shard_map/ppermute | solution.py:517
  93.5 8.5 %collective-permute-start.8 = (bf16[16,272,128]{2,1,0:T(8,128)(2,1)S(1)}, bf16[16,272,128]{2,1,0:T(8,128)(2,1)S(1)}, u32[]{:S(2)}, u32[]{:S(2)}) collective-permute-start(bf16[16,272,128]{2,1,0:T(8,128)(2,1)S(1)} %all_to_all.17.got_ref), channel_id=1, source_target_pairs={{0,1},{1,0},{2,3},{3,2},{4,5},{5,4},{6,7},{7,6},{8,9},{9,8},{10,11... | collective-permute-start | bytes 3342344 | tf_op jit(solution)/shard_map/ppermute | solution.py:488

commit v4 on v3

--- a/solution.py
+++ b/solution.py
@@ -187,15 +187,13 @@
     first = lax.axis_index("x_hi") == 0
     mine = mine_ref[...]
     other = other_ref[...]
-    total = mine + other
-    row = lax.broadcasted_iota(jnp.int32, (40, LANE), 0)
-    cot = jnp.logical_and(row >= 32, row < 36)
-    low = jnp.where(cot, jnp.where(first, mine, other), total)
+    low = jnp.where(first, mine, other)[32:36]
     high = jnp.where(first, other, mine)[32:36]
+    out = mine + other
     for p in range(N_Z):
-        out_ref[p, 0:40, :] = low
-        out_ref[p, 40:44, :] = high
-        out_ref[p, 44:48, :] = high
+        out_ref[p, 0:32, :] = out[0:32]
+        out_ref[p, 32:36, :] = low + pltpu.roll(high, LANE // 2, 1)
+        out_ref[p, 36:40, :] = out[36:40]
 
 
 def middle_kernel(
@@ -207,14 +205,13 @@
     total = got_ref[0]
     for p in range(1, N_Z):
         total = total + got_ref[p]
-    cot = jnp.concatenate(
-        [
-            got_ref[2 * b, row : row + 4, :] + got_ref[2 * b + 1, row : row + 4, :]
-            for row in (32, 40)
-            for b in range(N_Z // 2)
-        ],
-        axis=1,
-    )
+    even = lax.broadcasted_iota(jnp.int32, (4, LANE), 1) < LANE // 2
+    cots = [got_ref[p, 32:36, :] for p in range(N_Z)]
+    lows = [jnp.where(even, cots[p], cots[p + 1]) for p in range(0, N_Z, 2)]
+    highs = [
+        pltpu.roll(jnp.where(even, cots[p + 1], cots[p]), LANE // 2, 1) for p in range(0, N_Z, 2)
+    ]
+    cot = jnp.concatenate(lows + highs, axis=1)
     member, live = members(ids_ref)
     cot_tile = jnp.zeros((SLOTS, FEAT), F32)
     pooled_tile = jnp.zeros((SLOTS, FEAT), F32)
@@ -396,7 +393,7 @@
     out_ref[MAIN:TALL, :] = tail_block(small + small_o, profile, sums + sums_o)
 
 
-def z_sum_kernel(mine_ref, near_ref, far_ref, cross_ref, out_ref):
+def z_sum_kernel(mine_ref, near_ref, cross_ref, far_ref, out_ref):
     near = mine_ref[0:MAIN, :].astype(F32) + near_ref[0:MAIN, :].astype(F32)
     far = far_ref[0:MAIN, :].astype(F32) + cross_ref[0:MAIN, :].astype(F32)
     main = (near + far).astype(BF16)
@@ -504,10 +501,11 @@
     flat = [(pieces[1:], BF16)]
     (part,) = call(plane_sum_kernel, flat, got, profile, sums, name="plane_sum")
     (pair,) = call(z_pair_kernel, flat, part, cross_z(part, 1), name="z_pair")
+    near, cross, far = [cross_z(pair, bits) for bits in (2, 6, 4)]
     (whole,) = call(
         z_sum_kernel,
         [(pieces, BF16)],
-        pair, cross_z(pair, 2), cross_z(pair, 4), cross_z(pair, 6),
+        pair, near, cross, far,
         name="z_sum",
     )
     return lax.all_to_all(whole, PLANE, 0, 0, tiled=True)
@@ -608,7 +606,7 @@
         name="keep",
     )
     across, mask, act, slope = lax.optimization_barrier((swap(half, "x_hi"), mask, act, slope))
-    (spread,) = call(spread_kernel, [((N_Z, 48, LANE), F32)], half, across, name="spread")
+    (spread,) = call(spread_kernel, [((N_Z, 40, LANE), F32)], half, across, name="spread")
     got = lax.all_to_all(spread, "z", 0, 0, tiled=True)
 
     back, pooled, small, keep_a, send_a, keep_sum, profile = pl.pallas_call(

time: 104 us -> 104 us (level)
  starting transfers between devices: 19.8 us -> 17.7 us
  blocking collectives: 54.5 us -> 56.3 us
    ppermute x5, starting transfers between devices: 13.7 us -> 11.6 us  [swap(): return lax.ppermute(v, axis, [(0, 1), (1, 0)])]
    all_to_all x1, blocking collectives: 15.6 us -> 17.4 us  [reduce_all(): return lax.all_to_all(whole, PLANE, 0, 0, tiled=True)]
where the time goes in v4:
time: 104 us
  blocking collectives  56.3 us (54%)
  Pallas kernels  18.8 us (18%)
  starting transfers between devices  17.7 us (17%)
  waiting for transfers between devices  9.64 us (9%)
  between operations  1.5 us (1%)
    all_to_all x1, blocking collectives, reduce_all(): got = lax.all_to_all(paired, PLANE, 0, 0, tiled=True)  22.7 us
    all_to_all x1, blocking collectives, reduce_all(): return lax.all_to_all(whole, PLANE, 0, 0, tiled=True)  17.4 us
    all_to_all x1, blocking collectives, per_device(): got = lax.all_to_all(spread, 'z', 0, 0, tiled=True)  16.2 us
    ppermute x5, starting transfers between devices, swap(): return lax.ppermute(v, axis, [(0, 1), (1, 0)])  11.6 us
    pallas_call x9, Pallas kernels, call(): pl.pallas_call(body, out_shape=[jax.ShapeDtypeStruct(s, d) for s, d in ou...  8.05 us
    ppermute x4, waiting for transfers between devices, cross_z(): return lax.ppermute(v, 'z', [(i, i ^ bits) for i in range(N_Z)])  6.69 us
    ppermute x4, starting transfers between devices, cross_z(): return lax.ppermute(v, 'z', [(i, i ^ bits) for i in range(N_Z)])  6.11 us
    pallas_call x1, Pallas kernels, encode(): pl.pallas_call(forward_kernel, in_specs=[hbm] * 10 + [pl.BlockSpec(memory...  5.61 us
  transfers between devices with their start and end apart: 9, of which 6 were waited for; matrix products, arithmetic and copies ran while one was open for 0% of the time, Pallas kernels for 6%

profile of v4, /device:TPU:1, one launch (start us, length us, event | category | flops | bytes accessed | tf_op | source)
XLA Modules:
  0.0 103.9 jit_solution(5202374959102826226)
XLA Ops:
  1.3 5.6 %encode.1 = (bf16[2048,1024]{1,0:T(8,128)(2,1)S(1)}, bf16[2048,256]{1,0:T(8,128)(2,1)S(1)}, f32[2048,256]{1,0:T(8,128)S(1)}, f32[32,1024]{1,0:T(8,128)S(1)}, f32...) custom-call(bf16[2048,1024]{1,0:T(8,128)(2,1)} %bitcast.7, ...), custom_call_target="tpu_custom_call" | custom-call | tf_op jit(solution)/shard_map/encode/pallas_call | solution.py:564
  6.9 3.3 %collective-permute-start = (f32[40,128]{1,0:T(8,128)S(1)}, f32[40,128]{1,0:T(8,128)S(1)}, u32[]{:S(2)}, u32[]{:S(2)}) collective-permute-start(f32[40,128]{1,0:T(8,128)S(1)} %get-tuple-element.62.mine_ref), channel_id=1, source_target_pairs={{0,1},{1,0},{2,3},{3,2},{4,5},{5,4},{6,7},{7,6},{8,9},{9,8},{10,11... | collective-permute-start | bytes 61448 | tf_op jit(solution)/shard_map/ppermute | solution.py:485
  10.2 0.8 collective-permute-done.other_ref
  11.1 1.0 collective-permute-start.1
  12.1 3.1 %keep.1 = (bf16[2048,1024]{1,0:T(8,128)(2,1)S(1)}, f32[32,1024]{1,0:T(8,128)S(1)}, f32[32,1024]{1,0:T(8,128)S(1)}) custom-call(bf16[2048,1024]{1,0:T(8,128)(2,1)S(1)} %get-tuple-element.63.x_ref, bf16[2048,256]{1,0:T(8,128)(2,1)S(1)} %get-tuple-element.64.hid_ref, bf16[256,1024]{1,0:T(8,128)(2,1)S(1)} %get-tuple-element.65.wd_ref, ...), custom_call_target="tpu_custom_call" | custom-call | tf_op jit(solution)/shard_map/keep/pallas_call | solution.py:476
  15.3 16.2 %all_to_all.15.got_ref = f32[8,40,128]{2,1,0:T(8,128)S(1)} all-to-all(f32[8,40,128]{2,1,0:T(8,128)S(1)} %spread.1), channel_id=1, replica_groups=mesh['x_lo'=2,'y'=4,'x_hi'=2,'z'=8,'core'=2] {'z'}, dimensions={0} | all-to-all | bytes 327680 | tf_op jit(solution)/shard_map/all_to_all | solution.py:610
  31.5 1.5 %middle.1 = (f32[32,1024]{1,0:T(8,128)S(1)}, f32[4,1024]{1,0:T(4,128)}, f32[16,128]{1,0:T(8,128)S(1)}, f32[256,1024]{1,0:T(8,128)S(1)}, bf16[272,1024]{1,0:T(8,1...) custom-call(s32[1,32]{1,0:T(1,128)S(1)} %get-tuple-element.61.ids_ref, f32[8,40,128]{2,1,0:T(8,128)S(1)} %all_to_all.15.got_ref, ...), custom_call_target="tpu_custom_call" | custom-call | tf_op jit(solution)/shard_map/middle/pallas_call | solution.py:612
  33.0 2.4 %collective-permute-start.2 = (bf16[272,1024]{1,0:T(8,128)(2,1)S(1)}, bf16[272,1024]{1,0:T(8,128)(2,1)S(1)}, u32[]{:S(2)}, u32[]{:S(2)}) collective-permute-start(bf16[272,1024]{1,0:T(8,128)(2,1)S(1)} %get-tuple-element.82), channel_id=1, source_target_pairs={{0,1},{1,0},{2,3},{3,2},{4,5},{5,4},{6,7},{7,6},{8,9},{9,8},{10,11... | collective-permute-start | bytes 1671176 | tf_op jit(solution)/shard_map/ppermute | solution.py:485
  35.5 1.6 %backward_rows.1 = (bf16[2048,1024]{1,0:T(8,128)(2,1)S(1)}, bf16[2048,256]{1,0:T(8,128)(2,1)S(1)}, f32[16,128]{1,0:T(8,128)S(1)}) custom-call(bf16[2048,1024]{1,0:T(8,128)(2,1)S(1)} %get-tuple-element.83.mask_ref, f32[2048,256]{1,0:T(8,128)S(1)} %get-tuple-element.84.up_ref, f32[32,1024]{1,0:T(8,128)S(1)} %get-tuple-element.85.back_ref, ...), custom_call_target="tpu_custom_call" | custom-call | tf_op jit(solution)/shard_map/backward_rows/pallas_call | solution.py:476
  37.1 2.7 %backward_sums.1 = (f32[256,1024]{1,0:T(8,128)S(1)}, bf16[272,1024]{1,0:T(8,128)(2,1)S(1)}, f32[16,128]{1,0:T(8,128)S(1)}) custom-call(bf16[2048,1024]{1,0:T(8,128)(2,1)S(1)} %get-tuple-element.63.x_ref, bf16[2048,256]{1,0:T(8,128)(2,1)S(1)} %get-tuple-element.64.hid_ref, bf16[2048,1024]{1,0:T(8,128)(2,1)S(1)} %get-tuple-element.90.dback_ref, ...), custom_call_target="tpu_custom_call" | custom-call | tf_op jit(solution)/shard_map/backward_sums/pallas_call | solution.py:476
  39.7 0.4 collective-permute-start.3
  40.2 1.6 %collective-permute-done.3.got_b_ref = bf16[272,1024]{1,0:T(8,128)(2,1)S(1)} collective-permute-done((bf16[272,1024]{1,0:T(8,128)(2,1)S(1)}, bf16[272,1024]{1,0:T(8,128)(2,1)S(1)}, u32[]{:S(2)}, u32[]{:S(2)}) %collective-permute-start.3) | collective-permute-done | bytes 557088 | tf_op jit(solution)/shard_map/ppermute | solution.py:485
  42.1 22.7 %all_to_all.16.got_ref = bf16[16,272,128]{2,1,0:T(8,128)(2,1)S(1)} all-to-all(bf16[16,272,128]{2,1,0:T(8,128)(2,1)S(1)} %get-tuple-element.97), channel_id=1, replica_groups=mesh['x_lo'=2,'y'=4,'x_hi'=2,'z'=8,'core'=2] {'x_lo','y','x_hi'}, dimensions={0} | all-to-all | bytes 2228224 | tf_op jit(solution)/shard_map/all_to_all | solution.py:500
  64.9 0.4 collective-permute-start.4
  65.3 2.9 %collective-permute-done.4.other_ref = bf16[272,128]{1,0:T(8,128)(2,1)S(1)} collective-permute-done((bf16[272,128]{1,0:T(8,128)(2,1)S(1)}, bf16[272,128]{1,0:T(8,128)(2,1)S(1)}, u32[]{:S(2)}, u32[]{:S(2)}) %collective-permute-start.4) | collective-permute-done | bytes 69664 | tf_op jit(solution)/shard_map/ppermute | solution.py:515
  68.5 2.6 %collective-permute-start.6 = (bf16[272,128]{1,0:T(8,128)(2,1)S(1)}, bf16[272,128]{1,0:T(8,128)(2,1)S(1)}, u32[]{:S(2)}, u32[]{:S(2)}) collective-permute-start(bf16[272,128]{1,0:T(8,128)(2,1)S(1)} %z_pair.1.mine_ref), channel_id=1, source_target_pairs={{0,12},{2,14},{4,8},{6,10},{8,4},{10,6},{12,0},{14,2},{1,13},{3,15... | collective-permute-start | bytes 208904 | tf_op jit(solution)/shard_map/ppermute | solution.py:515
  71.1 2.8 %collective-permute-start.5 = (bf16[272,128]{1,0:T(8,128)(2,1)S(1)}, bf16[272,128]{1,0:T(8,128)(2,1)S(1)}, u32[]{:S(2)}, u32[]{:S(2)}) collective-permute-start(bf16[272,128]{1,0:T(8,128)(2,1)S(1)} %z_pair.1.mine_ref), channel_id=1, source_target_pairs={{0,4},{2,6},{4,0},{6,2},{8,12},{10,14},{12,8},{14,10},{1,5},{3,7},... | collective-permute-start | bytes 208904 | tf_op jit(solution)/shard_map/ppermute | solution.py:515
  73.9 1.6 %collective-permute-done.7.far_ref = bf16[272,128]{1,0:T(8,128)(2,1)S(1)} collective-permute-done((bf16[272,128]{1,0:T(8,128)(2,1)S(1)}, bf16[272,128]{1,0:T(8,128)(2,1)S(1)}, u32[]{:S(2)}, u32[]{:S(2)}) %collective-permute-start.7) | collective-permute-done | bytes 69664 | tf_op jit(solution)/shard_map/ppermute | solution.py:515
  75.5 2.2 %collective-permute-done.5.near_ref = bf16[272,128]{1,0:T(8,128)(2,1)S(1)} collective-permute-done((bf16[272,128]{1,0:T(8,128)(2,1)S(1)}, bf16[272,128]{1,0:T(8,128)(2,1)S(1)}, u32[]{:S(2)}, u32[]{:S(2)}) %collective-permute-start.5) | collective-permute-done | bytes 69664 | tf_op jit(solution)/shard_map/ppermute | solution.py:515
  77.8 17.4 %all_to_all.17.got_ref = bf16[16,272,128]{2,1,0:T(8,128)(2,1)S(1)} all-to-all(bf16[16,272,128]{2,1,0:T(8,128)(2,1)S(1)} %z_sum.1), channel_id=1, replica_groups=mesh['x_lo'=2,'y'=4,'x_hi'=2,'z'=8,'core'=2] {'x_lo','y','x_hi'}, dimensions={0} | all-to-all | bytes 2228224 | tf_op jit(solution)/shard_map/all_to_all | solution.py:511
  95.2 4.4 %collective-permute-start.8 = (bf16[16,272,128]{2,1,0:T(8,128)(2,1)S(1)}, bf16[16,272,128]{2,1,0:T(8,128)(2,1)S(1)}, u32[]{:S(2)}, u32[]{:S(2)}) collective-permute-start(bf16[16,272,128]{2,1,0:T(8,128)(2,1)S(1)} %all_to_all.17.got_ref), channel_id=1, source_target_pairs={{0,1},{1,0},{2,3},{3,2},{4,5},{5,4},{6,7},{7,6},{8,9},{9,8},{10,11... | collective-permute-start | bytes 3342344 | tf_op jit(solution)/shard_map/ppermute | solution.py:485
  99.6 1.9 %unpack_own.1 = (f32[1024,256]{1,0:T(8,128)}, f32[256,1024]{1,0:T(8,128)}, f32[1024,256]{1,0:T(8,128)}, f32[1024,256]{1,0:T(8,128)}, f32[1,256]{1,0:T(1,128)}, /*index=5*/f32[1,1024]{1,0:T(1,128)}, f32[1,256]{1,0:T(1,128)}) custom-call(bf16[16,272,128]{2,1,0:T(8,128)(2,1)S(1)} %all_to_all.17.got_ref), custom_call_target="tpu_custom_call" | custom-call | tf_op jit(solution)/shard_map/unpack_own/pallas_call | solution.py:523
  101.5 0.5 collective-permute-done.8.got_ref
  102.0 1.8 %unpack_other.1 = (f32[1024,256]{1,0:T(8,128)}, f32[256,1024]{1,0:T(8,128)}, f32[1024,256]{1,0:T(8,128)}, f32[1024,256]{1,0:T(8,128)}, f32[1,256]{1,0:T(1,128)}, /*index=5*/f32[1,1024]{1,0:T(1,128)}, f32[1,256]{1,0:T(1,128)}) custom-call(bf16[16,272,128]{2,1,0:T(8,128)(2,1)S(1)} %collective-pe, ...), custom_call_target="tpu_custom_call", output_to_operand_aliasing={{0}: (1, {}), {1}: (2, {}), {2}: (3, {}), {3}: (4, {}), {4}... | custom-call | tf_op jit(solution)/shard_map/unpack_other/pallas_call | solution.py:523
  (10 shorter events, 1.0 us)
Async XLA Ops:
  6.9 4.2 %collective-permute-start = (f32[40,128]{1,0:T(8,128)S(1)}, f32[40,128]{1,0:T(8,128)S(1)}, u32[]{:S(2)}, u32[]{:S(2)}) collective-permute-start(f32[40,128]{1,0:T(8,128)S(1)} %get-tuple-element.62.mine_ref), channel_id=1, source_target_pairs={{0,1},{1,0},{2,3},{3,2},{4,5},{5,4},{6,7},{7,6},{8,9},{9,8},{10,11... | collective-permute-start | bytes 61448 | tf_op jit(solution)/shard_map/ppermute | solution.py:485
  11.1 4.1 %collective-permute-start.1 = (f32[40,128]{1,0:T(8,128)S(1)}, f32[40,128]{1,0:T(8,128)S(1)}, u32[]{:S(2)}, u32[]{:S(2)}) collective-permute-start(f32[40,128]{1,0:T(8,128)S(1)} %pair.1.mine_ref), channel_id=1, source_target_pairs={{0,16},{16,0},{1,17},{17,1},{2,18},{18,2},{3,19},{19,3},{4,20},{20... | collective-permute-start | bytes 61448 | tf_op jit(solution)/shard_map/ppermute | solution.py:485
  33.0 4.0 %collective-permute-start.2 = (bf16[272,1024]{1,0:T(8,128)(2,1)S(1)}, bf16[272,1024]{1,0:T(8,128)(2,1)S(1)}, u32[]{:S(2)}, u32[]{:S(2)}) collective-permute-start(bf16[272,1024]{1,0:T(8,128)(2,1)S(1)} %get-tuple-element.82), channel_id=1, source_target_pairs={{0,1},{1,0},{2,3},{3,2},{4,5},{5,4},{6,7},{7,6},{8,9},{9,8},{10,11... | collective-permute-start | bytes 1671176 | tf_op jit(solution)/shard_map/ppermute | solution.py:485
  39.7 2.0 %collective-permute-start.3 = (bf16[272,1024]{1,0:T(8,128)(2,1)S(1)}, bf16[272,1024]{1,0:T(8,128)(2,1)S(1)}, u32[]{:S(2)}, u32[]{:S(2)}) collective-permute-start(bf16[272,1024]{1,0:T(8,128)(2,1)S(1)} %get-tuple-element.94), channel_id=1, source_target_pairs={{0,1},{1,0},{2,3},{3,2},{4,5},{5,4},{6,7},{7,6},{8,9},{9,8},{10,11... | collective-permute-start | bytes 1671176 | tf_op jit(solution)/shard_map/ppermute | solution.py:485
  64.9 3.2 %collective-permute-start.4 = (bf16[272,128]{1,0:T(8,128)(2,1)S(1)}, bf16[272,128]{1,0:T(8,128)(2,1)S(1)}, u32[]{:S(2)}, u32[]{:S(2)}) collective-permute-start(bf16[272,128]{1,0:T(8,128)(2,1)S(1)} %plane_sum.1.mine_ref), channel_id=1, source_target_pairs={{0,2},{2,0},{4,6},{6,4},{8,10},{10,8},{12,14},{14,12},{1,3},{3,1},... | collective-permute-start | bytes 208904 | tf_op jit(solution)/shard_map/ppermute | solution.py:515
  68.2 7.3 %collective-permute-start.7 = (bf16[272,128]{1,0:T(8,128)(2,1)S(1)}, bf16[272,128]{1,0:T(8,128)(2,1)S(1)}, u32[]{:S(2)}, u32[]{:S(2)}) collective-permute-start(bf16[272,128]{1,0:T(8,128)(2,1)S(1)} %z_pair.1.mine_ref), channel_id=1, source_target_pairs={{0,8},{2,10},{4,12},{6,14},{8,0},{10,2},{12,4},{14,6},{1,9},{3,11}... | collective-permute-start | bytes 208904 | tf_op jit(solution)/shard_map/ppermute | solution.py:515
  68.5 7.0 %collective-permute-start.6 = (bf16[272,128]{1,0:T(8,128)(2,1)S(1)}, bf16[272,128]{1,0:T(8,128)(2,1)S(1)}, u32[]{:S(2)}, u32[]{:S(2)}) collective-permute-start(bf16[272,128]{1,0:T(8,128)(2,1)S(1)} %z_pair.1.mine_ref), channel_id=1, source_target_pairs={{0,12},{2,14},{4,8},{6,10},{8,4},{10,6},{12,0},{14,2},{1,13},{3,15... | collective-permute-start | bytes 208904 | tf_op jit(solution)/shard_map/ppermute | solution.py:515
  71.1 6.6 %collective-permute-start.5 = (bf16[272,128]{1,0:T(8,128)(2,1)S(1)}, bf16[272,128]{1,0:T(8,128)(2,1)S(1)}, u32[]{:S(2)}, u32[]{:S(2)}) collective-permute-start(bf16[272,128]{1,0:T(8,128)(2,1)S(1)} %z_pair.1.mine_ref), channel_id=1, source_target_pairs={{0,4},{2,6},{4,0},{6,2},{8,12},{10,14},{12,8},{14,10},{1,5},{3,7},... | collective-permute-start | bytes 208904 | tf_op jit(solution)/shard_map/ppermute | solution.py:515
  95.2 6.8 %collective-permute-start.8 = (bf16[16,272,128]{2,1,0:T(8,128)(2,1)S(1)}, bf16[16,272,128]{2,1,0:T(8,128)(2,1)S(1)}, u32[]{:S(2)}, u32[]{:S(2)}) collective-permute-start(bf16[16,272,128]{2,1,0:T(8,128)(2,1)S(1)} %all_to_all.17.got_ref), channel_id=1, source_target_pairs={{0,1},{1,0},{2,3},{3,2},{4,5},{5,4},{6,7},{7,6},{8,9},{9,8},{10,11... | collective-permute-start | bytes 3342344 | tf_op jit(solution)/shard_map/ppermute | solution.py:485

commit v5 on v4

--- a/solution.py
+++ b/solution.py
@@ -30,7 +30,9 @@
 HALF = 16
 BLOCKS = FEAT // LANE
 MAIN = PIECE * BLOCKS
-TALL = MAIN + HALF
+TAIL = 32
+TALL = MAIN + TAIL
+SMALLS = 12
 ROWS = GROUP * POS
 
 CHUNKS = 8
@@ -329,13 +331,6 @@
     send_ref[BOT : BOT + HALF, LANE : 2 * LANE] = (sent - high.astype(F32)).astype(BF16)
 
 
-def two_terms(row):
-    high = row.astype(BF16).astype(F32)
-    rows = lax.broadcasted_iota(jnp.int32, (HALF, LANE), 0)
-    block = jnp.where(rows == 0, high, jnp.where(rows == 1, row - high, 0.0))
-    return block.astype(BF16)
-
-
 def paired_kernel(
     keep_a_ref, got_a_ref, keep_b_ref, got_b_ref, extra_ref, keep_sum_ref, out_ref, sum_ref
 ):
@@ -345,7 +340,7 @@
         total = total + term[0:1, :]
     sum_ref[0:1, :] = total[:, 0:LANE]
     sum_ref[1:2, :] = total[:, LANE : 2 * LANE]
-    sum_ref[2:8, :] = jnp.zeros((6, LANE), F32)
+    sum_ref[14:16, :] = jnp.zeros((2, LANE), F32)
     for p in range(N_PLANE):
         at = slice(HALF * p, HALF * (p + 1))
         for j in range(BLOCKS):
@@ -354,26 +349,21 @@
             sum_b = keep_b_ref[at, lanes] + got_b_ref[at, lanes].astype(F32)
             out_ref[p, PIECE * j : PIECE * j + HALF, :] = sum_a.astype(BF16)
             out_ref[p, PIECE * j + HALF : PIECE * (j + 1), :] = sum_b.astype(BF16)
-        cols = slice(0, LANE), slice(LANE, 2 * LANE)
-        small = extra_ref[p : p + 1, :]
-        for col in cols:
-            small = small + got_b_ref[BOT : BOT + HALF, col].astype(F32)[p : p + 1, :]
-        out_ref[p, MAIN:TALL, :] = two_terms(small)
-
-
-def small_row(block):
-    return block[MAIN : MAIN + 1, :].astype(F32) + block[MAIN + 1 : MAIN + 2, :].astype(F32)
+    small = extra_ref[0:SMALLS, :]
+    for col in (slice(0, LANE), slice(LANE, 2 * LANE)):
+        small = small + got_b_ref[BOT : BOT + HALF, col].astype(F32)[0:SMALLS, :]
+    sum_ref[2 : 2 + SMALLS, :] = small
 
 
 def tail_parts(ref):
     tail = ref[MAIN:TALL, :].astype(F32)
-    return tail[0:1] + tail[1:2], tail[2:10], tail[10:12] + tail[12:14]
-
-
-def tail_block(small, profile, sums):
+    return tail[0:4], tail[4:6] + tail[6:8], tail[8:20] + tail[20:32]
+
+
+def tail_block(profile, sums, small):
+    sums_high = sums.astype(BF16).astype(F32)
     high = small.astype(BF16).astype(F32)
-    sums_high = sums.astype(BF16).astype(F32)
-    rows = [high, small - high, profile, sums_high, sums - sums_high, jnp.zeros((2, LANE), F32)]
+    rows = [profile, sums_high, sums - sums_high, high, small - high]
     return jnp.concatenate(rows, axis=0).astype(BF16)
 
 
@@ -381,28 +371,30 @@
     total = got_ref[0].astype(F32)
     for p in range(1, N_PLANE):
         total = total + got_ref[p].astype(F32)
-    out_ref[0:MAIN, :] = total[0:MAIN].astype(BF16)
-    out_ref[MAIN:TALL, :] = tail_block(small_row(total), profile_ref[...], sum_ref[0:2, :])
+    out_ref[0:MAIN, :] = total.astype(BF16)
+    profile = profile_ref[...]
+    profile = jnp.where(lax.axis_index("x_hi") == 0, profile[0:4], profile[4:8])
+    out_ref[MAIN:TALL, :] = tail_block(profile, sum_ref[0:2, :], sum_ref[2 : 2 + SMALLS, :])
 
 
 def z_pair_kernel(mine_ref, other_ref, out_ref):
     total = mine_ref[0:MAIN, :].astype(F32) + other_ref[0:MAIN, :].astype(F32)
     out_ref[0:MAIN, :] = total.astype(BF16)
-    small, profile, sums = tail_parts(mine_ref)
-    small_o, _, sums_o = tail_parts(other_ref)
-    out_ref[MAIN:TALL, :] = tail_block(small + small_o, profile, sums + sums_o)
+    profile, sums, small = tail_parts(mine_ref)
+    _, sums_o, small_o = tail_parts(other_ref)
+    out_ref[MAIN:TALL, :] = tail_block(profile, sums + sums_o, small + small_o)
 
 
 def z_sum_kernel(mine_ref, near_ref, cross_ref, far_ref, out_ref):
     near = mine_ref[0:MAIN, :].astype(F32) + near_ref[0:MAIN, :].astype(F32)
     far = far_ref[0:MAIN, :].astype(F32) + cross_ref[0:MAIN, :].astype(F32)
     main = (near + far).astype(BF16)
-    small, profile, sums = tail_parts(mine_ref)
-    small_n, _, sums_n = tail_parts(near_ref)
-    small_f, _, sums_f = tail_parts(far_ref)
-    small_c, _, sums_c = tail_parts(cross_ref)
-    small = (small + small_n) + (small_f + small_c)
-    tail = tail_block(small, profile, (sums + sums_n) + (sums_f + sums_c))
+    profile, sums, small = tail_parts(mine_ref)
+    _, sums_n, small_n = tail_parts(near_ref)
+    _, sums_f, small_f = tail_parts(far_ref)
+    _, sums_c, small_c = tail_parts(cross_ref)
+    sums = (sums + sums_n) + (sums_f + sums_c)
+    tail = tail_block(profile, sums, (small + small_n) + (small_f + small_c))
     for p in range(N_PLANE):
         out_ref[p, 0:MAIN, :] = main
         out_ref[p, MAIN:TALL, :] = tail
@@ -412,60 +404,82 @@
     up_hbm, down_hbm, v_hbm, u_hbm, gup_hbm, gdown_hbm, aw_hbm = refs[-14:-7]
     attn_ref, down_ref, up_ref, gup_ref, gdown_ref, aw_ref, sems = refs[-7:]
     first = (lax.axis_index("core") == 0) if own else (lax.axis_index("core") != 0)
-    to_v = pltpu.make_async_copy(attn_ref, v_hbm, sems.at[0])
-    to_u = pltpu.make_async_copy(attn_ref, u_hbm, sems.at[0])
-    to_down = pltpu.make_async_copy(down_ref, down_hbm, sems.at[1])
-    to_up = pltpu.make_async_copy(up_ref, up_hbm, sems.at[1])
+
+    def halves(src, dst, sem):
+        rows = src.shape[0] // 2
+        cuts = [pl.ds(rows * h, rows) for h in range(2)]
+        return [
+            pltpu.make_async_copy(src.at[cut, :], dst.at[cut, :], sems.at[sem + h])
+            for h, cut in enumerate(cuts)
+        ]
+
+    to_v = halves(attn_ref, v_hbm, 0)
+    to_u = halves(attn_ref, u_hbm, 0)
+    to_down = halves(down_ref, down_hbm, 2)
+    to_up = halves(up_ref, up_hbm, 2)
     smalls = [
-        pltpu.make_async_copy(gup_ref, gup_hbm, sems.at[2]),
-        pltpu.make_async_copy(gdown_ref, gdown_hbm, sems.at[3]),
-        pltpu.make_async_copy(aw_ref, aw_hbm, sems.at[4]),
+        pltpu.make_async_copy(gup_ref, gup_hbm, sems.at[4]),
+        pltpu.make_async_copy(gdown_ref, gdown_hbm, sems.at[5]),
+        pltpu.make_async_copy(aw_ref, aw_hbm, sems.at[6]),
     ]
     tails = [got_ref[p, MAIN:TALL, :].astype(F32) for p in range(N_PLANE)]
-    sums = [tail[10:12] + tail[12:14] for tail in tails]
+    sums = [tail[4:6] + tail[6:8] for tail in tails]
+    sums = [sums[p] + sums[p + 1] for p in range(0, N_PLANE, 2)]
     sums = [jnp.concatenate([v[0:1], v[1:2]], axis=1) for v in sums]
     sums = jnp.concatenate(split3(jnp.concatenate(sums, axis=0)), axis=0)
     for j in range(BLOCKS):
         rows = slice(PIECE * j, PIECE * j + HALF)
         attn = got_ref[:, rows, :].astype(F32).reshape(ATT, LANE)
-        profile = jnp.concatenate([tail[2 + j : 3 + j] for tail in tails], axis=0).astype(BF16)
-        outer = tn(jnp.concatenate([profile, profile, profile], axis=0), sums)
+        row = slice(j % 4, j % 4 + 1)
+        profile = [tails[p + j // 4][row] for p in range(0, N_PLANE, 2)]
+        profile = jnp.concatenate([v for _ in range(3) for v in profile], axis=0)
+        outer = tn(profile.astype(BF16), sums)
         attn_ref[LANE * j : LANE * (j + 1), :] = attn.T + outer
+        if j % 4 == 3:
+
+            @pl.when(first)
+            def _():
+                to_v[j // 4].start()
+
+            @pl.when(jnp.logical_not(first))
+            def _():
+                to_u[j // 4].start()
 
     @pl.when(first)
     def _():
-        to_v.start()
-        for j in range(BLOCKS):
-            rows = slice(PIECE * j + HALF, PIECE * (j + 1))
-            enc = got_ref[:, rows, :].astype(F32).reshape(BOT, LANE)
-            down_ref[:, LANE * j : LANE * (j + 1)] = enc
-        to_down.start()
-        for r in range(12):
-            block = got_ref[r, MAIN:TALL, :].astype(F32)
-            small = block[0:1, :] + block[1:2, :]
+        for h in range(2):
+            pieces = slice(N_PLANE // 2 * h, N_PLANE // 2 * (h + 1))
+            at = slice(BOT // 2 * h, BOT // 2 * (h + 1))
+            for j in range(BLOCKS):
+                rows = slice(PIECE * j + HALF, PIECE * (j + 1))
+                enc = got_ref[pieces, rows, :].astype(F32).reshape(BOT // 2, LANE)
+                down_ref[at, LANE * j : LANE * (j + 1)] = enc
+            to_down[h].start()
+        small = tails[0][8:20] + tails[0][20:32]
+        for tail in tails[1:]:
+            small = small + (tail[8:20] + tail[20:32])
+        for r in range(SMALLS):
             if r < 8:
-                gdown_ref[:, LANE * r : LANE * (r + 1)] = small
+                gdown_ref[:, LANE * r : LANE * (r + 1)] = small[r : r + 1]
             elif r < 10:
-                aw_ref[:, LANE * (r - 8) : LANE * (r - 7)] = small
+                aw_ref[:, LANE * (r - 8) : LANE * (r - 7)] = small[r : r + 1]
             else:
-                gup_ref[:, LANE * (r - 10) : LANE * (r - 9)] = small
+                gup_ref[:, LANE * (r - 10) : LANE * (r - 9)] = small[r : r + 1]
         for copy in smalls:
             copy.start()
-        to_v.wait()
-        to_down.wait()
-        for copy in smalls:
+        for copy in to_v + to_down + smalls:
             copy.wait()
 
     @pl.when(jnp.logical_not(first))
     def _():
-        to_u.start()
-        for j in range(BLOCKS):
-            rows = slice(PIECE * j + HALF, PIECE * (j + 1))
-            enc = got_ref[:, rows, :].astype(F32).reshape(BOT, LANE)
-            up_ref[LANE * j : LANE * (j + 1), :] = enc.T
-        to_up.start()
-        to_u.wait()
-        to_up.wait()
+        for h in range(2):
+            for j in range(4 * h, 4 * h + 4):
+                rows = slice(PIECE * j + HALF, PIECE * (j + 1))
+                enc = got_ref[:, rows, :].astype(F32).reshape(BOT, LANE)
+                up_ref[LANE * j : LANE * (j + 1), :] = enc.T
+            to_up[h].start()
+        for copy in to_u + to_up:
+            copy.wait()
 
 
 def whole_spec(shape):
@@ -491,9 +505,10 @@
 
 def reduce_all(keep_a, got_a, keep_b, got_b, extra, keep_sum, profile):
     pieces = (N_PLANE, TALL, LANE)
+    scattered = (N_PLANE, MAIN, LANE)
     paired, sums = call(
         paired_kernel,
-        [(pieces, BF16), ((8, LANE), F32)],
+        [(scattered, BF16), ((HALF, LANE), F32)],
         keep_a, got_a, keep_b, got_b, extra, keep_sum,
         name="paired",
     )
@@ -533,7 +548,7 @@
             pltpu.VMEM((1, BOT), F32),
             pltpu.VMEM((1, FEAT), F32),
             pltpu.VMEM((1, ATT), F32),
-            pltpu.SemaphoreType.DMA((5,)),
+            pltpu.SemaphoreType.DMA((7,)),
         ],
         compiler_params=params(),
         name="unpack_other" if before else "unpack_own",

time: 104 us -> 104 us (level)
    all_to_all x1, blocking collectives: 22.7 us -> 20.5 us  [reduce_all(): got = lax.all_to_all(paired, PLANE, 0, 0, tiled=True)]
    all_to_all x1, blocking collectives: 17.4 us -> 19.1 us  [reduce_all(): return lax.all_to_all(whole, PLANE, 0, 0, tiled=True)]
where the time goes in v5:
time: 104 us
  blocking collectives  55.8 us (54%)
  Pallas kernels  18.5 us (18%)
  starting transfers between devices  17.8 us (17%)
  waiting for transfers between devices  10.2 us (10%)
  between operations  1.5 us (1%)
    all_to_all x1, blocking collectives, reduce_all(): got = lax.all_to_all(paired, PLANE, 0, 0, tiled=True)  20.5 us
    all_to_all x1, blocking collectives, reduce_all(): return lax.all_to_all(whole, PLANE, 0, 0, tiled=True)  19.1 us
    all_to_all x1, blocking collectives, per_device(): got = lax.all_to_all(spread, 'z', 0, 0, tiled=True)  16.2 us
    ppermute x5, starting transfers between devices, swap(): return lax.ppermute(v, axis, [(0, 1), (1, 0)])  11.7 us
    pallas_call x9, Pallas kernels, call(): pl.pallas_call(body, out_shape=[jax.ShapeDtypeStruct(s, d) for s, d in ou...  8.01 us
    ppermute x4, waiting for transfers between devices, cross_z(): return lax.ppermute(v, 'z', [(i, i ^ bits) for i in range(N_Z)])  6.9 us
    ppermute x4, starting transfers between devices, cross_z(): return lax.ppermute(v, 'z', [(i, i ^ bits) for i in range(N_Z)])  6.11 us
    pallas_call x1, Pallas kernels, encode(): pl.pallas_call(forward_kernel, in_specs=[hbm] * 10 + [pl.BlockSpec(memory...  5.61 us
  transfers between devices with their start and end apart: 9, of which 6 were waited for; matrix products, arithmetic and copies ran while one was open for 0% of the time, Pallas kernels for 6%

profile of v5, /device:TPU:1, one launch (start us, length us, event | category | flops | bytes accessed | tf_op | source)
XLA Modules:
  0.0 103.8 jit_solution(14556790391372484883)
XLA Ops:
  1.3 5.6 %encode.1 = (bf16[2048,1024]{1,0:T(8,128)(2,1)S(1)}, bf16[2048,256]{1,0:T(8,128)(2,1)S(1)}, f32[2048,256]{1,0:T(8,128)S(1)}, f32[32,1024]{1,0:T(8,128)S(1)}, f32...) custom-call(bf16[2048,1024]{1,0:T(8,128)(2,1)} %bitcast.7, ...), custom_call_target="tpu_custom_call" | custom-call | tf_op jit(solution)/shard_map/encode/pallas_call | solution.py:579
  6.9 3.3 %collective-permute-start = (f32[40,128]{1,0:T(8,128)S(1)}, f32[40,128]{1,0:T(8,128)S(1)}, u32[]{:S(2)}, u32[]{:S(2)}) collective-permute-start(f32[40,128]{1,0:T(8,128)S(1)} %get-tuple-element.62.mine_ref), channel_id=1, source_target_pairs={{0,1},{1,0},{2,3},{3,2},{4,5},{5,4},{6,7},{7,6},{8,9},{9,8},{10,11... | collective-permute-start | bytes 61448 | tf_op jit(solution)/shard_map/ppermute | solution.py:499
  10.2 0.8 collective-permute-done.other_ref
  11.1 1.0 collective-permute-start.1
  12.1 3.1 %keep.1 = (bf16[2048,1024]{1,0:T(8,128)(2,1)S(1)}, f32[32,1024]{1,0:T(8,128)S(1)}, f32[32,1024]{1,0:T(8,128)S(1)}) custom-call(bf16[2048,1024]{1,0:T(8,128)(2,1)S(1)} %get-tuple-element.63.x_ref, bf16[2048,256]{1,0:T(8,128)(2,1)S(1)} %get-tuple-element.64.hid_ref, bf16[256,1024]{1,0:T(8,128)(2,1)S(1)} %get-tuple-element.65.wd_ref, ...), custom_call_target="tpu_custom_call" | custom-call | tf_op jit(solution)/shard_map/keep/pallas_call | solution.py:490
  15.3 16.2 %all_to_all.15.got_ref = f32[8,40,128]{2,1,0:T(8,128)S(1)} all-to-all(f32[8,40,128]{2,1,0:T(8,128)S(1)} %spread.1), channel_id=1, replica_groups=mesh['x_lo'=2,'y'=4,'x_hi'=2,'z'=8,'core'=2] {'z'}, dimensions={0} | all-to-all | bytes 327680 | tf_op jit(solution)/shard_map/all_to_all | solution.py:625
  31.5 1.5 %middle.1 = (f32[32,1024]{1,0:T(8,128)S(1)}, f32[4,1024]{1,0:T(4,128)}, f32[16,128]{1,0:T(8,128)S(1)}, f32[256,1024]{1,0:T(8,128)S(1)}, bf16[272,1024]{1,0:T(8,1...) custom-call(s32[1,32]{1,0:T(1,128)S(1)} %get-tuple-element.61.ids_ref, f32[8,40,128]{2,1,0:T(8,128)S(1)} %all_to_all.15.got_ref, ...), custom_call_target="tpu_custom_call" | custom-call | tf_op jit(solution)/shard_map/middle/pallas_call | solution.py:627
  33.0 2.4 %collective-permute-start.2 = (bf16[272,1024]{1,0:T(8,128)(2,1)S(1)}, bf16[272,1024]{1,0:T(8,128)(2,1)S(1)}, u32[]{:S(2)}, u32[]{:S(2)}) collective-permute-start(bf16[272,1024]{1,0:T(8,128)(2,1)S(1)} %get-tuple-element.82), channel_id=1, source_target_pairs={{0,1},{1,0},{2,3},{3,2},{4,5},{5,4},{6,7},{7,6},{8,9},{9,8},{10,11... | collective-permute-start | bytes 1671176 | tf_op jit(solution)/shard_map/ppermute | solution.py:499
  35.5 1.6 %backward_rows.1 = (bf16[2048,1024]{1,0:T(8,128)(2,1)S(1)}, bf16[2048,256]{1,0:T(8,128)(2,1)S(1)}, f32[16,128]{1,0:T(8,128)S(1)}) custom-call(bf16[2048,1024]{1,0:T(8,128)(2,1)S(1)} %get-tuple-element.83.mask_ref, f32[2048,256]{1,0:T(8,128)S(1)} %get-tuple-element.84.up_ref, f32[32,1024]{1,0:T(8,128)S(1)} %get-tuple-element.85.back_ref, ...), custom_call_target="tpu_custom_call" | custom-call | tf_op jit(solution)/shard_map/backward_rows/pallas_call | solution.py:490
  37.1 2.7 %backward_sums.1 = (f32[256,1024]{1,0:T(8,128)S(1)}, bf16[272,1024]{1,0:T(8,128)(2,1)S(1)}, f32[16,128]{1,0:T(8,128)S(1)}) custom-call(bf16[2048,1024]{1,0:T(8,128)(2,1)S(1)} %get-tuple-element.63.x_ref, bf16[2048,256]{1,0:T(8,128)(2,1)S(1)} %get-tuple-element.64.hid_ref, bf16[2048,1024]{1,0:T(8,128)(2,1)S(1)} %get-tuple-element.90.dback_ref, ...), custom_call_target="tpu_custom_call" | custom-call | tf_op jit(solution)/shard_map/backward_sums/pallas_call | solution.py:490
  39.7 0.4 collective-permute-start.3
  40.2 1.6 %collective-permute-done.3.got_b_ref = bf16[272,1024]{1,0:T(8,128)(2,1)S(1)} collective-permute-done((bf16[272,1024]{1,0:T(8,128)(2,1)S(1)}, bf16[272,1024]{1,0:T(8,128)(2,1)S(1)}, u32[]{:S(2)}, u32[]{:S(2)}) %collective-permute-start.3) | collective-permute-done | bytes 557088 | tf_op jit(solution)/shard_map/ppermute | solution.py:499
  42.0 20.5 %all_to_all.16.got_ref = bf16[16,256,128]{2,1,0:T(8,128)(2,1)S(1)} all-to-all(bf16[16,256,128]{2,1,0:T(8,128)(2,1)S(1)} %get-tuple-element.97), channel_id=1, replica_groups=mesh['x_lo'=2,'y'=4,'x_hi'=2,'z'=8,'core'=2] {'x_lo','y','x_hi'}, dimensions={0} | all-to-all | bytes 2097152 | tf_op jit(solution)/shard_map/all_to_all | solution.py:515
  62.6 0.4 collective-permute-start.4
  63.0 2.9 %collective-permute-done.4.other_ref = bf16[288,128]{1,0:T(8,128)(2,1)S(1)} collective-permute-done((bf16[288,128]{1,0:T(8,128)(2,1)S(1)}, bf16[288,128]{1,0:T(8,128)(2,1)S(1)}, u32[]{:S(2)}, u32[]{:S(2)}) %collective-permute-start.4) | collective-permute-done | bytes 73760 | tf_op jit(solution)/shard_map/ppermute | solution.py:530
  66.3 2.6 %collective-permute-start.6 = (bf16[288,128]{1,0:T(8,128)(2,1)S(1)}, bf16[288,128]{1,0:T(8,128)(2,1)S(1)}, u32[]{:S(2)}, u32[]{:S(2)}) collective-permute-start(bf16[288,128]{1,0:T(8,128)(2,1)S(1)} %z_pair.1.mine_ref), channel_id=1, source_target_pairs={{0,12},{2,14},{4,8},{6,10},{8,4},{10,6},{12,0},{14,2},{1,13},{3,15... | collective-permute-start | bytes 221192 | tf_op jit(solution)/shard_map/ppermute | solution.py:530
  68.9 2.8 %collective-permute-start.5 = (bf16[288,128]{1,0:T(8,128)(2,1)S(1)}, bf16[288,128]{1,0:T(8,128)(2,1)S(1)}, u32[]{:S(2)}, u32[]{:S(2)}) collective-permute-start(bf16[288,128]{1,0:T(8,128)(2,1)S(1)} %z_pair.1.mine_ref), channel_id=1, source_target_pairs={{0,4},{2,6},{4,0},{6,2},{8,12},{10,14},{12,8},{14,10},{1,5},{3,7},... | collective-permute-start | bytes 221192 | tf_op jit(solution)/shard_map/ppermute | solution.py:530
  71.7 1.9 %collective-permute-done.7.far_ref = bf16[288,128]{1,0:T(8,128)(2,1)S(1)} collective-permute-done((bf16[288,128]{1,0:T(8,128)(2,1)S(1)}, bf16[288,128]{1,0:T(8,128)(2,1)S(1)}, u32[]{:S(2)}, u32[]{:S(2)}) %collective-permute-start.7) | collective-permute-done | bytes 73760 | tf_op jit(solution)/shard_map/ppermute | solution.py:530
  73.6 2.1 %collective-permute-done.5.near_ref = bf16[288,128]{1,0:T(8,128)(2,1)S(1)} collective-permute-done((bf16[288,128]{1,0:T(8,128)(2,1)S(1)}, bf16[288,128]{1,0:T(8,128)(2,1)S(1)}, u32[]{:S(2)}, u32[]{:S(2)}) %collective-permute-start.5) | collective-permute-done | bytes 73760 | tf_op jit(solution)/shard_map/ppermute | solution.py:530
  75.8 19.1 %all_to_all.17.got_ref = bf16[16,288,128]{2,1,0:T(8,128)(2,1)S(1)} all-to-all(bf16[16,288,128]{2,1,0:T(8,128)(2,1)S(1)} %z_sum.1), channel_id=1, replica_groups=mesh['x_lo'=2,'y'=4,'x_hi'=2,'z'=8,'core'=2] {'x_lo','y','x_hi'}, dimensions={0} | all-to-all | bytes 2359296 | tf_op jit(solution)/shard_map/all_to_all | solution.py:526
  94.9 4.5 %collective-permute-start.8 = (bf16[16,288,128]{2,1,0:T(8,128)(2,1)S(1)}, bf16[16,288,128]{2,1,0:T(8,128)(2,1)S(1)}, u32[]{:S(2)}, u32[]{:S(2)}) collective-permute-start(bf16[16,288,128]{2,1,0:T(8,128)(2,1)S(1)} %all_to_all.17.got_ref), channel_id=1, source_target_pairs={{0,1},{1,0},{2,3},{3,2},{4,5},{5,4},{6,7},{7,6},{8,9},{9,8},{10,11... | collective-permute-start | bytes 3538952 | tf_op jit(solution)/shard_map/ppermute | solution.py:499
  99.5 1.7 %unpack_own.1 = (f32[1024,256]{1,0:T(8,128)}, f32[256,1024]{1,0:T(8,128)}, f32[1024,256]{1,0:T(8,128)}, f32[1024,256]{1,0:T(8,128)}, f32[1,256]{1,0:T(1,128)}, /*index=5*/f32[1,1024]{1,0:T(1,128)}, f32[1,256]{1,0:T(1,128)}) custom-call(bf16[16,288,128]{2,1,0:T(8,128)(2,1)S(1)} %all_to_all.17.got_ref), custom_call_target="tpu_custom_call" | custom-call | tf_op jit(solution)/shard_map/unpack_own/pallas_call | solution.py:538
  101.1 0.8 collective-permute-done.8.got_ref
  101.9 1.7 %unpack_other.1 = (f32[1024,256]{1,0:T(8,128)}, f32[256,1024]{1,0:T(8,128)}, f32[1024,256]{1,0:T(8,128)}, f32[1024,256]{1,0:T(8,128)}, f32[1,256]{1,0:T(1,128)}, /*index=5*/f32[1,1024]{1,0:T(1,128)}, f32[1,256]{1,0:T(1,128)}) custom-call(bf16[16,288,128]{2,1,0:T(8,128)(2,1)S(1)} %collective-pe, ...), custom_call_target="tpu_custom_call", output_to_operand_aliasing={{0}: (1, {}), {1}: (2, {}), {2}: (3, {}), {3}: (4, {}), {4}... | custom-call | tf_op jit(solution)/shard_map/unpack_other/pallas_call | solution.py:538
  (10 shorter events, 1.0 us)
Async XLA Ops:
  6.9 4.2 %collective-permute-start = (f32[40,128]{1,0:T(8,128)S(1)}, f32[40,128]{1,0:T(8,128)S(1)}, u32[]{:S(2)}, u32[]{:S(2)}) collective-permute-start(f32[40,128]{1,0:T(8,128)S(1)} %get-tuple-element.62.mine_ref), channel_id=1, source_target_pairs={{0,1},{1,0},{2,3},{3,2},{4,5},{5,4},{6,7},{7,6},{8,9},{9,8},{10,11... | collective-permute-start | bytes 61448 | tf_op jit(solution)/shard_map/ppermute | solution.py:499
  11.1 4.1 %collective-permute-start.1 = (f32[40,128]{1,0:T(8,128)S(1)}, f32[40,128]{1,0:T(8,128)S(1)}, u32[]{:S(2)}, u32[]{:S(2)}) collective-permute-start(f32[40,128]{1,0:T(8,128)S(1)} %pair.1.mine_ref), channel_id=1, source_target_pairs={{0,16},{16,0},{1,17},{17,1},{2,18},{18,2},{3,19},{19,3},{4,20},{20... | collective-permute-start | bytes 61448 | tf_op jit(solution)/shard_map/ppermute | solution.py:499
  33.0 4.0 %collective-permute-start.2 = (bf16[272,1024]{1,0:T(8,128)(2,1)S(1)}, bf16[272,1024]{1,0:T(8,128)(2,1)S(1)}, u32[]{:S(2)}, u32[]{:S(2)}) collective-permute-start(bf16[272,1024]{1,0:T(8,128)(2,1)S(1)} %get-tuple-element.82), channel_id=1, source_target_pairs={{0,1},{1,0},{2,3},{3,2},{4,5},{5,4},{6,7},{7,6},{8,9},{9,8},{10,11... | collective-permute-start | bytes 1671176 | tf_op jit(solution)/shard_map/ppermute | solution.py:499
  39.7 2.0 %collective-permute-start.3 = (bf16[272,1024]{1,0:T(8,128)(2,1)S(1)}, bf16[272,1024]{1,0:T(8,128)(2,1)S(1)}, u32[]{:S(2)}, u32[]{:S(2)}) collective-permute-start(bf16[272,1024]{1,0:T(8,128)(2,1)S(1)} %get-tuple-element.94), channel_id=1, source_target_pairs={{0,1},{1,0},{2,3},{3,2},{4,5},{5,4},{6,7},{7,6},{8,9},{9,8},{10,11... | collective-permute-start | bytes 1671176 | tf_op jit(solution)/shard_map/ppermute | solution.py:499
  62.6 3.3 %collective-permute-start.4 = (bf16[288,128]{1,0:T(8,128)(2,1)S(1)}, bf16[288,128]{1,0:T(8,128)(2,1)S(1)}, u32[]{:S(2)}, u32[]{:S(2)}) collective-permute-start(bf16[288,128]{1,0:T(8,128)(2,1)S(1)} %plane_sum.1.mine_ref), channel_id=1, source_target_pairs={{0,2},{2,0},{4,6},{6,4},{8,10},{10,8},{12,14},{14,12},{1,3},{3,1},... | collective-permute-start | bytes 221192 | tf_op jit(solution)/shard_map/ppermute | solution.py:530
  66.0 7.7 %collective-permute-start.7 = (bf16[288,128]{1,0:T(8,128)(2,1)S(1)}, bf16[288,128]{1,0:T(8,128)(2,1)S(1)}, u32[]{:S(2)}, u32[]{:S(2)}) collective-permute-start(bf16[288,128]{1,0:T(8,128)(2,1)S(1)} %z_pair.1.mine_ref), channel_id=1, source_target_pairs={{0,8},{2,10},{4,12},{6,14},{8,0},{10,2},{12,4},{14,6},{1,9},{3,11}... | collective-permute-start | bytes 221192 | tf_op jit(solution)/shard_map/ppermute | solution.py:530
  66.3 7.3 %collective-permute-start.6 = (bf16[288,128]{1,0:T(8,128)(2,1)S(1)}, bf16[288,128]{1,0:T(8,128)(2,1)S(1)}, u32[]{:S(2)}, u32[]{:S(2)}) collective-permute-start(bf16[288,128]{1,0:T(8,128)(2,1)S(1)} %z_pair.1.mine_ref), channel_id=1, source_target_pairs={{0,12},{2,14},{4,8},{6,10},{8,4},{10,6},{12,0},{14,2},{1,13},{3,15... | collective-permute-start | bytes 221192 | tf_op jit(solution)/shard_map/ppermute | solution.py:530
  68.9 6.8 %collective-permute-start.5 = (bf16[288,128]{1,0:T(8,128)(2,1)S(1)}, bf16[288,128]{1,0:T(8,128)(2,1)S(1)}, u32[]{:S(2)}, u32[]{:S(2)}) collective-permute-start(bf16[288,128]{1,0:T(8,128)(2,1)S(1)} %z_pair.1.mine_ref), channel_id=1, source_target_pairs={{0,4},{2,6},{4,0},{6,2},{8,12},{10,14},{12,8},{14,10},{1,5},{3,7},... | collective-permute-start | bytes 221192 | tf_op jit(solution)/shard_map/ppermute | solution.py:530
  94.9 7.0 %collective-permute-start.8 = (bf16[16,288,128]{2,1,0:T(8,128)(2,1)S(1)}, bf16[16,288,128]{2,1,0:T(8,128)(2,1)S(1)}, u32[]{:S(2)}, u32[]{:S(2)}) collective-permute-start(bf16[16,288,128]{2,1,0:T(8,128)(2,1)S(1)} %all_to_all.17.got_ref), channel_id=1, source_target_pairs={{0,1},{1,0},{2,3},{3,2},{4,5},{5,4},{6,7},{7,6},{8,9},{9,8},{10,11... | collective-permute-start | bytes 3538952 | tf_op jit(solution)/shard_map/ppermute | solution.py:499

commit v6 on v4

--- a/solution.py
+++ b/solution.py
@@ -412,10 +412,19 @@
     up_hbm, down_hbm, v_hbm, u_hbm, gup_hbm, gdown_hbm, aw_hbm = refs[-14:-7]
     attn_ref, down_ref, up_ref, gup_ref, gdown_ref, aw_ref, sems = refs[-7:]
     first = (lax.axis_index("core") == 0) if own else (lax.axis_index("core") != 0)
-    to_v = pltpu.make_async_copy(attn_ref, v_hbm, sems.at[0])
-    to_u = pltpu.make_async_copy(attn_ref, u_hbm, sems.at[0])
-    to_down = pltpu.make_async_copy(down_ref, down_hbm, sems.at[1])
-    to_up = pltpu.make_async_copy(up_ref, up_hbm, sems.at[1])
+
+    def halves(src, dst, sem):
+        rows = src.shape[0] // 2
+        cuts = [pl.ds(rows * h, rows) for h in range(2)]
+        return [
+            pltpu.make_async_copy(src.at[cut, :], dst.at[cut, :], sems.at[sem + h])
+            for h, cut in enumerate(cuts)
+        ]
+
+    to_v = halves(attn_ref, v_hbm, 5)
+    to_u = halves(attn_ref, u_hbm, 5)
+    to_down = halves(down_ref, down_hbm, 0)
+    to_up = halves(up_ref, up_hbm, 0)
     smalls = [
         pltpu.make_async_copy(gup_ref, gup_hbm, sems.at[2]),
         pltpu.make_async_copy(gdown_ref, gdown_hbm, sems.at[3]),
@@ -431,15 +440,26 @@
         profile = jnp.concatenate([tail[2 + j : 3 + j] for tail in tails], axis=0).astype(BF16)
         outer = tn(jnp.concatenate([profile, profile, profile], axis=0), sums)
         attn_ref[LANE * j : LANE * (j + 1), :] = attn.T + outer
+        if j % 4 == 3:
+
+            @pl.when(first)
+            def _():
+                to_v[j // 4].start()
+
+            @pl.when(jnp.logical_not(first))
+            def _():
+                to_u[j // 4].start()
 
     @pl.when(first)
     def _():
-        to_v.start()
-        for j in range(BLOCKS):
-            rows = slice(PIECE * j + HALF, PIECE * (j + 1))
-            enc = got_ref[:, rows, :].astype(F32).reshape(BOT, LANE)
-            down_ref[:, LANE * j : LANE * (j + 1)] = enc
-        to_down.start()
+        for h in range(2):
+            pieces = slice(N_PLANE // 2 * h, N_PLANE // 2 * (h + 1))
+            at = slice(BOT // 2 * h, BOT // 2 * (h + 1))
+            for j in range(BLOCKS):
+                rows = slice(PIECE * j + HALF, PIECE * (j + 1))
+                enc = got_ref[pieces, rows, :].astype(F32).reshape(BOT // 2, LANE)
+                down_ref[at, LANE * j : LANE * (j + 1)] = enc
+            to_down[h].start()
         for r in range(12):
             block = got_ref[r, MAIN:TALL, :].astype(F32)
             small = block[0:1, :] + block[1:2, :]
@@ -451,21 +471,19 @@
                 gup_ref[:, LANE * (r - 10) : LANE * (r - 9)] = small
         for copy in smalls:
             copy.start()
-        to_v.wait()
-        to_down.wait()
-        for copy in smalls:
+        for copy in to_v + to_down + smalls:
             copy.wait()
 
     @pl.when(jnp.logical_not(first))
     def _():
-        to_u.start()
-        for j in range(BLOCKS):
-            rows = slice(PIECE * j + HALF, PIECE * (j + 1))
-            enc = got_ref[:, rows, :].astype(F32).reshape(BOT, LANE)
-            up_ref[LANE * j : LANE * (j + 1), :] = enc.T
-        to_up.start()
-        to_u.wait()
-        to_up.wait()
+        for h in range(2):
+            for j in range(4 * h, 4 * h + 4):
+                rows = slice(PIECE * j + HALF, PIECE * (j + 1))
+                enc = got_ref[:, rows, :].astype(F32).reshape(BOT, LANE)
+                up_ref[LANE * j : LANE * (j + 1), :] = enc.T
+            to_up[h].start()
+        for copy in to_u + to_up:
+            copy.wait()
 
 
 def whole_spec(shape):
@@ -533,7 +551,7 @@
             pltpu.VMEM((1, BOT), F32),
             pltpu.VMEM((1, FEAT), F32),
             pltpu.VMEM((1, ATT), F32),
-            pltpu.SemaphoreType.DMA((5,)),
+            pltpu.SemaphoreType.DMA((7,)),
         ],
         compiler_params=params(),
         name="unpack_other" if before else "unpack_own",

time: 104 us -> 104 us (level)
  no operation moved by 1% of the time
where the time goes in v6:
time: 104 us
  blocking collectives  56.3 us (54%)
  Pallas kernels  18.6 us (18%)
  starting transfers between devices  17.7 us (17%)
  waiting for transfers between devices  9.83 us (9%)
  between operations  1.5 us (1%)
    all_to_all x1, blocking collectives, reduce_all(): got = lax.all_to_all(paired, PLANE, 0, 0, tiled=True)  22.7 us
    all_to_all x1, blocking collectives, reduce_all(): return lax.all_to_all(whole, PLANE, 0, 0, tiled=True)  17.4 us
    all_to_all x1, blocking collectives, per_device(): got = lax.all_to_all(spread, 'z', 0, 0, tiled=True)  16.2 us
    ppermute x5, starting transfers between devices, swap(): return lax.ppermute(v, axis, [(0, 1), (1, 0)])  11.6 us
    pallas_call x9, Pallas kernels, call(): pl.pallas_call(body, out_shape=[jax.ShapeDtypeStruct(s, d) for s, d in ou...  8.05 us
    ppermute x4, waiting for transfers between devices, cross_z(): return lax.ppermute(v, 'z', [(i, i ^ bits) for i in range(N_Z)])  6.69 us
    ppermute x4, starting transfers between devices, cross_z(): return lax.ppermute(v, 'z', [(i, i ^ bits) for i in range(N_Z)])  6.11 us
    pallas_call x1, Pallas kernels, encode(): pl.pallas_call(forward_kernel, in_specs=[hbm] * 10 + [pl.BlockSpec(memory...  5.61 us
  transfers between devices with their start and end apart: 9, of which 6 were waited for; matrix products, arithmetic and copies ran while one was open for 0% of the time, Pallas kernels for 6%

profile of v6, /device:TPU:1, one launch (start us, length us, event | category | flops | bytes accessed | tf_op | source)
XLA Modules:
  0.0 103.9 jit_solution(15339797516398192739)
XLA Ops:
  1.3 5.6 %encode.1 = (bf16[2048,1024]{1,0:T(8,128)(2,1)S(1)}, bf16[2048,256]{1,0:T(8,128)(2,1)S(1)}, f32[2048,256]{1,0:T(8,128)S(1)}, f32[32,1024]{1,0:T(8,128)S(1)}, f32...) custom-call(bf16[2048,1024]{1,0:T(8,128)(2,1)} %bitcast.7, ...), custom_call_target="tpu_custom_call" | custom-call | tf_op jit(solution)/shard_map/encode/pallas_call | solution.py:582
  6.9 3.3 %collective-permute-start = (f32[40,128]{1,0:T(8,128)S(1)}, f32[40,128]{1,0:T(8,128)S(1)}, u32[]{:S(2)}, u32[]{:S(2)}) collective-permute-start(f32[40,128]{1,0:T(8,128)S(1)} %get-tuple-element.62.mine_ref), channel_id=1, source_target_pairs={{0,1},{1,0},{2,3},{3,2},{4,5},{5,4},{6,7},{7,6},{8,9},{9,8},{10,11... | collective-permute-start | bytes 61448 | tf_op jit(solution)/shard_map/ppermute | solution.py:503
  10.2 0.8 collective-permute-done.other_ref
  11.1 1.0 collective-permute-start.1
  12.1 3.1 %keep.1 = (bf16[2048,1024]{1,0:T(8,128)(2,1)S(1)}, f32[32,1024]{1,0:T(8,128)S(1)}, f32[32,1024]{1,0:T(8,128)S(1)}) custom-call(bf16[2048,1024]{1,0:T(8,128)(2,1)S(1)} %get-tuple-element.63.x_ref, bf16[2048,256]{1,0:T(8,128)(2,1)S(1)} %get-tuple-element.64.hid_ref, bf16[256,1024]{1,0:T(8,128)(2,1)S(1)} %get-tuple-element.65.wd_ref, ...), custom_call_target="tpu_custom_call" | custom-call | tf_op jit(solution)/shard_map/keep/pallas_call | solution.py:494
  15.3 16.2 %all_to_all.15.got_ref = f32[8,40,128]{2,1,0:T(8,128)S(1)} all-to-all(f32[8,40,128]{2,1,0:T(8,128)S(1)} %spread.1), channel_id=1, replica_groups=mesh['x_lo'=2,'y'=4,'x_hi'=2,'z'=8,'core'=2] {'z'}, dimensions={0} | all-to-all | bytes 327680 | tf_op jit(solution)/shard_map/all_to_all | solution.py:628
  31.5 1.5 %middle.1 = (f32[32,1024]{1,0:T(8,128)S(1)}, f32[4,1024]{1,0:T(4,128)}, f32[16,128]{1,0:T(8,128)S(1)}, f32[256,1024]{1,0:T(8,128)S(1)}, bf16[272,1024]{1,0:T(8,1...) custom-call(s32[1,32]{1,0:T(1,128)S(1)} %get-tuple-element.61.ids_ref, f32[8,40,128]{2,1,0:T(8,128)S(1)} %all_to_all.15.got_ref, ...), custom_call_target="tpu_custom_call" | custom-call | tf_op jit(solution)/shard_map/middle/pallas_call | solution.py:630
  33.0 2.4 %collective-permute-start.2 = (bf16[272,1024]{1,0:T(8,128)(2,1)S(1)}, bf16[272,1024]{1,0:T(8,128)(2,1)S(1)}, u32[]{:S(2)}, u32[]{:S(2)}) collective-permute-start(bf16[272,1024]{1,0:T(8,128)(2,1)S(1)} %get-tuple-element.82), channel_id=1, source_target_pairs={{0,1},{1,0},{2,3},{3,2},{4,5},{5,4},{6,7},{7,6},{8,9},{9,8},{10,11... | collective-permute-start | bytes 1671176 | tf_op jit(solution)/shard_map/ppermute | solution.py:503
  35.5 1.6 %backward_rows.1 = (bf16[2048,1024]{1,0:T(8,128)(2,1)S(1)}, bf16[2048,256]{1,0:T(8,128)(2,1)S(1)}, f32[16,128]{1,0:T(8,128)S(1)}) custom-call(bf16[2048,1024]{1,0:T(8,128)(2,1)S(1)} %get-tuple-element.83.mask_ref, f32[2048,256]{1,0:T(8,128)S(1)} %get-tuple-element.84.up_ref, f32[32,1024]{1,0:T(8,128)S(1)} %get-tuple-element.85.back_ref, ...), custom_call_target="tpu_custom_call" | custom-call | tf_op jit(solution)/shard_map/backward_rows/pallas_call | solution.py:494
  37.1 2.7 %backward_sums.1 = (f32[256,1024]{1,0:T(8,128)S(1)}, bf16[272,1024]{1,0:T(8,128)(2,1)S(1)}, f32[16,128]{1,0:T(8,128)S(1)}) custom-call(bf16[2048,1024]{1,0:T(8,128)(2,1)S(1)} %get-tuple-element.63.x_ref, bf16[2048,256]{1,0:T(8,128)(2,1)S(1)} %get-tuple-element.64.hid_ref, bf16[2048,1024]{1,0:T(8,128)(2,1)S(1)} %get-tuple-element.90.dback_ref, ...), custom_call_target="tpu_custom_call" | custom-call | tf_op jit(solution)/shard_map/backward_sums/pallas_call | solution.py:494
  39.7 0.4 collective-permute-start.3
  40.2 1.6 %collective-permute-done.3.got_b_ref = bf16[272,1024]{1,0:T(8,128)(2,1)S(1)} collective-permute-done((bf16[272,1024]{1,0:T(8,128)(2,1)S(1)}, bf16[272,1024]{1,0:T(8,128)(2,1)S(1)}, u32[]{:S(2)}, u32[]{:S(2)}) %collective-permute-start.3) | collective-permute-done | bytes 557088 | tf_op jit(solution)/shard_map/ppermute | solution.py:503
  42.1 22.7 %all_to_all.16.got_ref = bf16[16,272,128]{2,1,0:T(8,128)(2,1)S(1)} all-to-all(bf16[16,272,128]{2,1,0:T(8,128)(2,1)S(1)} %get-tuple-element.97), channel_id=1, replica_groups=mesh['x_lo'=2,'y'=4,'x_hi'=2,'z'=8,'core'=2] {'x_lo','y','x_hi'}, dimensions={0} | all-to-all | bytes 2228224 | tf_op jit(solution)/shard_map/all_to_all | solution.py:518
  64.9 0.4 collective-permute-start.4
  65.3 2.9 %collective-permute-done.4.other_ref = bf16[272,128]{1,0:T(8,128)(2,1)S(1)} collective-permute-done((bf16[272,128]{1,0:T(8,128)(2,1)S(1)}, bf16[272,128]{1,0:T(8,128)(2,1)S(1)}, u32[]{:S(2)}, u32[]{:S(2)}) %collective-permute-start.4) | collective-permute-done | bytes 69664 | tf_op jit(solution)/shard_map/ppermute | solution.py:533
  68.5 2.6 %collective-permute-start.6 = (bf16[272,128]{1,0:T(8,128)(2,1)S(1)}, bf16[272,128]{1,0:T(8,128)(2,1)S(1)}, u32[]{:S(2)}, u32[]{:S(2)}) collective-permute-start(bf16[272,128]{1,0:T(8,128)(2,1)S(1)} %z_pair.1.mine_ref), channel_id=1, source_target_pairs={{0,12},{2,14},{4,8},{6,10},{8,4},{10,6},{12,0},{14,2},{1,13},{3,15... | collective-permute-start | bytes 208904 | tf_op jit(solution)/shard_map/ppermute | solution.py:533
  71.1 2.8 %collective-permute-start.5 = (bf16[272,128]{1,0:T(8,128)(2,1)S(1)}, bf16[272,128]{1,0:T(8,128)(2,1)S(1)}, u32[]{:S(2)}, u32[]{:S(2)}) collective-permute-start(bf16[272,128]{1,0:T(8,128)(2,1)S(1)} %z_pair.1.mine_ref), channel_id=1, source_target_pairs={{0,4},{2,6},{4,0},{6,2},{8,12},{10,14},{12,8},{14,10},{1,5},{3,7},... | collective-permute-start | bytes 208904 | tf_op jit(solution)/shard_map/ppermute | solution.py:533
  73.9 1.6 %collective-permute-done.7.far_ref = bf16[272,128]{1,0:T(8,128)(2,1)S(1)} collective-permute-done((bf16[272,128]{1,0:T(8,128)(2,1)S(1)}, bf16[272,128]{1,0:T(8,128)(2,1)S(1)}, u32[]{:S(2)}, u32[]{:S(2)}) %collective-permute-start.7) | collective-permute-done | bytes 69664 | tf_op jit(solution)/shard_map/ppermute | solution.py:533
  75.5 2.2 %collective-permute-done.5.near_ref = bf16[272,128]{1,0:T(8,128)(2,1)S(1)} collective-permute-done((bf16[272,128]{1,0:T(8,128)(2,1)S(1)}, bf16[272,128]{1,0:T(8,128)(2,1)S(1)}, u32[]{:S(2)}, u32[]{:S(2)}) %collective-permute-start.5) | collective-permute-done | bytes 69664 | tf_op jit(solution)/shard_map/ppermute | solution.py:533
  77.8 17.4 %all_to_all.17.got_ref = bf16[16,272,128]{2,1,0:T(8,128)(2,1)S(1)} all-to-all(bf16[16,272,128]{2,1,0:T(8,128)(2,1)S(1)} %z_sum.1), channel_id=1, replica_groups=mesh['x_lo'=2,'y'=4,'x_hi'=2,'z'=8,'core'=2] {'x_lo','y','x_hi'}, dimensions={0} | all-to-all | bytes 2228224 | tf_op jit(solution)/shard_map/all_to_all | solution.py:529
  95.2 4.4 %collective-permute-start.8 = (bf16[16,272,128]{2,1,0:T(8,128)(2,1)S(1)}, bf16[16,272,128]{2,1,0:T(8,128)(2,1)S(1)}, u32[]{:S(2)}, u32[]{:S(2)}) collective-permute-start(bf16[16,272,128]{2,1,0:T(8,128)(2,1)S(1)} %all_to_all.17.got_ref), channel_id=1, source_target_pairs={{0,1},{1,0},{2,3},{3,2},{4,5},{5,4},{6,7},{7,6},{8,9},{9,8},{10,11... | collective-permute-start | bytes 3342344 | tf_op jit(solution)/shard_map/ppermute | solution.py:503
  99.6 1.7 %unpack_own.1 = (f32[1024,256]{1,0:T(8,128)}, f32[256,1024]{1,0:T(8,128)}, f32[1024,256]{1,0:T(8,128)}, f32[1024,256]{1,0:T(8,128)}, f32[1,256]{1,0:T(1,128)}, /*index=5*/f32[1,1024]{1,0:T(1,128)}, f32[1,256]{1,0:T(1,128)}) custom-call(bf16[16,272,128]{2,1,0:T(8,128)(2,1)S(1)} %all_to_all.17.got_ref), custom_call_target="tpu_custom_call" | custom-call | tf_op jit(solution)/shard_map/unpack_own/pallas_call | solution.py:541
  101.3 0.7 collective-permute-done.8.got_ref
  102.0 1.7 %unpack_other.1 = (f32[1024,256]{1,0:T(8,128)}, f32[256,1024]{1,0:T(8,128)}, f32[1024,256]{1,0:T(8,128)}, f32[1024,256]{1,0:T(8,128)}, f32[1,256]{1,0:T(1,128)}, /*index=5*/f32[1,1024]{1,0:T(1,128)}, f32[1,256]{1,0:T(1,128)}) custom-call(bf16[16,272,128]{2,1,0:T(8,128)(2,1)S(1)} %collective-pe, ...), custom_call_target="tpu_custom_call", output_to_operand_aliasing={{0}: (1, {}), {1}: (2, {}), {2}: (3, {}), {3}: (4, {}), {4}... | custom-call | tf_op jit(solution)/shard_map/unpack_other/pallas_call | solution.py:541
  (10 shorter events, 1.0 us)
Async XLA Ops:
  6.9 4.2 %collective-permute-start = (f32[40,128]{1,0:T(8,128)S(1)}, f32[40,128]{1,0:T(8,128)S(1)}, u32[]{:S(2)}, u32[]{:S(2)}) collective-permute-start(f32[40,128]{1,0:T(8,128)S(1)} %get-tuple-element.62.mine_ref), channel_id=1, source_target_pairs={{0,1},{1,0},{2,3},{3,2},{4,5},{5,4},{6,7},{7,6},{8,9},{9,8},{10,11... | collective-permute-start | bytes 61448 | tf_op jit(solution)/shard_map/ppermute | solution.py:503
  11.1 4.1 %collective-permute-start.1 = (f32[40,128]{1,0:T(8,128)S(1)}, f32[40,128]{1,0:T(8,128)S(1)}, u32[]{:S(2)}, u32[]{:S(2)}) collective-permute-start(f32[40,128]{1,0:T(8,128)S(1)} %pair.1.mine_ref), channel_id=1, source_target_pairs={{0,16},{16,0},{1,17},{17,1},{2,18},{18,2},{3,19},{19,3},{4,20},{20... | collective-permute-start | bytes 61448 | tf_op jit(solution)/shard_map/ppermute | solution.py:503
  33.0 4.0 %collective-permute-start.2 = (bf16[272,1024]{1,0:T(8,128)(2,1)S(1)}, bf16[272,1024]{1,0:T(8,128)(2,1)S(1)}, u32[]{:S(2)}, u32[]{:S(2)}) collective-permute-start(bf16[272,1024]{1,0:T(8,128)(2,1)S(1)} %get-tuple-element.82), channel_id=1, source_target_pairs={{0,1},{1,0},{2,3},{3,2},{4,5},{5,4},{6,7},{7,6},{8,9},{9,8},{10,11... | collective-permute-start | bytes 1671176 | tf_op jit(solution)/shard_map/ppermute | solution.py:503
  39.7 2.0 %collective-permute-start.3 = (bf16[272,1024]{1,0:T(8,128)(2,1)S(1)}, bf16[272,1024]{1,0:T(8,128)(2,1)S(1)}, u32[]{:S(2)}, u32[]{:S(2)}) collective-permute-start(bf16[272,1024]{1,0:T(8,128)(2,1)S(1)} %get-tuple-element.94), channel_id=1, source_target_pairs={{0,1},{1,0},{2,3},{3,2},{4,5},{5,4},{6,7},{7,6},{8,9},{9,8},{10,11... | collective-permute-start | bytes 1671176 | tf_op jit(solution)/shard_map/ppermute | solution.py:503
  64.9 3.2 %collective-permute-start.4 = (bf16[272,128]{1,0:T(8,128)(2,1)S(1)}, bf16[272,128]{1,0:T(8,128)(2,1)S(1)}, u32[]{:S(2)}, u32[]{:S(2)}) collective-permute-start(bf16[272,128]{1,0:T(8,128)(2,1)S(1)} %plane_sum.1.mine_ref), channel_id=1, source_target_pairs={{0,2},{2,0},{4,6},{6,4},{8,10},{10,8},{12,14},{14,12},{1,3},{3,1},... | collective-permute-start | bytes 208904 | tf_op jit(solution)/shard_map/ppermute | solution.py:533
  68.2 7.3 %collective-permute-start.7 = (bf16[272,128]{1,0:T(8,128)(2,1)S(1)}, bf16[272,128]{1,0:T(8,128)(2,1)S(1)}, u32[]{:S(2)}, u32[]{:S(2)}) collective-permute-start(bf16[272,128]{1,0:T(8,128)(2,1)S(1)} %z_pair.1.mine_ref), channel_id=1, source_target_pairs={{0,8},{2,10},{4,12},{6,14},{8,0},{10,2},{12,4},{14,6},{1,9},{3,11}... | collective-permute-start | bytes 208904 | tf_op jit(solution)/shard_map/ppermute | solution.py:533
  68.5 7.0 %collective-permute-start.6 = (bf16[272,128]{1,0:T(8,128)(2,1)S(1)}, bf16[272,128]{1,0:T(8,128)(2,1)S(1)}, u32[]{:S(2)}, u32[]{:S(2)}) collective-permute-start(bf16[272,128]{1,0:T(8,128)(2,1)S(1)} %z_pair.1.mine_ref), channel_id=1, source_target_pairs={{0,12},{2,14},{4,8},{6,10},{8,4},{10,6},{12,0},{14,2},{1,13},{3,15... | collective-permute-start | bytes 208904 | tf_op jit(solution)/shard_map/ppermute | solution.py:533
  71.1 6.6 %collective-permute-start.5 = (bf16[272,128]{1,0:T(8,128)(2,1)S(1)}, bf16[272,128]{1,0:T(8,128)(2,1)S(1)}, u32[]{:S(2)}, u32[]{:S(2)}) collective-permute-start(bf16[272,128]{1,0:T(8,128)(2,1)S(1)} %z_pair.1.mine_ref), channel_id=1, source_target_pairs={{0,4},{2,6},{4,0},{6,2},{8,12},{10,14},{12,8},{14,10},{1,5},{3,7},... | collective-permute-start | bytes 208904 | tf_op jit(solution)/shard_map/ppermute | solution.py:533
  95.2 6.8 %collective-permute-start.8 = (bf16[16,272,128]{2,1,0:T(8,128)(2,1)S(1)}, bf16[16,272,128]{2,1,0:T(8,128)(2,1)S(1)}, u32[]{:S(2)}, u32[]{:S(2)}) collective-permute-start(bf16[16,272,128]{2,1,0:T(8,128)(2,1)S(1)} %all_to_all.17.got_ref), channel_id=1, source_target_pairs={{0,1},{1,0},{2,3},{3,2},{4,5},{5,4},{6,7},{7,6},{8,9},{9,8},{10,11... | collective-permute-start | bytes 3342344 | tf_op jit(solution)/shard_map/ppermute | solution.py:503
